TPU v7x, 512 devices: a whole 4x8x8 slice. The times are simulated.
512 devices in a mesh: dp: 32 (over y, x_lo, core), owner: 16 (over z, x_hi).
Axes of the slice: x: 4 (x_hi: 2, x_lo: 2; x = x_hi * 2 + x_lo), y: 8, z: 8, core: 2. Of those that a mesh axis runs over, the one named last changes fastest.
Arguments:
- grad_parts: bfloat16 [32, 16, 512, 512], P('dp', 'owner'), may hold values from -0.4375 to 0.4375
- assign: int32 [16], replicated, may hold values from 0 to 15, as said below
- left_basis: bfloat16 [16, 3, 512, 512], P('owner', None, 'dp'), may hold values from -0.25 to 0.25
- right_basis: bfloat16 [16, 3, 512, 512], P('owner', None, 'dp'), may hold values from -0.25 to 0.25
- left_stat: float32 [16, 3, 512, 512], P('owner', None, 'dp'), may hold values from -0.15625 to 0.15625
- right_stat: float32 [16, 3, 512, 512], P('owner', None, 'dp'), may hold values from -0.15625 to 0.15625
- moment: float32 [16, 3, 512, 512], P('owner', None, 'dp'), may hold values from -1.5 to 1.5
- second: float32 [16, 3, 512, 512], P('owner', None, 'dp'), may hold values from 0.001 to 0.01
Outputs:
- update: bfloat16 [16, 512, 512], P('owner', 'dp')
- new_left: float32 [16, 3, 512, 512], P('owner', None, 'dp')
- new_right: float32 [16, 3, 512, 512], P('owner', None, 'dp')
- new_moment: float32 [16, 3, 512, 512], P('owner', None, 'dp')
- new_second: float32 [16, 3, 512, 512], P('owner', None, 'dp')
Inputs may be any that keep to these rules, and one draw needn't show every extreme that they name: `assign`: each owner keeps at most 3 blocks and one owner exactly 3; some owners keep none; owners 0 and 15 both keep blocks.
All inputs are finite; a program needn't handle non-finite values.
Results may differ from a plain program's by a relative error of at most 0.024.
Values may be sent and summed in bfloat16 or wider, within the bound.
No kernel may reach another device: no remote copies, remote signals or barrier semaphores. Data moves between devices by JAX's collectives and lax.ppermute only.
A program may use at most 64 MiB of HBM per device.

v0:
```python
import jax
import jax.numpy as jnp
from jax import lax
from jax.sharding import PartitionSpec as P

beta_one = 0.9
beta_two = 0.95
step_count = 10.0
adam_eps = 1e-08
bias_one = 1.0 - beta_one**step_count
bias_two = 1.0 - beta_two**step_count


def slot_numbers(assign):
    positions = jnp.arange(assign.shape[0], dtype=jnp.int32)
    matching = assign[:, None] == assign[None, :]
    earlier = positions[None, :] < positions[:, None]
    return jnp.sum((matching & earlier).astype(jnp.int32), axis=1)


def summed_rows(grad_parts):
    summed = lax.psum_scatter(
        grad_parts.astype(jnp.float32).astype(jnp.bfloat16), "dp", scatter_dimension=2, tiled=True
    ).astype(jnp.float32)
    return summed[0].astype(jnp.bfloat16)


def rotate_in(grad_half, left_rows, right_rows, col_first):
    block_num, row_num, col_num = grad_half.shape
    piece_grad = lax.all_gather(grad_half, "dp", axis=1, tiled=True)
    piece_left = lax.all_gather(left_rows, "dp", axis=1, tiled=True)
    own_cols = lax.dynamic_slice_in_dim(piece_grad, col_first, row_num, 2)
    own_left = lax.dynamic_slice_in_dim(piece_left, col_first, row_num, 2)
    gram_part = jnp.einsum(
        "kab,knb->kan", grad_half, piece_grad, preferred_element_type=jnp.float32
    )
    left_term = gram_part
    right_term = jnp.einsum(
        "knc,knb->kcb", own_cols, piece_grad, preferred_element_type=jnp.float32
    )
    turned = jnp.einsum("knc,knb->kcb", own_left, piece_grad, preferred_element_type=jnp.float32)
    left_term, right_term, turned = (left_term, right_term, turned)
    right_full = lax.all_gather(right_rows, "dp", axis=1, tiled=True)
    rotated = jnp.einsum(
        "kab,kbc->kac", turned.astype(jnp.bfloat16), right_full, preferred_element_type=jnp.float32
    )
    return (left_term, right_term, rotated, right_full)


def rotate_out(direction, left_rows, right_full):
    back_half = jnp.einsum(
        "kac,kbc->kab", direction, right_full, preferred_element_type=jnp.float32
    ).astype(jnp.bfloat16)
    summed_back = jnp.einsum(
        "kan,knb->kab",
        left_rows,
        lax.all_gather(back_half, "dp", axis=1, tiled=True),
        preferred_element_type=jnp.float32,
    )
    return summed_back.astype(jnp.bfloat16)


def adam_states(left_term, right_term, rotated, left_stat, right_stat, moment, second):
    new_left = beta_two * left_stat + (1.0 - beta_two) * left_term
    new_right = beta_two * right_stat + (1.0 - beta_two) * right_term
    new_moment = beta_one * moment + (1.0 - beta_one) * rotated
    new_second = beta_two * second + (1.0 - beta_two) * rotated * rotated
    direction = (new_moment / bias_one / (jnp.sqrt(new_second / bias_two) + adam_eps)).astype(
        jnp.bfloat16
    )
    return (new_left, new_right, new_moment, new_second, direction)


def on_device(grad_parts, assign, left_basis, right_basis, left_stat, right_stat, moment, second):
    row_index = lax.axis_index("dp")
    owner_index = lax.axis_index("owner")
    home_num = grad_parts.shape[1]
    col_num = grad_parts.shape[3]
    row_num = col_num // lax.axis_size("dp")
    slot_cap = left_basis.shape[1]
    col_first = row_index * row_num
    slot_code = assign * slot_cap + slot_numbers(assign)
    slot_range = owner_index * slot_cap + jnp.arange(slot_cap, dtype=jnp.int32)
    pick_slot = slot_code[None, :] == slot_range[:, None]
    home_code = lax.dynamic_slice_in_dim(slot_code, owner_index * home_num, home_num)
    all_codes = jnp.arange(lax.axis_size("owner") * slot_cap, dtype=jnp.int32)
    pick_home = (home_code[:, None] == all_codes[None, :]).astype(jnp.bfloat16)
    left_rows = left_basis[0]
    right_rows = right_basis[0]
    pick_half = pick_slot.astype(jnp.bfloat16)
    grad_half = summed_rows(grad_parts)
    window = pick_half
    slot_grad = jnp.einsum(
        "sn,nrc->src",
        window,
        lax.all_gather(grad_half, "owner", axis=0, tiled=True),
        preferred_element_type=jnp.float32,
    ).astype(jnp.bfloat16)
    slot_left, slot_right, slot_rotated, right_full = rotate_in(
        slot_grad, left_rows, right_rows, col_first
    )
    new_left, new_right, new_moment, new_second, direction = adam_states(
        slot_left, slot_right, slot_rotated, left_stat[0], right_stat[0], moment[0], second[0]
    )
    slot_update = rotate_out(direction, left_rows, right_full)
    window = pick_home
    update = jnp.einsum(
        "hn,nrc->hrc",
        window,
        lax.all_gather(slot_update, "owner", axis=0, tiled=True),
        preferred_element_type=jnp.float32,
    ).astype(jnp.bfloat16)
    return (update, new_left[None], new_right[None], new_moment[None], new_second[None])


def solution(mesh):
    placed = (
        P("dp", "owner", None, None),
        P(),
        P("owner", None, "dp", None),
        P("owner", None, "dp", None),
        P("owner", None, "dp", None),
        P("owner", None, "dp", None),
        P("owner", None, "dp", None),
        P("owner", None, "dp", None),
    )
    return jax.shard_map(
        on_device,
        mesh=mesh,
        in_specs=placed,
        out_specs=(
            P("owner", "dp", None),
            P("owner", None, "dp", None),
            P("owner", None, "dp", None),
            P("owner", None, "dp", None),
            P("owner", None, "dp", None),
        ),
        check_vma=False,
    )
```

profile of v0, /device:TPU:1, one launch (start us, length us, event | category | flops | bytes accessed | tf_op | source)
XLA Modules:
  0.0 462.0 jit_solution(18026171229641985720)
XLA Ops:
  7.2 1.9 copy.57
  9.1 0.9 copy.58
  10.1 0.7 all-gather.14.cloned.1.call-update
  10.8 0.7 all-gather.12.cloned.1.call-update
  11.6 0.2 convert_reduce_fusion
  11.8 119.8 %reduce-scatter.4.cloned.1.call-done = bf16[16,512]{1,0:T(8,128)(2,1)} async-done(((bf16[512,512]{1,0:T(8,128)(2,1)}), bf16[16,512]{1,0:T(8,128)(2,1)}) %reduce-scatter.4.cloned.1.call-update) | async-done | bytes 16400
  131.6 0.7 reshape_bitcast_fusion
  132.4 35.5 %all-gather.1 = bf16[16,1,16,512]{3,2,1,0:T(8,128)(2,1)S(1)} all-gather(bf16[1,1,16,512]{3,2,1,0:T(8,128)(2,1)S(1)} %copy.33), channel_id=3, replica_groups=mesh['dp'=32,'owner'=16] {'owner'}, dimensions={0}, use_global_device_ids=true | all-gather | bytes 278528 | tf_op jit(solution)/shard_map/all_gather | solution.py:96
  167.8 0.3 fusion.19
  168.1 0.6 copy.56
  168.8 34.0 %all-gather.14.cloned.1.call-done = bf16[1,3,512,512]{3,2,1,0:T(8,128)(2,1)} async-done(((bf16[1,3,16,512]{3,2,1,0:T(8,128)(2,1)}), bf16[1,3,512,512]{3,2,1,0:T(8,128)(2,1)}) %all-gather.14.cloned.1.call-update) | async-done | bytes 1572880 | tf_op jit(solution)/shard_map/all_gather | solution.py:43
  202.9 69.1 %all-gather.12.cloned.1.call-done = bf16[1,3,512,512]{3,2,1,0:T(8,128)(2,1)} async-done(((bf16[1,3,16,512]{3,2,1,0:T(8,128)(2,1)}), bf16[1,3,512,512]{3,2,1,0:T(8,128)(2,1)}) %all-gather.12.cloned.1.call-update) | async-done | bytes 1572880 | tf_op jit(solution)/shard_map/all_gather | solution.py:31
  272.0 69.6 %all-gather.8.cloned.1.call-done = bf16[3,512,512]{2,1,0:T(8,128)(2,1)} async-done(((bf16[3,16,512]{2,1,0:T(8,128)(2,1)}), bf16[3,512,512]{2,1,0:T(8,128)(2,1)}) %all-gather.8.cloned.1.call-update) | async-done | bytes 1572880 | tf_op jit(solution)/shard_map/all_gather | solution.py:30
  341.6 2.8 fusion.2
  344.5 1.2 fusion.8
  345.7 0.6 dynamic_slice.9
  346.3 2.1 fusion.5
  348.3 1.2 fusion.7
  349.5 0.7 fusion.28
  350.2 62.4 %all-gather.10.cloned.1.call-done = bf16[3,512,512]{2,1,0:T(8,128)(2,1)} async-done(((bf16[3,16,512]{2,1,0:T(8,128)(2,1)}), bf16[3,512,512]{2,1,0:T(8,128)(2,1)}) %all-gather.10.cloned.1.call-update) | async-done | bytes 1572880 | tf_op jit(solution)/shard_map/all_gather | solution.py:57
  412.6 1.7 fusion.11
  414.3 39.4 %all_gather.23 = bf16[48,16,512]{2,1,0:T(8,128)(2,1)S(1)} all-gather(bf16[3,16,512]{2,1,0:T(8,128)(2,1)S(1)} %fusion.11), channel_id=1, replica_groups=mesh['dp'=32,'owner'=16] {'owner'}, dimensions={0}, use_global_device_ids=true | all-gather | bytes 835584 | tf_op jit(solution)/shard_map/all_gather | solution.py:110
  453.7 1.2 fusion.12
  454.9 0.6 copy.59
  (27 shorter events, 0.3 us)
Async XLA Ops:
  7.2 4.4 copy-start.7
  7.2 124.4 %reduce-scatter.4.cloned.1.call-start = ((), (), s32[]{:S(2)}) async-start(), calls=%async_computation.5 | async-start | bytes 540672
  10.0 192.8 %all-gather.14.cloned.1.call-start = ((), (), s32[]{:S(2)}) async-start(), calls=%async_computation.4 | async-start | bytes 1622016 | tf_op jit(solution)/shard_map/all_gather | solution.py:43
  10.8 261.2 %all-gather.12.cloned.1.call-start = ((), (), s32[]{:S(2)}) async-start(), calls=%async_computation.3 | async-start | bytes 1622016 | tf_op jit(solution)/shard_map/all_gather | solution.py:31
  11.5 330.1 %all-gather.8.cloned.1.call-start = ((), (), s32[]{:S(2)}) async-start(), calls=%async_computation.1 | async-start | bytes 1622016 | tf_op jit(solution)/shard_map/all_gather | solution.py:30
  168.8 243.9 %all-gather.10.cloned.1.call-start = ((), (), s32[]{:S(2)}) async-start(), calls=%async_computation.2 | async-start | bytes 1622016 | tf_op jit(solution)/shard_map/all_gather | solution.py:57
  168.8 175.6 %copy-start.3 = (f32[1,3,16,512]{3,2,1,0:T(8,128)S(1)}, f32[1,3,16,512]{3,2,1,0:T(8,128)}, u32[]{:S(2)}) copy-start(f32[1,3,16,512]{3,2,1,0:T(8,128)} %param.14) | copy-start | bytes 294916
  168.8 175.6 %copy-start.4 = (f32[1,3,16,512]{3,2,1,0:T(8,128)S(1)}, f32[1,3,16,512]{3,2,1,0:T(8,128)}, u32[]{:S(2)}) copy-start(f32[1,3,16,512]{3,2,1,0:T(8,128)} %param.15) | copy-start | bytes 294916
  202.9 141.6 %copy-start.1 = (bf16[1,3,512,512]{3,2,1,0:T(8,128)(2,1)S(1)}, bf16[1,3,512,512]{3,2,1,0:T(8,128)(2,1)}, u32[]{:S(2)}) copy-start(bf16[1,3,512,512]{3,2,1,0:T(8,128)(2,1)} %all-gather.14.cloned.1.call-done) | copy-start | bytes 4718596
  344.5 1.8 copy-start
  344.5 3.8 copy-start.2
  345.6 2.7 copy-start.6
  348.3 64.3 %copy-start.5 = (bf16[1,3,16,512]{3,2,1,0:T(8,128)(2,1)S(1)}, bf16[1,3,16,512]{3,2,1,0:T(8,128)(2,1)}, u32[]{:S(2)}) copy-start(bf16[1,3,16,512]{3,2,1,0:T(8,128)(2,1)} %param.10) | copy-start | bytes 147460
Sparse Core Ops, SparseCore 0:
  10.8 120.7 reduce-scatter.3
  134.0 68.8 all-gather.13
  205.3 66.6 all-gather.11
  274.8 66.7 all-gather.7
  345.8 66.7 all-gather.9
where the time goes:
time: 468 us; the launch traced here: 462 us
  waiting for transfers between devices  356 us (76%)
  blocking collectives  74.8 us (16%)
  between operations  13.9 us (3%)
  matrix products  10.3 us (2%)
  local copies, waits for them, and re-layouts  5.41 us (1%)
    unnamed x6, waiting for transfers between devices  121 us
    all_gather x1, waiting for transfers between devices, rotate_in(): piece_grad = lax.all_gather(grad_half, 'dp', axis=1, tiled=True)  69.6 us
    all_gather x1, waiting for transfers between devices, rotate_in(): piece_left = lax.all_gather(left_rows, 'dp', axis=1, tiled=True)  69.1 us
    all_gather x1, waiting for transfers between devices, rotate_out(): lax.all_gather(back_half, 'dp', axis=1, tiled=True)  62.4 us
    all_gather x1, blocking collectives, on_device(): lax.all_gather(slot_update, 'owner', axis=0, tiled=True)  39.4 us
    all_gather x1, blocking collectives, on_device(): lax.all_gather(grad_half, 'owner', axis=0, tiled=True)  35.5 us
    all_gather x1, waiting for transfers between devices, rotate_in(): right_full = lax.all_gather(right_rows, 'dp', axis=1, tiled=True)  34 us
  transfers between devices with their start and end apart: 5, of which 5 were waited for; matrix products, arithmetic and copies ran while one was open for 1% of the time, Pallas kernels for 0%

commit v1 on v0

v1 whole, which is shorter than its diff:
```python
import jax
import jax.numpy as jnp
from jax import lax
from jax.sharding import PartitionSpec as P

beta_one = 0.9
beta_two = 0.95
step_count = 10.0
adam_eps = 1e-08
bias_one = 1.0 - beta_one**step_count
bias_two = 1.0 - beta_two**step_count

Y_NUM = 8
XC_NUM = 4


def slot_numbers(assign):
    positions = jnp.arange(assign.shape[0], dtype=jnp.int32)
    matching = assign[:, None] == assign[None, :]
    earlier = positions[None, :] < positions[:, None]
    return jnp.sum((matching & earlier).astype(jnp.int32), axis=1)


def swap_bit(value, bit, size):
    return lax.ppermute(value, "dp", [(i, i ^ bit) for i in range(size)])


def finish_gather(over_y, size):
    index = lax.axis_index("dp")
    x_bit = (index // 2) % 2
    core_bit = index % 2
    other = swap_bit(over_y, 2, size)
    pair = jnp.where(
        x_bit == 0, jnp.stack([over_y, other], 1), jnp.stack([other, over_y], 1)
    )
    other = swap_bit(pair, 1, size)
    quad = jnp.where(core_bit == 0, jnp.stack([pair, other], 2), jnp.stack([other, pair], 2))
    y_num, x_num, core_num, slots, rows, cols = quad.shape
    return quad.transpose(3, 0, 1, 2, 4, 5).reshape(slots, y_num * x_num * core_num * rows, cols)


def y_groups():
    return [[y * XC_NUM + rest for y in range(Y_NUM)] for rest in range(XC_NUM)]


def gather_exchange(rows):
    size = lax.axis_size("dp")
    copies = jnp.broadcast_to(rows[None], (Y_NUM,) + rows.shape)
    over_y = lax.all_to_all(copies, "dp", 0, 0, axis_index_groups=y_groups())
    return finish_gather(over_y, size)


def gather_permutes(rows):
    size = lax.axis_size("dp")
    index = lax.axis_index("dp")
    y_index = index // XC_NUM
    pieces = [rows]
    for step in range(1, Y_NUM):
        pieces.append(
            lax.ppermute(rows, "dp", [(i, (i + step * XC_NUM) % size) for i in range(size)])
        )
    stacked = jnp.stack(pieces, 0)
    order = (y_index - jnp.arange(Y_NUM)) % Y_NUM
    over_y = stacked[order]
    return finish_gather(over_y, size)


def on_device(grad_parts, assign, left_basis, right_basis, left_stat, right_stat, moment, second):
    row_index = lax.axis_index("dp")
    owner_index = lax.axis_index("owner")
    dp_num = lax.axis_size("dp")
    owner_num = lax.axis_size("owner")
    col_num = grad_parts.shape[3]
    row_num = col_num // dp_num
    slot_cap = left_basis.shape[1]
    numbers = slot_numbers(assign)
    left_rows = left_basis[0]
    right_rows = right_basis[0]

    right_full = gather_permutes(right_rows)

    parts = lax.all_to_all(grad_parts.reshape(dp_num, row_num, col_num), "dp", 0, 0)
    left_cut = left_rows.reshape(slot_cap, row_num, dp_num, row_num).transpose(2, 0, 1, 3)
    left_cols = lax.all_to_all(left_cut, "dp", 0, 0)
    left_cols = left_cols.transpose(1, 3, 0, 2).reshape(slot_cap, row_num, col_num)

    grad_half = jnp.sum(parts.astype(jnp.float32), axis=0).astype(jnp.bfloat16)
    blocks = lax.all_to_all(
        jnp.broadcast_to(grad_half[None], (owner_num, row_num, col_num)), "owner", 0, 0
    )
    slot_range = jnp.arange(slot_cap, dtype=jnp.int32)
    pick = ((assign == owner_index)[None, :] & (numbers[None, :] == slot_range[:, None]))
    slot_grad = jnp.einsum(
        "sn,nrc->src",
        pick.astype(jnp.bfloat16),
        blocks,
        preferred_element_type=jnp.float32,
    ).astype(jnp.bfloat16)

    full_grad = gather_exchange(slot_grad)
    own_cols = lax.dynamic_slice_in_dim(full_grad, row_index * row_num, row_num, 2)
    left_term = jnp.einsum(
        "kab,knb->kan", slot_grad, full_grad, preferred_element_type=jnp.float32
    )
    right_term = jnp.einsum(
        "knc,knb->kcb", own_cols, full_grad, preferred_element_type=jnp.float32
    )
    turned = jnp.einsum("kcn,knb->kcb", left_cols, full_grad, preferred_element_type=jnp.float32)
    rotated = jnp.einsum(
        "kab,kbc->kac", turned.astype(jnp.bfloat16), right_full, preferred_element_type=jnp.float32
    )
    new_moment = beta_one * moment[0] + (1.0 - beta_one) * rotated
    new_second = beta_two * second[0] + (1.0 - beta_two) * rotated * rotated
    direction = (new_moment / bias_one / (jnp.sqrt(new_second / bias_two) + adam_eps)).astype(
        jnp.bfloat16
    )
    back_half = jnp.einsum(
        "kac,kbc->kab", direction, right_full, preferred_element_type=jnp.float32
    ).astype(jnp.bfloat16)
    back_full = gather_exchange(back_half)
    slot_update = jnp.einsum(
        "kan,knb->kab", left_rows, back_full, preferred_element_type=jnp.float32
    ).astype(jnp.bfloat16)

    home_pick = (numbers[:, None] == slot_range[None, :]) & (assign == owner_index)[:, None]
    outgoing = jnp.einsum(
        "os,src->orc",
        home_pick.astype(jnp.bfloat16),
        slot_update,
        preferred_element_type=jnp.float32,
    ).astype(jnp.bfloat16)
    incoming = lax.all_to_all(outgoing, "owner", 0, 0)
    update = lax.dynamic_index_in_dim(incoming, assign[owner_index], 0, keepdims=True)

    new_left = beta_two * left_stat[0] + (1.0 - beta_two) * left_term
    new_right = beta_two * right_stat[0] + (1.0 - beta_two) * right_term
    return (update, new_left[None], new_right[None], new_moment[None], new_second[None])


def solution(mesh):
    placed = (
        P("dp", "owner", None, None),
        P(),
        P("owner", None, "dp", None),
        P("owner", None, "dp", None),
        P("owner", None, "dp", None),
        P("owner", None, "dp", None),
        P("owner", None, "dp", None),
        P("owner", None, "dp", None),
    )
    return jax.shard_map(
        on_device,
        mesh=mesh,
        in_specs=placed,
        out_specs=(
            P("owner", "dp", None),
            P("owner", None, "dp", None),
            P("owner", None, "dp", None),
            P("owner", None, "dp", None),
            P("owner", None, "dp", None),
        ),
        check_vma=False,
    )
```

time: 468 us -> 187 us (0.40); the launches traced: 462 us -> 186 us
  waiting for transfers between devices: 356 us -> 57.9 us
  starting transfers between devices: 0.2 us -> 84.6 us
  blocking collectives: 74.8 us -> 17.5 us
  between operations: 13.9 us -> 3.09 us
  other arithmetic: 0.9 us -> 8.98 us
  matrix products: 10.3 us -> 5.08 us
    all_gather x4 -> x0, waiting for transfers between devices: 235 us -> none  [the longest x1 69.6 us: rotate_in(): piece_grad = lax.all_gather(grad_half, 'dp', axis=1, tiled=True)]
    unnamed x6 -> x0, waiting for transfers between devices: 121 us -> none
    all_gather x2 -> x0, blocking collectives: 74.8 us -> none  [the longest x1 39.4 us: on_device(): lax.all_gather(slot_update, 'owner', axis=0, tiled=True)]
    ppermute x0 -> x13, starting transfers between devices: none -> 50.9 us  [the longest x7 26.8 us: gather_permutes(): lax.ppermute(rows, 'dp', [(i, (i + step * XC_NUM) % size) for i in range(...]
    all_to_all x0 -> x5, waiting for transfers between devices: none -> 37.1 us  [the longest x1 11.5 us: on_device(): lax.all_to_all(jnp.broadcast_to(grad_half[None], (owner_num, row_num, col...]
    all_to_all x0 -> x5, starting transfers between devices: none -> 33.7 us  [the longest x1 12.1 us: on_device(): lax.all_to_all(jnp.broadcast_to(grad_half[None], (owner_num, row_num, col...]
    ppermute x0 -> x13, waiting for transfers between devices: none -> 20.8 us  [the longest x7 10.6 us: gather_permutes(): lax.ppermute(rows, 'dp', [(i, (i + step * XC_NUM) % size) for i in range(...]
    all_to_all x0 -> x1, blocking collectives: none -> 17.5 us  [gather_exchange(): over_y = lax.all_to_all(copies, 'dp', 0, 0, axis_index_groups=y_groups())]
  transfers between devices with their start and end apart: 5 -> 18, of which waited for: 5 -> 6; matrix products, arithmetic and copies ran while one was open for 1% -> 8% of each run, Pallas kernels for 0% -> 0%
where the time goes in v1:
time: 187 us; the launch traced here: 186 us
  starting transfers between devices  84.6 us (45%)
  waiting for transfers between devices  57.9 us (31%)
  blocking collectives  17.5 us (9%)
  local copies, waits for them, and re-layouts  9.08 us (5%)
  other arithmetic  8.98 us (5%)
  matrix products  5.08 us (3%)
  between operations  3.09 us (2%)
    ppermute x7, starting transfers between devices, gather_permutes(): lax.ppermute(rows, 'dp', [(i, (i + step * XC_NUM) % size) for i in range(...  26.8 us
    ppermute x6, starting transfers between devices, swap_bit(): return lax.ppermute(value, 'dp', [(i, i ^ bit) for i in range(size)])  24 us
    all_to_all x1, blocking collectives, gather_exchange(): over_y = lax.all_to_all(copies, 'dp', 0, 0, axis_index_groups=y_groups())  17.5 us
    all_to_all x1, starting transfers between devices, on_device(): lax.all_to_all(jnp.broadcast_to(grad_half[None], (owner_num, row_num, col...  12.1 us
    all_to_all x1, waiting for transfers between devices, on_device(): lax.all_to_all(jnp.broadcast_to(grad_half[None], (owner_num, row_num, col...  11.5 us
    ppermute x7, waiting for transfers between devices, gather_permutes(): lax.ppermute(rows, 'dp', [(i, (i + step * XC_NUM) % size) for i in range(...  10.6 us
    ppermute x6, waiting for transfers between devices, swap_bit(): return lax.ppermute(value, 'dp', [(i, i ^ bit) for i in range(size)])  10.2 us
    all_to_all x1, waiting for transfers between devices, on_device(): incoming = lax.all_to_all(outgoing, 'owner', 0, 0)  9.9 us
  transfers between devices with their start and end apart: 18, of which 6 were waited for; matrix products, arithmetic and copies ran while one was open for 8% of the time, Pallas kernels for 0%

profile of v1, /device:TPU:1, one launch (start us, length us, event | category | flops | bytes accessed | tf_op | source)
XLA Modules:
  0.0 186.2 jit_solution(2282272020419466639)
XLA Ops:
  0.6 5.9 %collective-permute-start.8 = (bf16[3,16,512]{2,1,0:T(8,128)(2,1)}, bf16[3,16,512]{2,1,0:T(8,128)(2,1)S(1)}, u32[]{:S(2)}, u32[]{:S(2)}) collective-permute-start(bf16[3,16,512]{2,1,0:T(8,128)(2,1)} %bitcast.123), channel_id=1, source_target_pairs={{0,448},{16,464},{32,480},{48,496},{64,0},{80,16},{96,32},{112,48}... | collective-permute-start | bytes 147464 | tf_op jit(solution)/shard_map/ppermute | solution.py:60
  6.6 3.8 %collective-permute-start.7 = (bf16[3,16,512]{2,1,0:T(8,128)(2,1)}, bf16[3,16,512]{2,1,0:T(8,128)(2,1)S(1)}, u32[]{:S(2)}, u32[]{:S(2)}) collective-permute-start(bf16[3,16,512]{2,1,0:T(8,128)(2,1)} %bitcast.124), channel_id=1, source_target_pairs={{0,384},{16,400},{32,416},{48,432},{64,448},{80,464},{96,480},{112... | collective-permute-start | bytes 147464 | tf_op jit(solution)/shard_map/ppermute | solution.py:60
  10.3 2.8 %collective-permute-start.6 = (bf16[3,16,512]{2,1,0:T(8,128)(2,1)}, bf16[3,16,512]{2,1,0:T(8,128)(2,1)S(1)}, u32[]{:S(2)}, u32[]{:S(2)}) collective-permute-start(bf16[3,16,512]{2,1,0:T(8,128)(2,1)} %bitcast.125), channel_id=1, source_target_pairs={{0,320},{16,336},{32,352},{48,368},{64,384},{80,400},{96,416},{112... | collective-permute-start | bytes 147464 | tf_op jit(solution)/shard_map/ppermute | solution.py:60
  13.1 5.7 %collective-permute-start.5 = (bf16[3,16,512]{2,1,0:T(8,128)(2,1)}, bf16[3,16,512]{2,1,0:T(8,128)(2,1)S(1)}, u32[]{:S(2)}, u32[]{:S(2)}) collective-permute-start(bf16[3,16,512]{2,1,0:T(8,128)(2,1)} %bitcast.126), channel_id=1, source_target_pairs={{0,256},{16,272},{32,288},{48,304},{64,320},{80,336},{96,352},{112... | collective-permute-start | bytes 147464 | tf_op jit(solution)/shard_map/ppermute | solution.py:60
  18.8 2.3 %collective-permute-start.2 = (bf16[3,16,512]{2,1,0:T(8,128)(2,1)}, bf16[3,16,512]{2,1,0:T(8,128)(2,1)S(1)}, u32[]{:S(2)}, u32[]{:S(2)}) collective-permute-start(bf16[3,16,512]{2,1,0:T(8,128)(2,1)} %bitcast.127), channel_id=1, source_target_pairs={{0,64},{16,80},{32,96},{48,112},{64,128},{80,144},{96,160},{112,17... | collective-permute-start | bytes 147464 | tf_op jit(solution)/shard_map/ppermute | solution.py:60
  21.1 7.5 %all-to-all-start = ((bf16[32,16,512]{2,1,0:T(8,128)(2,1)}), bf16[32,16,512]{2,1,0:T(8,128)(2,1)S(1)}, u32[]{:S(2)}, u32[]{:S(2)}) async-start(bf16[32,16,512]{2,1,0:T(8,128)(2,1)} %bitcast.122), calls=%async_computation | async-start | bytes 1048576 | tf_op jit(solution)/shard_map/all_to_all | solution.py:82
  31.1 4.2 %collective-permute-start.3 = (bf16[3,16,512]{2,1,0:T(8,128)(2,1)}, bf16[3,16,512]{2,1,0:T(8,128)(2,1)S(1)}, u32[]{:S(2)}, u32[]{:S(2)}) collective-permute-start(bf16[3,16,512]{2,1,0:T(8,128)(2,1)} %bitcast.128), channel_id=1, source_target_pairs={{0,128},{16,144},{32,160},{48,176},{64,192},{80,208},{96,224},{112... | collective-permute-start | bytes 147464 | tf_op jit(solution)/shard_map/ppermute | solution.py:60
  35.3 10.6 %collective-permute-done.3 = bf16[3,16,512]{2,1,0:T(8,128)(2,1)S(1)} collective-permute-done((bf16[3,16,512]{2,1,0:T(8,128)(2,1)}, bf16[3,16,512]{2,1,0:T(8,128)(2,1)S(1)}, u32[]{:S(2)}, u32[]{:S(2)}) %collective-permute-start.3) | collective-permute-done | bytes 49184 | tf_op jit(solution)/shard_map/ppermute | solution.py:60
  45.9 2.2 %collective-permute-start.4 = (bf16[3,16,512]{2,1,0:T(8,128)(2,1)}, bf16[3,16,512]{2,1,0:T(8,128)(2,1)S(1)}, u32[]{:S(2)}, u32[]{:S(2)}) collective-permute-start(bf16[3,16,512]{2,1,0:T(8,128)(2,1)} %bitcast.129), channel_id=1, source_target_pairs={{0,192},{16,208},{32,224},{48,240},{64,256},{80,272},{96,288},{112... | collective-permute-start | bytes 147464 | tf_op jit(solution)/shard_map/ppermute | solution.py:60
  49.0 12.1 %all-to-all-start.1 = ((bf16[16,16,512]{2,1,0:T(8,128)(2,1)}), bf16[16,16,512]{2,1,0:T(8,128)(2,1)S(1)}, u32[]{:S(2)}, u32[]{:S(2)}) async-start(bf16[16,16,512]{2,1,0:T(8,128)(2,1)} %broadcast_in_dim.14), calls=%async_computation.1 | async-start | bytes 524288 | tf_op jit(solution)/shard_map/all_to_all | solution.py:88
  61.2 11.5 %all-to-all-done.1 = bf16[16,16,512]{2,1,0:T(8,128)(2,1)S(1)} async-done(((bf16[16,16,512]{2,1,0:T(8,128)(2,1)}), bf16[16,16,512]{2,1,0:T(8,128)(2,1)S(1)}, u32[]{:S(2)}, u32[]{:S(2)}) %all-to-all-start.1) | async-done | bytes 262176 | tf_op jit(solution)/shard_map/all_to_all | solution.py:88
  73.7 5.1 %all-to-all-start.2 = ((bf16[8,3,16,512]{3,2,1,0:T(8,128)(2,1)}), bf16[8,3,16,512]{3,2,1,0:T(8,128)(2,1)S(1)}, u32[]{:S(2)}, u32[]{:S(2)}) async-start(bf16[8,3,16,512]{3,2,1,0:T(8,128)(2,1)} %broadcast_in_dim.15), calls=%async_computation.2 | async-start | bytes 786432 | tf_op jit(solution)/shard_map/all_to_all | solution.py:49
  79.5 2.5 %collective-permute-start.9 = (bf16[8,3,16,512]{3,2,1,0:T(8,128)(2,1)S(1)}, bf16[8,3,16,512]{3,2,1,0:T(8,128)(2,1)S(1)}, u32[]{:S(2)}, u32[]{:S(2)}) collective-permute-start(bf16[8,3,16,512]{3,2,1,0:T(8,128)(2,1)S(1)} %gather_fusion), channel_id=1, source_target_pairs={{0,32},{16,48},{32,0},{48,16},{64,96},{80,112},{96,64},{112,80},{1... | collective-permute-start | bytes 1179656 | tf_op jit(solution)/shard_map/ppermute | solution.py:25
  82.0 7.5 %all-to-all-done.2 = bf16[8,3,16,512]{3,2,1,0:T(8,128)(2,1)S(1)} async-done(((bf16[8,3,16,512]{3,2,1,0:T(8,128)(2,1)}), bf16[8,3,16,512]{3,2,1,0:T(8,128)(2,1)S(1)}, u32[]{:S(2)}, u32[]{:S(2)}) %all-to-all-start.2) | async-done | bytes 393248 | tf_op jit(solution)/shard_map/all_to_all | solution.py:49
  89.5 2.5 %collective-permute-start = (bf16[8,3,16,512]{3,2,1,0:T(8,128)(2,1)S(1)}, bf16[8,3,16,512]{3,2,1,0:T(8,128)(2,1)S(1)}, u32[]{:S(2)}, u32[]{:S(2)}) collective-permute-start(bf16[8,3,16,512]{3,2,1,0:T(8,128)(2,1)S(1)} %all-to-all-done.2), channel_id=1, source_target_pairs={{0,32},{16,48},{32,0},{48,16},{64,96},{80,112},{96,64},{112,80},{1... | collective-permute-start | bytes 1179656 | tf_op jit(solution)/shard_map/ppermute | solution.py:25
  92.2 7.2 %collective-permute-start.10 = (bf16[8,2,3,16,512]{4,3,2,0,1:T(8,128)(2,1)S(1)}, bf16[8,2,3,16,512]{4,3,2,0,1:T(8,128)(2,1)}, u32[]{:S(2)}, u32[]{:S(2)}) collective-permute-start(bf16[8,2,3,16,512]{4,3,2,0,1:T(8,128)(2,1)S(1)} %maximum_select_fusion.6), channel_id=1, source_target_pairs={{0,16},{16,0},{32,48},{48,32},{64,80},{80,64},{96,112},{112,96},{1... | collective-permute-start | bytes 2359304 | tf_op jit(solution)/shard_map/ppermute | solution.py:25
  100.5 6.6 %collective-permute-start.1 = (bf16[8,2,3,16,512]{4,3,2,0,1:T(8,128)(2,1)}, bf16[8,2,3,16,512]{4,3,2,0,1:T(8,128)(2,1)}, u32[]{:S(2)}, u32[]{:S(2)}) collective-permute-start(bf16[8,2,3,16,512]{4,3,2,0,1:T(8,128)(2,1)} %maximum_select_fusion.4), channel_id=1, source_target_pairs={{0,16},{16,0},{32,48},{48,32},{64,80},{80,64},{96,112},{112,96},{1... | collective-permute-start | bytes 2359304 | tf_op jit(solution)/shard_map/ppermute | solution.py:25
  108.7 4.8 %all-to-all-start.3 = ((bf16[32,2,384]{2,1,0:T(2,128)(2,1)}), bf16[32,2,384]{2,1,0:T(2,128)(2,1)S(1)}, u32[]{:S(2)}, u32[]{:S(2)}) async-start(bf16[32,2,384]{2,1,0:T(2,128)(2,1)} %reshape.283), calls=%async_computation.3 | async-start | bytes 98304 | tf_op jit(solution)/shard_map/all_to_all | solution.py:84
  113.5 8.1 %all-to-all-done.3 = bf16[32,2,384]{2,1,0:T(2,128)(2,1)S(1)} async-done(((bf16[32,2,384]{2,1,0:T(2,128)(2,1)}), bf16[32,2,384]{2,1,0:T(2,128)(2,1)S(1)}, u32[]{:S(2)}, u32[]{:S(2)}) %all-to-all-start.3) | async-done | bytes 49184 | tf_op jit(solution)/shard_map/all_to_all | solution.py:84
  129.5 17.5 %all_to_all.30 = bf16[8,3,16,512]{3,2,1,0:T(8,128)(2,1)S(1)} all-to-all(bf16[8,3,16,512]{3,2,1,0:T(8,128)(2,1)S(1)} %broadcast_in_dim.16), channel_id=1, replica_groups={{0,64,128,192,256,320,384,448},{16,80,144,208,272,336,400,464},{32,96,1..., dimensions={0} | all-to-all | bytes 786432 | tf_op jit(solution)/shard_map/all_to_all | solution.py:49
  149.0 10.1 %collective-permute-done.11 = bf16[8,3,16,512]{3,2,1,0:T(8,128)(2,1)S(1)} collective-permute-done((bf16[8,3,16,512]{3,2,1,0:T(8,128)(2,1)S(1)}, bf16[8,3,16,512]{3,2,1,0:T(8,128)(2,1)S(1)}, u32[]{:S(2)}, u32[]{:S(2)}) %collective-permute-start.11) | collective-permute-done | bytes 393248 | tf_op jit(solution)/shard_map/ppermute | solution.py:25
  159.3 3.3 %collective-permute-start.12 = (bf16[8,2,3,16,512]{4,3,2,0,1:T(8,128)(2,1)S(1)}, bf16[8,2,3,16,512]{4,3,2,0,1:T(8,128)(2,1)}, u32[]{:S(2)}, u32[]{:S(2)}) collective-permute-start(bf16[8,2,3,16,512]{4,3,2,0,1:T(8,128)(2,1)S(1)} %maximum_select_fusion.7), channel_id=1, source_target_pairs={{0,16},{16,0},{32,48},{48,32},{64,80},{80,64},{96,112},{112,96},{1... | collective-permute-start | bytes 2359304 | tf_op jit(solution)/shard_map/ppermute | solution.py:25
  168.5 4.1 %all-to-all-start.5 = ((bf16[16,16,512]{2,1,0:T(8,128)(2,1)}), bf16[16,16,512]{2,1,0:T(8,128)(2,1)S(1)}, u32[]{:S(2)}, u32[]{:S(2)}) async-start(bf16[16,16,512]{2,1,0:T(8,128)(2,1)} %copy.83), calls=%async_computation.5 | async-start | bytes 524288 | tf_op jit(solution)/shard_map/all_to_all | solution.py:132
  175.7 9.9 %all-to-all-done.5 = bf16[16,16,512]{2,1,0:T(8,128)(2,1)S(1)} async-done(((bf16[16,16,512]{2,1,0:T(8,128)(2,1)}), bf16[16,16,512]{2,1,0:T(8,128)(2,1)S(1)}, u32[]{:S(2)}, u32[]{:S(2)}) %all-to-all-start.5) | async-done | bytes 262176 | tf_op jit(solution)/shard_map/all_to_all | solution.py:132
  (72 shorter events, 25.1 us)
Async XLA Ops:
  0.6 78.2 %collective-permute-start.8 = (bf16[3,16,512]{2,1,0:T(8,128)(2,1)}, bf16[3,16,512]{2,1,0:T(8,128)(2,1)S(1)}, u32[]{:S(2)}, u32[]{:S(2)}) collective-permute-start(bf16[3,16,512]{2,1,0:T(8,128)(2,1)} %bitcast.123), channel_id=1, source_target_pairs={{0,448},{16,464},{32,480},{48,496},{64,0},{80,16},{96,32},{112,48}... | collective-permute-start | bytes 147464 | tf_op jit(solution)/shard_map/ppermute | solution.py:60
  6.6 72.3 %collective-permute-start.7 = (bf16[3,16,512]{2,1,0:T(8,128)(2,1)}, bf16[3,16,512]{2,1,0:T(8,128)(2,1)S(1)}, u32[]{:S(2)}, u32[]{:S(2)}) collective-permute-start(bf16[3,16,512]{2,1,0:T(8,128)(2,1)} %bitcast.124), channel_id=1, source_target_pairs={{0,384},{16,400},{32,416},{48,432},{64,448},{80,464},{96,480},{112... | collective-permute-start | bytes 147464 | tf_op jit(solution)/shard_map/ppermute | solution.py:60
  10.3 50.8 %collective-permute-start.6 = (bf16[3,16,512]{2,1,0:T(8,128)(2,1)}, bf16[3,16,512]{2,1,0:T(8,128)(2,1)S(1)}, u32[]{:S(2)}, u32[]{:S(2)}) collective-permute-start(bf16[3,16,512]{2,1,0:T(8,128)(2,1)} %bitcast.125), channel_id=1, source_target_pairs={{0,320},{16,336},{32,352},{48,368},{64,384},{80,400},{96,416},{112... | collective-permute-start | bytes 147464 | tf_op jit(solution)/shard_map/ppermute | solution.py:60
  13.1 48.0 %collective-permute-start.5 = (bf16[3,16,512]{2,1,0:T(8,128)(2,1)}, bf16[3,16,512]{2,1,0:T(8,128)(2,1)S(1)}, u32[]{:S(2)}, u32[]{:S(2)}) collective-permute-start(bf16[3,16,512]{2,1,0:T(8,128)(2,1)} %bitcast.126), channel_id=1, source_target_pairs={{0,256},{16,272},{32,288},{48,304},{64,320},{80,336},{96,352},{112... | collective-permute-start | bytes 147464 | tf_op jit(solution)/shard_map/ppermute | solution.py:60
  18.8 12.3 %collective-permute-start.2 = (bf16[3,16,512]{2,1,0:T(8,128)(2,1)}, bf16[3,16,512]{2,1,0:T(8,128)(2,1)S(1)}, u32[]{:S(2)}, u32[]{:S(2)}) collective-permute-start(bf16[3,16,512]{2,1,0:T(8,128)(2,1)} %bitcast.127), channel_id=1, source_target_pairs={{0,64},{16,80},{32,96},{48,112},{64,128},{80,144},{96,160},{112,17... | collective-permute-start | bytes 147464 | tf_op jit(solution)/shard_map/ppermute | solution.py:60
  21.1 27.1 %all-to-all-start = ((bf16[32,16,512]{2,1,0:T(8,128)(2,1)}), bf16[32,16,512]{2,1,0:T(8,128)(2,1)S(1)}, u32[]{:S(2)}, u32[]{:S(2)}) async-start(bf16[32,16,512]{2,1,0:T(8,128)(2,1)} %bitcast.122), calls=%async_computation | async-start | bytes 1048576 | tf_op jit(solution)/shard_map/all_to_all | solution.py:82
  31.1 14.9 %collective-permute-start.3 = (bf16[3,16,512]{2,1,0:T(8,128)(2,1)}, bf16[3,16,512]{2,1,0:T(8,128)(2,1)S(1)}, u32[]{:S(2)}, u32[]{:S(2)}) collective-permute-start(bf16[3,16,512]{2,1,0:T(8,128)(2,1)} %bitcast.128), channel_id=1, source_target_pairs={{0,128},{16,144},{32,160},{48,176},{64,192},{80,208},{96,224},{112... | collective-permute-start | bytes 147464 | tf_op jit(solution)/shard_map/ppermute | solution.py:60
  45.9 15.1 %collective-permute-start.4 = (bf16[3,16,512]{2,1,0:T(8,128)(2,1)}, bf16[3,16,512]{2,1,0:T(8,128)(2,1)S(1)}, u32[]{:S(2)}, u32[]{:S(2)}) collective-permute-start(bf16[3,16,512]{2,1,0:T(8,128)(2,1)} %bitcast.129), channel_id=1, source_target_pairs={{0,192},{16,208},{32,224},{48,240},{64,256},{80,272},{96,288},{112... | collective-permute-start | bytes 147464 | tf_op jit(solution)/shard_map/ppermute | solution.py:60
  49.0 23.7 %all-to-all-start.1 = ((bf16[16,16,512]{2,1,0:T(8,128)(2,1)}), bf16[16,16,512]{2,1,0:T(8,128)(2,1)S(1)}, u32[]{:S(2)}, u32[]{:S(2)}) async-start(bf16[16,16,512]{2,1,0:T(8,128)(2,1)} %broadcast_in_dim.14), calls=%async_computation.1 | async-start | bytes 524288 | tf_op jit(solution)/shard_map/all_to_all | solution.py:88
  73.7 15.8 %all-to-all-start.2 = ((bf16[8,3,16,512]{3,2,1,0:T(8,128)(2,1)}), bf16[8,3,16,512]{3,2,1,0:T(8,128)(2,1)S(1)}, u32[]{:S(2)}, u32[]{:S(2)}) async-start(bf16[8,3,16,512]{3,2,1,0:T(8,128)(2,1)} %broadcast_in_dim.15), calls=%async_computation.2 | async-start | bytes 786432 | tf_op jit(solution)/shard_map/all_to_all | solution.py:49
  79.5 12.6 %collective-permute-start.9 = (bf16[8,3,16,512]{3,2,1,0:T(8,128)(2,1)S(1)}, bf16[8,3,16,512]{3,2,1,0:T(8,128)(2,1)S(1)}, u32[]{:S(2)}, u32[]{:S(2)}) collective-permute-start(bf16[8,3,16,512]{3,2,1,0:T(8,128)(2,1)S(1)} %gather_fusion), channel_id=1, source_target_pairs={{0,32},{16,48},{32,0},{48,16},{64,96},{80,112},{96,64},{112,80},{1... | collective-permute-start | bytes 1179656 | tf_op jit(solution)/shard_map/ppermute | solution.py:25
  89.5 10.0 %collective-permute-start = (bf16[8,3,16,512]{3,2,1,0:T(8,128)(2,1)S(1)}, bf16[8,3,16,512]{3,2,1,0:T(8,128)(2,1)S(1)}, u32[]{:S(2)}, u32[]{:S(2)}) collective-permute-start(bf16[8,3,16,512]{3,2,1,0:T(8,128)(2,1)S(1)} %all-to-all-done.2), channel_id=1, source_target_pairs={{0,32},{16,48},{32,0},{48,16},{64,96},{80,112},{96,64},{112,80},{1... | collective-permute-start | bytes 1179656 | tf_op jit(solution)/shard_map/ppermute | solution.py:25
  92.1 15.1 %copy-start.2 = (bf16[1,3,16,512]{3,2,1,0:T(8,128)(2,1)S(1)}, bf16[1,3,16,512]{3,2,1,0:T(8,128)(2,1)}, u32[]{:S(2)}) copy-start(bf16[1,3,16,512]{3,2,1,0:T(8,128)(2,1)} %param.10) | copy-start | bytes 147460
  92.2 31.6 %collective-permute-start.10 = (bf16[8,2,3,16,512]{4,3,2,0,1:T(8,128)(2,1)S(1)}, bf16[8,2,3,16,512]{4,3,2,0,1:T(8,128)(2,1)}, u32[]{:S(2)}, u32[]{:S(2)}) collective-permute-start(bf16[8,2,3,16,512]{4,3,2,0,1:T(8,128)(2,1)S(1)} %maximum_select_fusion.6), channel_id=1, source_target_pairs={{0,16},{16,0},{32,48},{48,32},{64,80},{80,64},{96,112},{112,96},{1... | collective-permute-start | bytes 2359304 | tf_op jit(solution)/shard_map/ppermute | solution.py:25
  100.5 25.3 %collective-permute-start.1 = (bf16[8,2,3,16,512]{4,3,2,0,1:T(8,128)(2,1)}, bf16[8,2,3,16,512]{4,3,2,0,1:T(8,128)(2,1)}, u32[]{:S(2)}, u32[]{:S(2)}) collective-permute-start(bf16[8,2,3,16,512]{4,3,2,0,1:T(8,128)(2,1)} %maximum_select_fusion.4), channel_id=1, source_target_pairs={{0,16},{16,0},{32,48},{48,32},{64,80},{80,64},{96,112},{112,96},{1... | collective-permute-start | bytes 2359304 | tf_op jit(solution)/shard_map/ppermute | solution.py:25
  108.7 13.0 %all-to-all-start.3 = ((bf16[32,2,384]{2,1,0:T(2,128)(2,1)}), bf16[32,2,384]{2,1,0:T(2,128)(2,1)S(1)}, u32[]{:S(2)}, u32[]{:S(2)}) async-start(bf16[32,2,384]{2,1,0:T(2,128)(2,1)} %reshape.283), calls=%async_computation.3 | async-start | bytes 98304 | tf_op jit(solution)/shard_map/all_to_all | solution.py:84
  127.6 1.4 copy-start
  127.6 1.4 copy-start.1
  129.5 33.1 %copy-start.5 = (s32[16]{0:T(128)S(1)}, s32[16]{0:T(128)}, u32[]{:S(2)}) copy-start(s32[16]{0:T(128)} %param.9) | copy-start | bytes 196
  147.1 12.1 %collective-permute-start.11 = (bf16[8,3,16,512]{3,2,1,0:T(8,128)(2,1)S(1)}, bf16[8,3,16,512]{3,2,1,0:T(8,128)(2,1)S(1)}, u32[]{:S(2)}, u32[]{:S(2)}) collective-permute-start(bf16[8,3,16,512]{3,2,1,0:T(8,128)(2,1)S(1)} %all_to_all.30), channel_id=1, source_target_pairs={{0,32},{16,48},{32,0},{48,16},{64,96},{80,112},{96,64},{112,80},{1... | collective-permute-start | bytes 1179656 | tf_op jit(solution)/shard_map/ppermute | solution.py:25
  159.3 6.0 %collective-permute-start.12 = (bf16[8,2,3,16,512]{4,3,2,0,1:T(8,128)(2,1)S(1)}, bf16[8,2,3,16,512]{4,3,2,0,1:T(8,128)(2,1)}, u32[]{:S(2)}, u32[]{:S(2)}) collective-permute-start(bf16[8,2,3,16,512]{4,3,2,0,1:T(8,128)(2,1)S(1)} %maximum_select_fusion.7), channel_id=1, source_target_pairs={{0,16},{16,0},{32,48},{48,32},{64,80},{80,64},{96,112},{112,96},{1... | collective-permute-start | bytes 2359304 | tf_op jit(solution)/shard_map/ppermute | solution.py:25
  167.0 5.6 %copy-start.4 = (f32[1,3,16,512]{3,2,1,0:T(8,128)S(1)}, f32[1,3,16,512]{3,2,1,0:T(8,128)}, u32[]{:S(2)}) copy-start(f32[1,3,16,512]{3,2,1,0:T(8,128)} %param.13) | copy-start | bytes 294916
  167.3 6.5 %copy-start.3 = (f32[1,3,16,512]{3,2,1,0:T(8,128)S(1)}, f32[1,3,16,512]{3,2,1,0:T(8,128)}, u32[]{:S(2)}) copy-start(f32[1,3,16,512]{3,2,1,0:T(8,128)} %param.12) | copy-start | bytes 294916
  168.5 17.1 %all-to-all-start.5 = ((bf16[16,16,512]{2,1,0:T(8,128)(2,1)}), bf16[16,16,512]{2,1,0:T(8,128)(2,1)S(1)}, u32[]{:S(2)}, u32[]{:S(2)}) async-start(bf16[16,16,512]{2,1,0:T(8,128)(2,1)} %copy.83), calls=%async_computation.5 | async-start | bytes 524288 | tf_op jit(solution)/shard_map/all_to_all | solution.py:132

commit v2 on v0

v2 whole, which is shorter than its diff:
```python
import jax
import jax.numpy as jnp
from jax import lax
from jax.sharding import PartitionSpec as P

beta_one = 0.9
beta_two = 0.95
step_count = 10.0
adam_eps = 1e-08
bias_one = 1.0 - beta_one**step_count
bias_two = 1.0 - beta_two**step_count

LANES = 128
half = jnp.bfloat16


def slot_numbers(assign):
    positions = jnp.arange(assign.shape[0], dtype=jnp.int32)
    matching = assign[:, None] == assign[None, :]
    earlier = positions[None, :] < positions[:, None]
    return jnp.sum((matching & earlier).astype(jnp.int32), axis=1)


def swap_cores(value):
    return lax.ppermute(value, "dp", [(i, i ^ 1) for i in range(lax.axis_size("dp"))])


def exchange(pieces, both_dp):
    chips = lax.axis_size("dp") // 2
    owners = lax.axis_size("owner")
    place = lambda chip, core, owner: (chip * 2 + core) * owners + owner
    groups = [[place(chip, 0, owner) for chip in range(chips)] for owner in range(owners)]
    if both_dp:
        groups += [[place(chip, 1, owner) for chip in range(chips)] for owner in range(owners)]
    else:
        groups += [[place(chip, 1, owner) for owner in range(owners)] for chip in range(chips)]
    return lax.all_to_all(pieces, ("dp", "owner"), 0, 0, axis_index_groups=groups)


def copies(value, count):
    return jnp.broadcast_to(value[None], (count,) + value.shape)


def dot(left, right, contract):
    return lax.dot_general(
        left, right, ((contract[:1], contract[1:]), ((), ())), preferred_element_type=jnp.float32
    )


def on_device(grad_parts, assign, left_basis, right_basis, left_stat, right_stat, moment, second):
    row_index = lax.axis_index("dp")
    owner = lax.axis_index("owner")
    dp_num = lax.axis_size("dp")
    owner_num = lax.axis_size("owner")
    col_num = grad_parts.shape[3]
    row_num = col_num // dp_num
    slot_cap = left_basis.shape[1]
    chunk_num = col_num // LANES
    chips = dp_num // 2
    chip = row_index // 2
    first = row_index % 2 == 0
    chip_rows = 2 * row_num
    kinds = 4

    grads = grad_parts[0, 0]
    slots = jnp.stack(
        [left_basis[0], right_basis[0], moment[0].astype(half), second[0].astype(half)], 1
    )
    slot_rows = slots.reshape(-1, col_num)
    came = swap_cores(
        jnp.where(first, jnp.concatenate([slot_rows, grads[slot_rows.shape[0] :]], 0), grads)
    )
    numbers = slot_numbers(assign)
    chip_grads = jnp.stack(
        [grads.reshape(chips, chip_rows, col_num), came.reshape(chips, chip_rows, col_num)], 1
    ).reshape(chips, 2 * chip_rows, col_num)
    chip_grads = jnp.concatenate([chip_grads, chip_grads], 1)
    chip_slots = jnp.stack([came[: slot_rows.shape[0]].reshape(slots.shape), slots], 2)
    chip_slots = chip_slots.reshape(slot_cap, kinds * chip_rows, col_num)
    number = numbers[:, None, None]
    picked = chip_slots[0][None]
    for slot in range(1, slot_cap):
        picked = jnp.where(number == slot, chip_slots[slot][None], picked)

    parts = exchange(jnp.where(first, chip_grads, picked), False)
    grad_rows = jnp.sum(
        parts[:, : 2 * chip_rows].reshape(2 * chips, chip_rows, col_num).astype(jnp.float32), axis=0
    ).astype(half)
    home = lax.dynamic_index_in_dim(parts, assign[owner], 0, keepdims=False)
    home_came = swap_cores(home)

    left_rows, right_rows = home.reshape(kinds, chip_rows, col_num)[:2]
    left_chunks = left_rows.reshape(chip_rows, chunk_num, LANES).transpose(1, 0, 2)
    left_chunks = jnp.broadcast_to(
        left_chunks[:, None], (chunk_num, chips // chunk_num, chip_rows, LANES)
    ).reshape(chips, chip_rows, LANES)
    rows = copies(jnp.where(first, grad_rows, right_rows), chips)
    mine = exchange(jnp.concatenate([rows, left_chunks], 2), True)
    mine = mine.reshape(col_num, col_num + LANES)
    other = swap_cores(mine)
    grad_full = jnp.where(first, mine[:, :col_num], other[:, :col_num])
    right_full = jnp.where(first, other[:, :col_num], mine[:, :col_num])
    left_cols = jnp.where(first, other[:, col_num:], mine[:, col_num:])
    home = jnp.where(first, home_came, home).reshape(kinds, chip_rows, col_num)

    chunk = chip // (chips // chunk_num)
    in_chunk = (chip % (chips // chunk_num)) * chip_rows
    own_rows = lambda value: lax.dynamic_slice_in_dim(value, in_chunk, chip_rows, 0)
    turned = own_rows(dot(left_cols, grad_full, (0, 0)).astype(half))
    rotated = dot(turned, right_full, (1, 0))
    home_moment = beta_one * home[2].astype(jnp.float32) + (1.0 - beta_one) * rotated
    home_second = beta_two * home[3].astype(jnp.float32) + (1.0 - beta_two) * rotated * rotated
    direction = (home_moment / bias_one / (jnp.sqrt(home_second / bias_two) + adam_eps)).astype(half)
    back_rows = dot(direction, right_full, (1, 1)).astype(half)
    grad_cols = lax.dynamic_slice_in_dim(grad_full, chunk * LANES, LANES, 1)
    chip_grad_rows = lax.dynamic_slice_in_dim(grad_full, chip * chip_rows, chip_rows, 0)
    left_term = dot(chip_grad_rows, grad_full, (1, 1)).astype(half)
    right_term = own_rows(dot(grad_cols, grad_full, (0, 0)).astype(half))

    results = jnp.concatenate(
        [jnp.where(first, back_rows, left_term), right_term, rotated.astype(half)], 0
    )
    gathered = exchange(copies(results, chips), False)
    back_full = gathered[:, :chip_rows].reshape(col_num, col_num)
    chip_update = dot(home[0], back_full, (1, 0)).astype(half)
    held = (assign == owner)[None, :] & (
        numbers[None, :] == jnp.arange(slot_cap, dtype=jnp.int32)[:, None]
    )
    chip_results = jnp.sum(
        jnp.where(held[:, :, None, None], gathered[None].astype(jnp.float32), 0.0), axis=1
    ).astype(half)
    chip_results = chip_results.reshape(slot_cap, 3, 2, row_num, col_num)
    for_first = chip_results[:, :, 0].reshape(-1, col_num)
    for_second = jnp.concatenate([chip_update[row_num:], for_first[row_num:]], 0)
    came = swap_cores(jnp.where(first, for_second, for_first))
    update = jnp.where(first, chip_update[:row_num], came[:row_num])
    terms = jnp.where(
        first, came.reshape(slot_cap, 3, row_num, col_num), chip_results[:, :, 1]
    ).astype(jnp.float32)

    new_left = beta_two * left_stat[0] + (1.0 - beta_two) * terms[:, 0]
    new_right = beta_two * right_stat[0] + (1.0 - beta_two) * terms[:, 1]
    new_moment = beta_one * moment[0] + (1.0 - beta_one) * terms[:, 2]
    new_second = beta_two * second[0] + (1.0 - beta_two) * terms[:, 2] * terms[:, 2]
    return (update[None], new_left[None], new_right[None], new_moment[None], new_second[None])


def solution(mesh):
    placed = (
        P("dp", "owner", None, None),
        P(),
        P("owner", None, "dp", None),
        P("owner", None, "dp", None),
        P("owner", None, "dp", None),
        P("owner", None, "dp", None),
        P("owner", None, "dp", None),
        P("owner", None, "dp", None),
    )
    return jax.shard_map(
        on_device,
        mesh=mesh,
        in_specs=placed,
        out_specs=(
            P("owner", "dp", None),
            P("owner", None, "dp", None),
            P("owner", None, "dp", None),
            P("owner", None, "dp", None),
            P("owner", None, "dp", None),
        ),
        check_vma=False,
    )
```

time: 468 us -> 134 us (0.29); the launches traced: 462 us -> 134 us
  waiting for transfers between devices: 356 us -> 57 us
  blocking collectives: 74.8 us -> 26.1 us
  starting transfers between devices: 0.2 us -> 34 us
  between operations: 13.9 us -> 3.03 us
  matrix products: 10.3 us -> 1.44 us
  other arithmetic: 0.9 us -> 8.88 us
    all_gather x4 -> x0, waiting for transfers between devices: 235 us -> none  [the longest x1 69.6 us: rotate_in(): piece_grad = lax.all_gather(grad_half, 'dp', axis=1, tiled=True)]
    unnamed x6 -> x0, waiting for transfers between devices: 121 us -> none
    all_gather x2 -> x0, blocking collectives: 74.8 us -> none  [the longest x1 39.4 us: on_device(): lax.all_gather(slot_update, 'owner', axis=0, tiled=True)]
    all_to_all x0 -> x2, waiting for transfers between devices: none -> 53.3 us  [exchange(): lax.all_to_all(pieces, ('dp', 'owner'), 0, 0, axis_index_groups=groups)]
    all_to_all x0 -> x1, blocking collectives: none -> 26.1 us  [exchange(): lax.all_to_all(pieces, ('dp', 'owner'), 0, 0, axis_index_groups=groups)]
    all_to_all x0 -> x2, starting transfers between devices: none -> 18.9 us  [exchange(): lax.all_to_all(pieces, ('dp', 'owner'), 0, 0, axis_index_groups=groups)]
    ppermute x0 -> x4, starting transfers between devices: none -> 15 us  [swap_cores(): lax.ppermute(value, 'dp', [(i, i ^ 1) for i in range(lax.axis_size('dp'))])]
    dot_general x7 -> x6, matrix products: 10.3 us -> 1.44 us  [dot(): lax.dot_general(left, right, ((contract[:1], contract[1:]), ((), ())), pr...]
  transfers between devices with their start and end apart: 5 -> 6, of which waited for: 5 -> 5; matrix products, arithmetic and copies ran while one was open for 1% -> 1% of each run, Pallas kernels for 0% -> 0%
where the time goes in v2:
time: 134 us
  waiting for transfers between devices  57 us (43%)
  starting transfers between devices  34 us (25%)
  blocking collectives  26.1 us (19%)
  other arithmetic  8.88 us (7%)
  local copies, waits for them, and re-layouts  3.35 us (2%)
  between operations  3.03 us (2%)
  matrix products  1.44 us (1%)
    all_to_all x2, waiting for transfers between devices, exchange(): lax.all_to_all(pieces, ('dp', 'owner'), 0, 0, axis_index_groups=groups)  53.3 us
    all_to_all x1, blocking collectives, exchange(): lax.all_to_all(pieces, ('dp', 'owner'), 0, 0, axis_index_groups=groups)  26.1 us
    all_to_all x2, starting transfers between devices, exchange(): lax.all_to_all(pieces, ('dp', 'owner'), 0, 0, axis_index_groups=groups)  18.9 us
    ppermute x4, starting transfers between devices, swap_cores(): lax.ppermute(value, 'dp', [(i, i ^ 1) for i in range(lax.axis_size('dp'))])  15 us
    ppermute x4, waiting for transfers between devices, swap_cores(): lax.ppermute(value, 'dp', [(i, i ^ 1) for i in range(lax.axis_size('dp'))])  3.69 us
  transfers between devices with their start and end apart: 6, of which 5 were waited for; matrix products, arithmetic and copies ran while one was open for 1% of the time, Pallas kernels for 0%

profile of v2, /device:TPU:1, one launch (start us, length us, event | category | flops | bytes accessed | tf_op | source)
XLA Modules:
  0.0 133.8 jit_solution(12339015164632355146)
XLA Ops:
  0.7 1.0 slice_bitcast_fusion
  1.7 1.0 convert_bitcast_fusion
  2.6 0.9 fusion.50
  3.5 1.2 maximum_select_fusion.1
  4.7 8.8 %collective-permute-start = (bf16[512,512]{1,0:T(8,128)(2,1)S(1)}, bf16[512,512]{1,0:T(8,128)(2,1)S(1)}, u32[]{:S(2)}, u32[]{:S(2)}) collective-permute-start(bf16[512,512]{1,0:T(8,128)(2,1)S(1)} %maximum_select_fusion.1), channel_id=1, source_target_pairs={{0,16},{16,0},{32,48},{48,32},{64,80},{80,64},{96,112},{112,96},{1... | collective-permute-start | bytes 1572872 | tf_op jit(solution)/shard_map/ppermute | solution.py:25
  13.7 1.3 collective-permute-done
  15.4 2.3 %maximum_select_fusion = bf16[16,128,512]{2,1,0:T(8,128)(2,1)} fusion(bf16[16,64,512]{2,1,0:T(8,128)(2,1)S(1)} %bitcast.81, pred[16]{0:T(512)(128)(4,1)S(1)} %get-tuple-element.17, pred[16]{0:T(512)(128)(4,1)S(1)} %get-tuple-element.16, pred[]{:T(512)S(6)} %eq.58, bf16[128,512]{1,0:T(8,128)(2,1)S(1)} %bitcast.97, bf16[128,512]{1,0:T(8,128)(2,1)S(1)} %bitcast.98, ...), kind=kLoop, calls=%fused_computation.1 | loop fusion | flops 7340032 | bytes 3538977 | tf_op jit(solution)/shard_map/jit(_where)/select_n | solution.py:85
  17.7 7.2 %all-to-all-start = ((bf16[16,128,512]{2,1,0:T(8,128)(2,1)}), bf16[16,128,512]{2,1,0:T(8,128)(2,1)S(1)}, u32[]{:S(2)}, u32[]{:S(2)}) async-start(bf16[16,128,512]{2,1,0:T(8,128)(2,1)} %maximum_select_fusion), calls=%async_computation | async-start | bytes 4194304 | tf_op jit(solution)/shard_map/all_to_all | solution.py:37
  24.9 0.6 dynamic_slice.19
  27.4 29.8 %all-to-all-done = bf16[16,128,512]{2,1,0:T(8,128)(2,1)S(1)} async-done(((bf16[16,128,512]{2,1,0:T(8,128)(2,1)}), bf16[16,128,512]{2,1,0:T(8,128)(2,1)S(1)}, u32[]{:S(2)}, u32[]{:S(2)}) %all-to-all-start) | async-done | bytes 2097184 | tf_op jit(solution)/shard_map/all_to_all | solution.py:37
  57.7 26.1 %all_to_all.15 = bf16[16,32,640]{2,1,0:T(8,128)(2,1)S(1)} all-to-all(bf16[16,32,640]{2,1,0:T(8,128)(2,1)S(1)} %pad_maximum_fusion.1), channel_id=1, replica_groups={{0,32,64,96,128,160,192,224,256,288,320,352,384,416,448,480},{1,33,65,9..., dimensions={0} | all-to-all | bytes 1310720 | tf_op jit(solution)/shard_map/all_to_all | solution.py:37
  83.8 1.9 %collective-permute-start.2 = (bf16[512,640]{1,0:T(8,128)(2,1)S(1)}, bf16[512,640]{1,0:T(8,128)(2,1)S(1)}, u32[]{:S(2)}, u32[]{:S(2)}) collective-permute-start(bf16[512,640]{1,0:T(8,128)(2,1)S(1)} %bitcast.83), channel_id=1, source_target_pairs={{0,16},{16,0},{32,48},{48,32},{64,80},{80,64},{96,112},{112,96},{1... | collective-permute-start | bytes 1966088 | tf_op jit(solution)/shard_map/ppermute | solution.py:25
  85.7 2.4 %collective-permute-start.1 = (bf16[128,512]{1,0:T(8,128)(2,1)S(1)}, bf16[128,512]{1,0:T(8,128)(2,1)}, u32[]{:S(2)}, u32[]{:S(2)}) collective-permute-start(bf16[128,512]{1,0:T(8,128)(2,1)S(1)} %dynamic-slice_bitcast_fusion), channel_id=1, source_target_pairs={{0,16},{16,0},{32,48},{48,32},{64,80},{80,64},{96,112},{112,96},{1... | collective-permute-start | bytes 393224 | tf_op jit(solution)/shard_map/ppermute | solution.py:25
  88.2 1.0 collective-permute-done.1
  90.3 0.3 fusion
  90.6 1.3 broadcast_in_dim.114
  92.0 11.7 %all-to-all-start.2 = ((bf16[16,96,512]{2,1,0:T(8,128)(2,1)}), bf16[16,96,512]{2,1,0:T(8,128)(2,1)S(1)}, u32[]{:S(2)}, u32[]{:S(2)}) async-start(bf16[16,96,512]{2,1,0:T(8,128)(2,1)} %broadcast_in_dim.114), calls=%async_computation.2 | async-start | bytes 3145728 | tf_op jit(solution)/shard_map/all_to_all | solution.py:37
  103.7 23.6 %all-to-all-done.2 = bf16[16,96,512]{2,1,0:T(8,128)(2,1)S(1)} async-done(((bf16[16,96,512]{2,1,0:T(8,128)(2,1)}), bf16[16,96,512]{2,1,0:T(8,128)(2,1)S(1)}, u32[]{:S(2)}, u32[]{:S(2)}) %all-to-all-start.2) | async-done | bytes 1572896 | tf_op jit(solution)/shard_map/all_to_all | solution.py:37
  127.5 0.4 convert_element_type.86
  128.0 1.0 select_reduce_fusion
  129.1 1.9 %collective-permute-start.3 = (bf16[144,512]{1,0:T(8,128)(2,1)S(1)}, bf16[144,512]{1,0:T(8,128)(2,1)S(1)}, u32[]{:S(2)}, u32[]{:S(2)}) collective-permute-start(bf16[144,512]{1,0:T(8,128)(2,1)S(1)} %maximum_select_fusion.2), channel_id=1, source_target_pairs={{0,16},{16,0},{32,48},{48,32},{64,80},{80,64},{96,112},{112,96},{1... | collective-permute-start | bytes 442376 | tf_op jit(solution)/shard_map/ppermute | solution.py:25
  131.0 1.3 collective-permute-done.3
  132.4 0.8 fusion.10
  133.2 0.6 fusion.37
  (48 shorter events, 2.4 us)
Async XLA Ops:
  0.6 12.9 %copy-start.5 = (s32[16]{0:T(128)S(1)}, s32[16]{0:T(128)}, u32[]{:S(2)}) copy-start(s32[16]{0:T(128)} %param.9) | copy-start | bytes 196
  2.6 12.5 %copy-start = (bf16[1,1,512,512]{3,2,1,0:T(8,128)(2,1)S(1)}, bf16[1,1,512,512]{3,2,1,0:T(8,128)(2,1)}, u32[]{:S(2)}) copy-start(bf16[1,1,512,512]{3,2,1,0:T(8,128)(2,1)} %param.8) | copy-start | bytes 1572868
  4.7 10.3 %collective-permute-start = (bf16[512,512]{1,0:T(8,128)(2,1)S(1)}, bf16[512,512]{1,0:T(8,128)(2,1)S(1)}, u32[]{:S(2)}, u32[]{:S(2)}) collective-permute-start(bf16[512,512]{1,0:T(8,128)(2,1)S(1)} %maximum_select_fusion.1), channel_id=1, source_target_pairs={{0,16},{16,0},{32,48},{48,32},{64,80},{80,64},{96,112},{112,96},{1... | collective-permute-start | bytes 1572872 | tf_op jit(solution)/shard_map/ppermute | solution.py:25
  17.7 39.5 %all-to-all-start = ((bf16[16,128,512]{2,1,0:T(8,128)(2,1)}), bf16[16,128,512]{2,1,0:T(8,128)(2,1)S(1)}, u32[]{:S(2)}, u32[]{:S(2)}) async-start(bf16[16,128,512]{2,1,0:T(8,128)(2,1)} %maximum_select_fusion), calls=%async_computation | async-start | bytes 4194304 | tf_op jit(solution)/shard_map/all_to_all | solution.py:37
  83.8 5.5 %collective-permute-start.2 = (bf16[512,640]{1,0:T(8,128)(2,1)S(1)}, bf16[512,640]{1,0:T(8,128)(2,1)S(1)}, u32[]{:S(2)}, u32[]{:S(2)}) collective-permute-start(bf16[512,640]{1,0:T(8,128)(2,1)S(1)} %bitcast.83), channel_id=1, source_target_pairs={{0,16},{16,0},{32,48},{48,32},{64,80},{80,64},{96,112},{112,96},{1... | collective-permute-start | bytes 1966088 | tf_op jit(solution)/shard_map/ppermute | solution.py:25
  85.7 3.5 %collective-permute-start.1 = (bf16[128,512]{1,0:T(8,128)(2,1)S(1)}, bf16[128,512]{1,0:T(8,128)(2,1)}, u32[]{:S(2)}, u32[]{:S(2)}) collective-permute-start(bf16[128,512]{1,0:T(8,128)(2,1)S(1)} %dynamic-slice_bitcast_fusion), channel_id=1, source_target_pairs={{0,16},{16,0},{32,48},{48,32},{64,80},{80,64},{96,112},{112,96},{1... | collective-permute-start | bytes 393224 | tf_op jit(solution)/shard_map/ppermute | solution.py:25
  92.0 35.3 %all-to-all-start.2 = ((bf16[16,96,512]{2,1,0:T(8,128)(2,1)}), bf16[16,96,512]{2,1,0:T(8,128)(2,1)S(1)}, u32[]{:S(2)}, u32[]{:S(2)}) async-start(bf16[16,96,512]{2,1,0:T(8,128)(2,1)} %broadcast_in_dim.114), calls=%async_computation.2 | async-start | bytes 3145728 | tf_op jit(solution)/shard_map/all_to_all | solution.py:37
  128.0 4.4 %copy-start.1 = (f32[1,3,16,512]{3,2,1,0:T(8,128)S(1)}, f32[1,3,16,512]{3,2,1,0:T(8,128)}, u32[]{:S(2)}) copy-start(f32[1,3,16,512]{3,2,1,0:T(8,128)} %param.15) | copy-start | bytes 294916
  128.0 4.4 %copy-start.2 = (f32[1,3,16,512]{3,2,1,0:T(8,128)S(1)}, f32[1,3,16,512]{3,2,1,0:T(8,128)}, u32[]{:S(2)}) copy-start(f32[1,3,16,512]{3,2,1,0:T(8,128)} %param.14) | copy-start | bytes 294916
  128.0 4.4 %copy-start.3 = (f32[1,3,16,512]{3,2,1,0:T(8,128)S(1)}, f32[1,3,16,512]{3,2,1,0:T(8,128)}, u32[]{:S(2)}) copy-start(f32[1,3,16,512]{3,2,1,0:T(8,128)} %param.12) | copy-start | bytes 294916
  128.0 4.4 %copy-start.4 = (f32[1,3,16,512]{3,2,1,0:T(8,128)S(1)}, f32[1,3,16,512]{3,2,1,0:T(8,128)}, u32[]{:S(2)}) copy-start(f32[1,3,16,512]{3,2,1,0:T(8,128)} %param.13) | copy-start | bytes 294916
  129.1 3.3 %collective-permute-start.3 = (bf16[144,512]{1,0:T(8,128)(2,1)S(1)}, bf16[144,512]{1,0:T(8,128)(2,1)S(1)}, u32[]{:S(2)}, u32[]{:S(2)}) collective-permute-start(bf16[144,512]{1,0:T(8,128)(2,1)S(1)} %maximum_select_fusion.2), channel_id=1, source_target_pairs={{0,16},{16,0},{32,48},{48,32},{64,80},{80,64},{96,112},{112,96},{1... | collective-permute-start | bytes 442376 | tf_op jit(solution)/shard_map/ppermute | solution.py:25

commit v3 on v2

--- a/solution.py
+++ b/solution.py
@@ -1,6 +1,8 @@
 import jax
 import jax.numpy as jnp
 from jax import lax
+from jax.experimental import pallas as pl
+from jax.experimental.pallas import tpu as pltpu
 from jax.sharding import PartitionSpec as P
 
 beta_one = 0.9
@@ -25,16 +27,84 @@
     return lax.ppermute(value, "dp", [(i, i ^ 1) for i in range(lax.axis_size("dp"))])
 
 
-def exchange(pieces, both_dp):
+def place(chip, core, owner):
+    return (chip * 2 + core) * lax.axis_size("owner") + owner
+
+
+def exchange_dp(pieces):
+    chips = lax.axis_size("dp") // 2
+    groups = [[chip * 2 + core for chip in range(chips)] for core in range(2)]
+    return lax.all_to_all(pieces, "dp", 0, 0, axis_index_groups=groups)
+
+
+def exchange(pieces):
     chips = lax.axis_size("dp") // 2
     owners = lax.axis_size("owner")
-    place = lambda chip, core, owner: (chip * 2 + core) * owners + owner
     groups = [[place(chip, 0, owner) for chip in range(chips)] for owner in range(owners)]
-    if both_dp:
-        groups += [[place(chip, 1, owner) for chip in range(chips)] for owner in range(owners)]
-    else:
-        groups += [[place(chip, 1, owner) for owner in range(owners)] for chip in range(chips)]
+    groups += [[place(chip, 1, owner) for owner in range(owners)] for chip in range(chips)]
     return lax.all_to_all(pieces, ("dp", "owner"), 0, 0, axis_index_groups=groups)
+
+
+def exchange_lines(pieces):
+    chips = lax.axis_size("dp") // 2
+    owners = lax.axis_size("owner")
+    groups = [
+        [place(2 * y + x, 0, owner) for y in range(chips // 2)]
+        for owner in range(owners)
+        for x in range(2)
+    ]
+    groups += [
+        [place(chip, 1, 2 * z + x) for z in range(owners // 2)]
+        for chip in range(chips)
+        for x in range(2)
+    ]
+    return lax.all_to_all(pieces, ("dp", "owner"), 0, 0, axis_index_groups=groups)
+
+
+def swap_x(value):
+    chips = lax.axis_size("dp") // 2
+    owners = lax.axis_size("owner")
+    pairs = []
+    for chip in range(chips):
+        for owner in range(owners):
+            pairs.append((place(chip, 0, owner), place(chip ^ 1, 0, owner)))
+            pairs.append((place(chip, 1, owner), place(chip, 1, owner ^ 1)))
+    return lax.ppermute(value, ("dp", "owner"), pairs)
+
+
+def first_payload_kernel(core, grads, left, right, moment, second, slots, payload):
+    for slot in range(left.shape[0]):
+        slots[slot, 0] = left[slot]
+        slots[slot, 1] = right[slot]
+        slots[slot, 2] = moment[slot].astype(half)
+        slots[slot, 3] = second[slot].astype(half)
+
+    @pl.when(core[0] == 0)
+    def _():
+        rows = left.shape[1]
+        for slot in range(left.shape[0]):
+            for kind in range(4):
+                payload[pl.ds((slot * 4 + kind) * rows, rows)] = slots[slot, kind]
+
+    @pl.when(core[0] != 0)
+    def _():
+        payload[...] = grads[...]
+
+
+def first_payload(core, grads, left, right, moment, second):
+    slot_cap, row_num, col_num = left.shape
+    vmem = pl.BlockSpec(memory_space=pltpu.VMEM)
+    return pl.pallas_call(
+        first_payload_kernel,
+        out_shape=(
+            jax.ShapeDtypeStruct((slot_cap, 4, row_num, col_num), half),
+            jax.ShapeDtypeStruct(grads.shape, half),
+        ),
+        in_specs=[pl.BlockSpec(memory_space=pltpu.SMEM)] + [vmem] * 5,
+        out_specs=(vmem, vmem),
+        compiler_params=pltpu.CompilerParams(vmem_limit_bytes=16 * 1024 * 1024),
+        name="first_payload",
+    )(core, grads, left, right, moment, second)
 
 
 def copies(value, count):
@@ -63,31 +133,50 @@
     kinds = 4
 
     grads = grad_parts[0, 0]
-    slots = jnp.stack(
-        [left_basis[0], right_basis[0], moment[0].astype(half), second[0].astype(half)], 1
-    )
-    slot_rows = slots.reshape(-1, col_num)
-    came = swap_cores(
-        jnp.where(first, jnp.concatenate([slot_rows, grads[slot_rows.shape[0] :]], 0), grads)
-    )
+    slots, payload = first_payload(
+        (row_index % 2).reshape(1), grads, left_basis[0], right_basis[0], moment[0], second[0]
+    )
+    came = swap_cores(payload)
     numbers = slot_numbers(assign)
-    chip_grads = jnp.stack(
-        [grads.reshape(chips, chip_rows, col_num), came.reshape(chips, chip_rows, col_num)], 1
-    ).reshape(chips, 2 * chip_rows, col_num)
-    chip_grads = jnp.concatenate([chip_grads, chip_grads], 1)
-    chip_slots = jnp.stack([came[: slot_rows.shape[0]].reshape(slots.shape), slots], 2)
+
+    y_num = chips // 2
+    z_num = owner_num // 2
+    pair = (grads.astype(jnp.float32) + came.astype(jnp.float32)).astype(half)
+    pair = pair.reshape(y_num, 2, chip_rows, col_num)
+    even = chip % 2 == 0
+    kept = jnp.where(even, pair[:, 0], pair[:, 1])
+    sent = jnp.where(even, pair[:, 1], pair[:, 0]).reshape(-1, col_num)
+    slot_rows = slot_cap * kinds * row_num
+    chip_slots = jnp.stack([came[:slot_rows].reshape(slots.shape), slots], 2)
+    chip_slots = chip_slots.reshape(slot_cap * kinds * chip_rows, col_num)
+    sent_num = sent.shape[0]
+    beside = swap_x(
+        jnp.concatenate(
+            [jnp.where(first, sent, chip_slots[:sent_num]), chip_slots[sent_num:]], 0
+        )
+    )
+    sums = kept.astype(jnp.float32) + beside[:sent_num].reshape(kept.shape).astype(jnp.float32)
+    sums = sums.astype(half)
+
+    owner_x = owner % 2
+    from_owner = lax.dynamic_index_in_dim(assign.reshape(z_num, 2), owner_x, 1, keepdims=False)
+    number = lax.dynamic_index_in_dim(numbers.reshape(z_num, 2), owner_x, 1, keepdims=False)
+    code = (number + slot_cap * (from_owner % 2 != owner_x))[:, None, None]
     chip_slots = chip_slots.reshape(slot_cap, kinds * chip_rows, col_num)
-    number = numbers[:, None, None]
+    beside = beside.reshape(chip_slots.shape)
     picked = chip_slots[0][None]
     for slot in range(1, slot_cap):
-        picked = jnp.where(number == slot, chip_slots[slot][None], picked)
-
-    parts = exchange(jnp.where(first, chip_grads, picked), False)
-    grad_rows = jnp.sum(
-        parts[:, : 2 * chip_rows].reshape(2 * chips, chip_rows, col_num).astype(jnp.float32), axis=0
-    ).astype(half)
-    home = lax.dynamic_index_in_dim(parts, assign[owner], 0, keepdims=False)
-    home_came = swap_cores(home)
+        picked = jnp.where(code == slot, chip_slots[slot][None], picked)
+    for slot in range(slot_cap):
+        picked = jnp.where(code == slot_cap + slot, beside[slot][None], picked)
+
+    parts = exchange_lines(
+        jnp.concatenate(
+            [jnp.where(first, sums, picked[:, :chip_rows]), picked[:, chip_rows:]], 1
+        )
+    )
+    grad_rows = jnp.sum(parts[:, :chip_rows].astype(jnp.float32), axis=0).astype(half)
+    home = lax.dynamic_index_in_dim(parts, assign[owner] // 2, 0, keepdims=False)
 
     left_rows, right_rows = home.reshape(kinds, chip_rows, col_num)[:2]
     left_chunks = left_rows.reshape(chip_rows, chunk_num, LANES).transpose(1, 0, 2)
@@ -95,13 +184,15 @@
         left_chunks[:, None], (chunk_num, chips // chunk_num, chip_rows, LANES)
     ).reshape(chips, chip_rows, LANES)
     rows = copies(jnp.where(first, grad_rows, right_rows), chips)
-    mine = exchange(jnp.concatenate([rows, left_chunks], 2), True)
+    mine = exchange_dp(jnp.concatenate([rows, left_chunks], 2))
     mine = mine.reshape(col_num, col_num + LANES)
-    other = swap_cores(mine)
+    wide_home = jnp.concatenate([home, home[:, :LANES]], 1)
+    other = swap_cores(jnp.concatenate([mine, wide_home], 0))
+    home = jnp.where(first, other[col_num:, :col_num], home).reshape(kinds, chip_rows, col_num)
+    other = other[:col_num]
     grad_full = jnp.where(first, mine[:, :col_num], other[:, :col_num])
     right_full = jnp.where(first, other[:, :col_num], mine[:, :col_num])
     left_cols = jnp.where(first, other[:, col_num:], mine[:, col_num:])
-    home = jnp.where(first, home_came, home).reshape(kinds, chip_rows, col_num)
 
     chunk = chip // (chips // chunk_num)
     in_chunk = (chip % (chips // chunk_num)) * chip_rows
@@ -120,7 +211,7 @@
     results = jnp.concatenate(
         [jnp.where(first, back_rows, left_term), right_term, rotated.astype(half)], 0
     )
-    gathered = exchange(copies(results, chips), False)
+    gathered = exchange(copies(results, chips))
     back_full = gathered[:, :chip_rows].reshape(col_num, col_num)
     chip_update = dot(home[0], back_full, (1, 0)).astype(half)
     held = (assign == owner)[None, :] & (

time: 134 us -> 126 us (0.940)
  blocking collectives: 26.1 us -> 0 us
  waiting for transfers between devices: 57 us -> 64.4 us
  starting transfers between devices: 34 us -> 40.8 us
  local copies, waits for them, and re-layouts: 3.35 us -> 7.74 us
  other arithmetic: 8.88 us -> 6.92 us
    all_to_all x2 -> x1, waiting for transfers between devices: 53.3 us -> 24.1 us  [exchange(): lax.all_to_all(pieces, ('dp', 'owner'), 0, 0, axis_index_groups=groups)]
    all_to_all x0 -> x2, waiting for transfers between devices: none -> 28.1 us  [the longest x1 14.6 us: exchange_lines(): lax.all_to_all(pieces, ('dp', 'owner'), 0, 0, axis_index_groups=groups)]
    all_to_all x1 -> x0, blocking collectives: 26.1 us -> none  [exchange(): lax.all_to_all(pieces, ('dp', 'owner'), 0, 0, axis_index_groups=groups)]
    all_to_all x0 -> x2, starting transfers between devices: none -> 16 us  [the longest x1 8.94 us: exchange_dp(): return lax.all_to_all(pieces, 'dp', 0, 0, axis_index_groups=groups)]
    all_to_all x2 -> x1, starting transfers between devices: 18.9 us -> 10 us  [exchange(): lax.all_to_all(pieces, ('dp', 'owner'), 0, 0, axis_index_groups=groups)]
    ppermute x0 -> x1, waiting for transfers between devices: none -> 8.64 us  [swap_x(): return lax.ppermute(value, ('dp', 'owner'), pairs)]
    unnamed x12 -> x22, local copies, waits for them, and re-layouts: 0.04 us -> 4.45 us
    select_n x3 -> x5, other arithmetic: 3.48 us -> 0.7 us  [the longest x1 0.44 us: on_device(): picked = jnp.where(code == slot_cap + slot, beside[slot][None], picked)]
  transfers between devices with their start and end apart: 6 -> 7, of which waited for: 5 -> 6; matrix products, arithmetic and copies ran while one was open for 1% -> 2% of each run, Pallas kernels for 0% -> 0%
where the time goes in v3:
time: 126 us; the launch traced here: 125 us
  waiting for transfers between devices  64.4 us (51%)
  starting transfers between devices  40.8 us (32%)
  local copies, waits for them, and re-layouts  7.74 us (6%)
  other arithmetic  6.92 us (5%)
  between operations  3.81 us (3%)
  matrix products  1.44 us (1%)
    all_to_all x1, waiting for transfers between devices, exchange(): lax.all_to_all(pieces, ('dp', 'owner'), 0, 0, axis_index_groups=groups)  24.1 us
    all_to_all x1, waiting for transfers between devices, exchange_lines(): lax.all_to_all(pieces, ('dp', 'owner'), 0, 0, axis_index_groups=groups)  14.6 us
    all_to_all x1, waiting for transfers between devices, exchange_dp(): return lax.all_to_all(pieces, 'dp', 0, 0, axis_index_groups=groups)  13.5 us
    ppermute x3, starting transfers between devices, swap_cores(): lax.ppermute(value, 'dp', [(i, i ^ 1) for i in range(lax.axis_size('dp'))])  12.9 us
    all_to_all x1, starting transfers between devices, exchange(): lax.all_to_all(pieces, ('dp', 'owner'), 0, 0, axis_index_groups=groups)  10 us
    all_to_all x1, starting transfers between devices, exchange_dp(): return lax.all_to_all(pieces, 'dp', 0, 0, axis_index_groups=groups)  8.94 us
    ppermute x1, waiting for transfers between devices, swap_x(): return lax.ppermute(value, ('dp', 'owner'), pairs)  8.64 us
    all_to_all x1, starting transfers between devices, exchange_lines(): lax.all_to_all(pieces, ('dp', 'owner'), 0, 0, axis_index_groups=groups)  7.07 us
  transfers between devices with their start and end apart: 7, of which 6 were waited for; matrix products, arithmetic and copies ran while one was open for 2% of the time, Pallas kernels for 0%

profile of v3, /device:TPU:1, one launch (start us, length us, event | category | flops | bytes accessed | tf_op | source)
XLA Modules:
  0.0 125.2 jit_solution(724510820556523762)
XLA Ops:
  0.7 1.0 copy-done
  1.7 0.9 copy-done.2
  2.6 0.9 copy-done.4
  3.5 0.8 copy-done.6
  4.3 0.8 copy-done.7
  5.1 8.9 %collective-permute-start = (bf16[512,512]{1,0:T(8,128)(2,1)S(1)}, bf16[512,512]{1,0:T(8,128)(2,1)S(1)}, u32[]{:S(2)}, u32[]{:S(2)}) collective-permute-start(bf16[512,512]{1,0:T(8,128)(2,1)S(1)} %get-tuple-element.7), channel_id=1, source_target_pairs={{0,16},{16,0},{32,48},{48,32},{64,80},{80,64},{96,112},{112,96},{1... | collective-permute-start | bytes 1572872 | tf_op jit(solution)/shard_map/ppermute | solution.py:27
  14.8 0.9 convert_reduce_fusion
  16.5 1.9 %collective-permute-start.1 = (bf16[384,512]{1,0:T(8,128)(2,1)S(1)}, bf16[384,512]{1,0:T(8,128)(2,1)S(1)}, u32[]{:S(2)}, u32[]{:S(2)}) collective-permute-start(bf16[384,512]{1,0:T(8,128)(2,1)S(1)} %pad_maximum_fusion.2), channel_id=1, source_target_pairs={{0,32},{16,17},{1,33},{17,16},{2,34},{18,19},{3,35},{19,18},{4,36}... | collective-permute-start | bytes 1179656 | tf_op jit(solution)/shard_map/ppermute | solution.py:72
  18.5 8.6 %collective-permute-done.1 = bf16[384,512]{1,0:T(8,128)(2,1)S(1)} collective-permute-done((bf16[384,512]{1,0:T(8,128)(2,1)S(1)}, bf16[384,512]{1,0:T(8,128)(2,1)S(1)}, u32[]{:S(2)}, u32[]{:S(2)}) %collective-permute-start.1) | collective-permute-done | bytes 393248 | tf_op jit(solution)/shard_map/ppermute | solution.py:72
  27.9 1.0 pad_maximum_fusion
  28.9 7.1 %all-to-all-start = ((bf16[8,128,512]{2,1,0:T(8,128)(2,1)}), bf16[8,128,512]{2,1,0:T(8,128)(2,1)S(1)}, u32[]{:S(2)}, u32[]{:S(2)}) async-start(bf16[8,128,512]{2,1,0:T(8,128)(2,1)} %pad_maximum_fusion), calls=%async_computation | async-start | bytes 2097152 | tf_op jit(solution)/shard_map/all_to_all | solution.py:61
  39.2 14.6 %all-to-all-done = bf16[8,128,512]{2,1,0:T(8,128)(2,1)S(1)} async-done(((bf16[8,128,512]{2,1,0:T(8,128)(2,1)}), bf16[8,128,512]{2,1,0:T(8,128)(2,1)S(1)}, u32[]{:S(2)}, u32[]{:S(2)}) %all-to-all-start) | async-done | bytes 1048608 | tf_op jit(solution)/shard_map/all_to_all | solution.py:61
  54.0 0.9 pad_maximum_fusion.1
  54.9 8.9 %all-to-all-start.1 = ((bf16[16,32,640]{2,1,0:T(8,128)(2,1)}), bf16[16,32,640]{2,1,0:T(8,128)(2,1)S(1)}, u32[]{:S(2)}, u32[]{:S(2)}) async-start(bf16[16,32,640]{2,1,0:T(8,128)(2,1)} %pad_maximum_fusion.1), calls=%async_computation.1 | async-start | bytes 1310720 | tf_op jit(solution)/shard_map/all_to_all | solution.py:37
  63.9 13.5 %all-to-all-done.1 = bf16[16,32,640]{2,1,0:T(8,128)(2,1)S(1)} async-done(((bf16[16,32,640]{2,1,0:T(8,128)(2,1)}), bf16[16,32,640]{2,1,0:T(8,128)(2,1)S(1)}, u32[]{:S(2)}, u32[]{:S(2)}) %all-to-all-start.1) | async-done | bytes 655392 | tf_op jit(solution)/shard_map/all_to_all | solution.py:37
  77.5 1.9 %collective-permute-start.2 = (bf16[640,640]{1,0:T(8,128)(2,1)S(1)}, bf16[640,640]{1,0:T(8,128)(2,1)S(1)}, u32[]{:S(2)}, u32[]{:S(2)}) collective-permute-start(bf16[640,640]{1,0:T(8,128)(2,1)S(1)} %maximum_maximum_fusion), channel_id=1, source_target_pairs={{0,16},{16,0},{32,48},{48,32},{64,80},{80,64},{96,112},{112,96},{1... | collective-permute-start | bytes 2457608 | tf_op jit(solution)/shard_map/ppermute | solution.py:27
  79.5 2.3 %collective-permute-done.2 = bf16[640,640]{1,0:T(8,128)(2,1)S(1)} collective-permute-done((bf16[640,640]{1,0:T(8,128)(2,1)S(1)}, bf16[640,640]{1,0:T(8,128)(2,1)S(1)}, u32[]{:S(2)}, u32[]{:S(2)}) %collective-permute-start.2) | collective-permute-done | bytes 819232 | tf_op jit(solution)/shard_map/ppermute | solution.py:27
  83.1 1.3 %broadcast_in_dim.147 = bf16[16,96,512]{2,1,0:T(8,128)(2,1)} broadcast(bf16[96,512]{1,0:T(8,128)(2,1)S(1)} %pad_maximum_fusion.4), dimensions={1,2} | broadcast | bytes 1671168 | tf_op jit(solution)/shard_map/broadcast_in_dim | solution.py:111
  84.5 10.0 %all-to-all-start.2 = ((bf16[16,96,512]{2,1,0:T(8,128)(2,1)}), bf16[16,96,512]{2,1,0:T(8,128)(2,1)S(1)}, u32[]{:S(2)}, u32[]{:S(2)}) async-start(bf16[16,96,512]{2,1,0:T(8,128)(2,1)} %broadcast_in_dim.147), calls=%async_computation.2 | async-start | bytes 3145728 | tf_op jit(solution)/shard_map/all_to_all | solution.py:45
  94.5 24.1 %all-to-all-done.2 = bf16[16,96,512]{2,1,0:T(8,128)(2,1)S(1)} async-done(((bf16[16,96,512]{2,1,0:T(8,128)(2,1)}), bf16[16,96,512]{2,1,0:T(8,128)(2,1)S(1)}, u32[]{:S(2)}, u32[]{:S(2)}) %all-to-all-start.2) | async-done | bytes 1572896 | tf_op jit(solution)/shard_map/all_to_all | solution.py:45
  119.3 1.0 select_reduce_fusion
  120.4 2.1 %collective-permute-start.3 = (bf16[144,512]{1,0:T(8,128)(2,1)S(1)}, bf16[144,512]{1,0:T(8,128)(2,1)S(1)}, u32[]{:S(2)}, u32[]{:S(2)}) collective-permute-start(bf16[144,512]{1,0:T(8,128)(2,1)S(1)} %maximum_select_fusion), channel_id=1, source_target_pairs={{0,16},{16,0},{32,48},{48,32},{64,80},{80,64},{96,112},{112,96},{1... | collective-permute-start | bytes 442376 | tf_op jit(solution)/shard_map/ppermute | solution.py:27
  122.4 1.3 %collective-permute-done.3 = bf16[144,512]{1,0:T(8,128)(2,1)S(1)} collective-permute-done((bf16[144,512]{1,0:T(8,128)(2,1)S(1)}, bf16[144,512]{1,0:T(8,128)(2,1)S(1)}, u32[]{:S(2)}, u32[]{:S(2)}) %collective-permute-start.3) | collective-permute-done | bytes 147488 | tf_op jit(solution)/shard_map/ppermute | solution.py:27
  123.8 0.8 fusion.13
  (70 shorter events, 5.8 us)
Async XLA Ops:
  0.6 1.0 copy-start
  1.7 0.9 copy-start.2
  2.6 0.9 copy-start.4
  3.5 0.8 copy-start.6
  4.3 0.8 copy-start.7
  5.1 11.1 %copy-start.1 = (bf16[1,1,512,512]{3,2,1,0:T(8,128)(2,1)S(1)}, bf16[1,1,512,512]{3,2,1,0:T(8,128)(2,1)}, u32[]{:S(2)}) copy-start(bf16[1,1,512,512]{3,2,1,0:T(8,128)(2,1)} %param.8) | copy-start | bytes 1572868
  5.1 10.9 %collective-permute-start = (bf16[512,512]{1,0:T(8,128)(2,1)S(1)}, bf16[512,512]{1,0:T(8,128)(2,1)S(1)}, u32[]{:S(2)}, u32[]{:S(2)}) collective-permute-start(bf16[512,512]{1,0:T(8,128)(2,1)S(1)} %get-tuple-element.7), channel_id=1, source_target_pairs={{0,16},{16,0},{32,48},{48,32},{64,80},{80,64},{96,112},{112,96},{1... | collective-permute-start | bytes 1572872 | tf_op jit(solution)/shard_map/ppermute | solution.py:27
  16.5 10.6 %collective-permute-start.1 = (bf16[384,512]{1,0:T(8,128)(2,1)S(1)}, bf16[384,512]{1,0:T(8,128)(2,1)S(1)}, u32[]{:S(2)}, u32[]{:S(2)}) collective-permute-start(bf16[384,512]{1,0:T(8,128)(2,1)S(1)} %pad_maximum_fusion.2), channel_id=1, source_target_pairs={{0,32},{16,17},{1,33},{17,16},{2,34},{18,19},{3,35},{19,18},{4,36}... | collective-permute-start | bytes 1179656 | tf_op jit(solution)/shard_map/ppermute | solution.py:72
  27.9 8.1 %copy-start.10 = (s32[16]{0:T(128)S(1)}, s32[16]{0:T(128)}, u32[]{:S(2)}) copy-start(s32[16]{0:T(128)} %param.9) | copy-start | bytes 196
  28.9 24.9 %all-to-all-start = ((bf16[8,128,512]{2,1,0:T(8,128)(2,1)}), bf16[8,128,512]{2,1,0:T(8,128)(2,1)S(1)}, u32[]{:S(2)}, u32[]{:S(2)}) async-start(bf16[8,128,512]{2,1,0:T(8,128)(2,1)} %pad_maximum_fusion), calls=%async_computation | async-start | bytes 2097152 | tf_op jit(solution)/shard_map/all_to_all | solution.py:61
  54.9 22.5 %all-to-all-start.1 = ((bf16[16,32,640]{2,1,0:T(8,128)(2,1)}), bf16[16,32,640]{2,1,0:T(8,128)(2,1)S(1)}, u32[]{:S(2)}, u32[]{:S(2)}) async-start(bf16[16,32,640]{2,1,0:T(8,128)(2,1)} %pad_maximum_fusion.1), calls=%async_computation.1 | async-start | bytes 1310720 | tf_op jit(solution)/shard_map/all_to_all | solution.py:37
  77.5 4.2 %collective-permute-start.2 = (bf16[640,640]{1,0:T(8,128)(2,1)S(1)}, bf16[640,640]{1,0:T(8,128)(2,1)S(1)}, u32[]{:S(2)}, u32[]{:S(2)}) collective-permute-start(bf16[640,640]{1,0:T(8,128)(2,1)S(1)} %maximum_maximum_fusion), channel_id=1, source_target_pairs={{0,16},{16,0},{32,48},{48,32},{64,80},{80,64},{96,112},{112,96},{1... | collective-permute-start | bytes 2457608 | tf_op jit(solution)/shard_map/ppermute | solution.py:27
  84.5 34.1 %all-to-all-start.2 = ((bf16[16,96,512]{2,1,0:T(8,128)(2,1)}), bf16[16,96,512]{2,1,0:T(8,128)(2,1)S(1)}, u32[]{:S(2)}, u32[]{:S(2)}) async-start(bf16[16,96,512]{2,1,0:T(8,128)(2,1)} %broadcast_in_dim.147), calls=%async_computation.2 | async-start | bytes 3145728 | tf_op jit(solution)/shard_map/all_to_all | solution.py:45
  120.2 3.6 %copy-start.3 = (f32[1,3,16,512]{3,2,1,0:T(8,128)S(1)}, f32[1,3,16,512]{3,2,1,0:T(8,128)}, u32[]{:S(2)}) copy-start(f32[1,3,16,512]{3,2,1,0:T(8,128)} %param.14) | copy-start | bytes 294916
  120.2 3.6 %copy-start.5 = (f32[1,3,16,512]{3,2,1,0:T(8,128)S(1)}, f32[1,3,16,512]{3,2,1,0:T(8,128)}, u32[]{:S(2)}) copy-start(f32[1,3,16,512]{3,2,1,0:T(8,128)} %param.15) | copy-start | bytes 294916
  120.3 3.6 %copy-start.8 = (f32[1,3,16,512]{3,2,1,0:T(8,128)S(1)}, f32[1,3,16,512]{3,2,1,0:T(8,128)}, u32[]{:S(2)}) copy-start(f32[1,3,16,512]{3,2,1,0:T(8,128)} %param.12) | copy-start | bytes 294916
  120.3 3.6 %copy-start.9 = (f32[1,3,16,512]{3,2,1,0:T(8,128)S(1)}, f32[1,3,16,512]{3,2,1,0:T(8,128)}, u32[]{:S(2)}) copy-start(f32[1,3,16,512]{3,2,1,0:T(8,128)} %param.13) | copy-start | bytes 294916
  120.4 3.4 %collective-permute-start.3 = (bf16[144,512]{1,0:T(8,128)(2,1)S(1)}, bf16[144,512]{1,0:T(8,128)(2,1)S(1)}, u32[]{:S(2)}, u32[]{:S(2)}) collective-permute-start(bf16[144,512]{1,0:T(8,128)(2,1)S(1)} %maximum_select_fusion), channel_id=1, source_target_pairs={{0,16},{16,0},{32,48},{48,32},{64,80},{80,64},{96,112},{112,96},{1... | collective-permute-start | bytes 442376 | tf_op jit(solution)/shard_map/ppermute | solution.py:27

commit v4 on v3

v4 whole, which is shorter than its diff:
```python
import jax
import jax.numpy as jnp
from jax import lax
from jax.experimental import pallas as pl
from jax.experimental.pallas import tpu as pltpu
from jax.sharding import PartitionSpec as P

beta_one = 0.9
beta_two = 0.95
step_count = 10.0
adam_eps = 1e-08
bias_one = 1.0 - beta_one**step_count
bias_two = 1.0 - beta_two**step_count

LANES = 128
half = jnp.bfloat16


def slot_numbers(assign):
    positions = jnp.arange(assign.shape[0], dtype=jnp.int32)
    matching = assign[:, None] == assign[None, :]
    earlier = positions[None, :] < positions[:, None]
    return jnp.sum((matching & earlier).astype(jnp.int32), axis=1)


def swap_cores(value):
    return lax.ppermute(value, "dp", [(i, i ^ 1) for i in range(lax.axis_size("dp"))])


def place(chip, core, owner):
    return (chip * 2 + core) * lax.axis_size("owner") + owner


def exchange_dp(pieces):
    chips = lax.axis_size("dp") // 2
    groups = [[chip * 2 + core for chip in range(chips)] for core in range(2)]
    return lax.all_to_all(pieces, "dp", 0, 0, axis_index_groups=groups)


def exchange(pieces):
    chips = lax.axis_size("dp") // 2
    owners = lax.axis_size("owner")
    groups = [[place(chip, 0, owner) for chip in range(chips)] for owner in range(owners)]
    groups += [[place(chip, 1, owner) for owner in range(owners)] for chip in range(chips)]
    return lax.all_to_all(pieces, ("dp", "owner"), 0, 0, axis_index_groups=groups)


def exchange_lines(pieces, y_core):
    chips = lax.axis_size("dp") // 2
    owners = lax.axis_size("owner")
    groups = [
        [place(2 * y + x, y_core, owner) for y in range(chips // 2)]
        for owner in range(owners)
        for x in range(2)
    ]
    groups += [
        [place(chip, 1 - y_core, 2 * z + x) for z in range(owners // 2)]
        for chip in range(chips)
        for x in range(2)
    ]
    return lax.all_to_all(pieces, ("dp", "owner"), 0, 0, axis_index_groups=groups)


def swap_x(value):
    chips = lax.axis_size("dp") // 2
    owners = lax.axis_size("owner")
    pairs = []
    for chip in range(chips):
        for owner in range(owners):
            pairs.append((place(chip, 0, owner), place(chip ^ 1, 0, owner)))
            pairs.append((place(chip, 1, owner), place(chip, 1, owner ^ 1)))
    return lax.ppermute(value, ("dp", "owner"), pairs)


def first_payload_kernel(core, grads, left, right, payload, sems):
    slot_cap, row_num = left.shape[1:3]

    @pl.when(core[0] == 0)
    def _():
        moves = []
        for slot in range(slot_cap):
            for kind, basis in enumerate((left, right)):
                place_of = slot * 2 + kind
                moves.append(
                    pltpu.make_async_copy(
                        basis.at[0, slot],
                        payload.at[pl.ds(place_of * row_num, row_num)],
                        sems.at[place_of],
                    )
                )
        for move in moves:
            move.start()
        for move in moves:
            move.wait()

    @pl.when(core[0] != 0)
    def _():
        move = pltpu.make_async_copy(grads.at[0, 0], payload, sems.at[0])
        move.start()
        move.wait()


def first_payload(core, grads, left, right):
    anywhere = pl.BlockSpec(memory_space=pl.ANY)
    return pl.pallas_call(
        first_payload_kernel,
        out_shape=jax.ShapeDtypeStruct(grads.shape[2:], half),
        in_specs=[pl.BlockSpec(memory_space=pltpu.SMEM)] + [anywhere] * 3,
        out_specs=anywhere,
        scratch_shapes=[pltpu.SemaphoreType.DMA((2 * left.shape[1],))],
        compiler_params=pltpu.CompilerParams(vmem_limit_bytes=60 * 1024 * 1024),
        name="first_payload",
    )(core, grads, left, right)


def state_pieces_kernel(assign, moment, second, pieces, wide, narrow, sems):
    moves = [
        pltpu.make_async_copy(source.at[0], wide.at[kind], sems.at[kind])
        for kind, source in enumerate((moment, second))
    ]
    for move in moves:
        move.start()
    for move in moves:
        move.wait()
    slot_cap = moment.shape[1]
    for slot in range(slot_cap):
        for kind in range(2):
            narrow[slot, kind] = wide[kind, slot].astype(half)
    for block in range(assign.shape[0]):
        number = jnp.int32(0)
        for earlier in range(block):
            number += (assign[earlier] == assign[block]).astype(jnp.int32)
        pieces[block] = narrow[jnp.minimum(number, slot_cap - 1)]


def state_pieces(assign, moment, second):
    slot_cap, row_num, col_num = moment.shape[1:]
    anywhere = pl.BlockSpec(memory_space=pl.ANY)
    return pl.pallas_call(
        state_pieces_kernel,
        out_shape=jax.ShapeDtypeStruct((assign.shape[0], 2, row_num, col_num), half),
        in_specs=[pl.BlockSpec(memory_space=pltpu.SMEM), anywhere, anywhere],
        out_specs=pl.BlockSpec(memory_space=pltpu.VMEM),
        scratch_shapes=[
            pltpu.VMEM((2, slot_cap, row_num, col_num), jnp.float32),
            pltpu.VMEM((slot_cap, 2, row_num, col_num), half),
            pltpu.SemaphoreType.DMA((2,)),
        ],
        name="state_pieces",
    )(assign, moment, second)


def copies(value, count):
    return jnp.broadcast_to(value[None], (count,) + value.shape)


def dot(left, right, contract):
    return lax.dot_general(
        left, right, ((contract[:1], contract[1:]), ((), ())), preferred_element_type=jnp.float32
    )


def on_device(grad_parts, assign, left_basis, right_basis, left_stat, right_stat, moment, second):
    row_index = lax.axis_index("dp")
    owner = lax.axis_index("owner")
    dp_num = lax.axis_size("dp")
    owner_num = lax.axis_size("owner")
    col_num = grad_parts.shape[3]
    row_num = col_num // dp_num
    slot_cap = left_basis.shape[1]
    chunk_num = col_num // LANES
    chips = dp_num // 2
    chip = row_index // 2
    first = row_index % 2 == 0
    chip_rows = 2 * row_num
    y_num = chips // 2
    z_num = owner_num // 2
    kinds = 2

    came = swap_cores(
        first_payload((row_index % 2).reshape(1), grad_parts, left_basis, right_basis)
    )

    numbers = slot_numbers(assign)
    states = lax.all_to_all(state_pieces(assign, moment, second), "owner", 0, 0)
    states = lax.dynamic_index_in_dim(states, assign[owner], 0, keepdims=False)

    pair = (grad_parts[0, 0].astype(jnp.float32) + came.astype(jnp.float32)).astype(half)
    pair = pair.reshape(y_num, 2, chip_rows, col_num)
    even = chip % 2 == 0
    kept = jnp.where(even, pair[:, 0], pair[:, 1])
    sent = jnp.where(even, pair[:, 1], pair[:, 0]).reshape(-1, col_num)
    slots = jnp.stack([left_basis[0], right_basis[0]], 1)
    slot_rows = slot_cap * kinds * row_num
    chip_slots = jnp.stack([came[:slot_rows].reshape(slots.shape), slots], 2)
    chip_slots = chip_slots.reshape(slot_cap * kinds * chip_rows, col_num)
    slot_rows = chip_slots.shape[0]
    beside = swap_x(
        jnp.concatenate([jnp.where(first, sent[:slot_rows], chip_slots), sent[slot_rows:]], 0)
    )
    sums = kept.astype(jnp.float32) + beside.reshape(kept.shape).astype(jnp.float32)
    sums = sums.astype(half)

    owner_x = owner % 2
    from_owner = lax.dynamic_index_in_dim(assign.reshape(z_num, 2), owner_x, 1, keepdims=False)
    number = lax.dynamic_index_in_dim(numbers.reshape(z_num, 2), owner_x, 1, keepdims=False)
    code = (number + slot_cap * (from_owner % 2 != owner_x))[:, None, None]
    chip_slots = chip_slots.reshape(slot_cap, kinds * chip_rows, col_num)
    beside = beside[:slot_rows].reshape(chip_slots.shape)
    picked = chip_slots[0][None]
    for slot in range(1, slot_cap):
        picked = jnp.where(code == slot, chip_slots[slot][None], picked)
    for slot in range(slot_cap):
        picked = jnp.where(code == slot_cap + slot, beside[slot][None], picked)

    parts = exchange_lines(
        jnp.concatenate(
            [jnp.where(first, sums, picked[:, :chip_rows]), picked[:, chip_rows:]], 1
        ),
        0,
    )
    grad_rows = jnp.sum(parts[:, :chip_rows].astype(jnp.float32), axis=0).astype(half)
    home = lax.dynamic_index_in_dim(parts, assign[owner] // 2, 0, keepdims=False)

    left_rows, right_rows = home.reshape(kinds, chip_rows, col_num)
    left_chunks = left_rows.reshape(chip_rows, chunk_num, LANES).transpose(1, 0, 2)
    left_chunks = jnp.broadcast_to(
        left_chunks[:, None], (chunk_num, chips // chunk_num, chip_rows, LANES)
    ).reshape(chips, chip_rows, LANES)
    rows = copies(jnp.where(first, grad_rows, right_rows), chips)
    mine = exchange_dp(jnp.concatenate([rows, left_chunks], 2))
    mine = mine.reshape(col_num, col_num + LANES)

    chunk = chip // (chips // chunk_num)
    in_chunk = (chip % (chips // chunk_num)) * chip_rows
    own_rows = lambda value: lax.dynamic_slice_in_dim(value, in_chunk, chip_rows, 0)
    core_full = mine[:, :col_num]
    grad_cols = lax.dynamic_slice_in_dim(core_full, chunk * LANES, LANES, 1)
    left_term = dot(grad_rows, core_full, (1, 1)).astype(half)
    right_term = own_rows(dot(grad_cols, core_full, (0, 0)).astype(half))
    grams = exchange_lines(copies(jnp.concatenate([left_term, right_term], 0), z_num), 1)

    extra = jnp.concatenate([left_rows, states.reshape(-1, col_num)], 0)
    extra = jnp.concatenate([extra, extra[:, :LANES]], 1)
    other = swap_cores(jnp.concatenate([mine, extra], 0))
    left_rows = other[col_num : col_num + chip_rows, :col_num]
    other_states = other[col_num + chip_rows :, :col_num].reshape(states.shape)
    states = jnp.concatenate([states, other_states], 1).astype(jnp.float32)
    other = other[:col_num]
    grad_full = jnp.where(first, core_full, other[:, :col_num])
    right_full = jnp.where(first, other[:, :col_num], core_full)
    left_cols = jnp.where(first, other[:, col_num:], mine[:, col_num:])

    turned = own_rows(dot(left_cols, grad_full, (0, 0)).astype(half))
    rotated = dot(turned, right_full, (1, 0))
    home_moment = beta_one * states[0] + (1.0 - beta_one) * rotated
    home_second = beta_two * states[1] + (1.0 - beta_two) * rotated * rotated
    direction = (home_moment / bias_one / (jnp.sqrt(home_second / bias_two) + adam_eps)).astype(half)
    back_rows = dot(direction, right_full, (1, 1)).astype(half)

    results = copies(jnp.where(first, back_rows, rotated.astype(half)), chips)
    results, grams = lax.optimization_barrier((results, grams))
    gathered = exchange(results)
    held = lambda blocks, counts, target: (blocks == target)[None, :] & (
        counts[None, :] == jnp.arange(slot_cap, dtype=jnp.int32)[:, None]
    )

    def taken(mask, values):
        values = jnp.where(mask[:, :, None, None], values[None].astype(jnp.float32), 0.0)
        return jnp.sum(values, axis=1).astype(half)

    own_grams = taken(held(from_owner, number, owner), grams)
    beside_grams = taken(held(from_owner, number, owner ^ 1), grams)
    owners_beside = [(i, i ^ 1) for i in range(owner_num)]
    own_grams = own_grams + lax.ppermute(beside_grams, "owner", owners_beside)
    own_grams = own_grams.reshape(slot_cap * 2, 2, row_num, col_num)

    back_full = gathered.reshape(col_num, col_num)
    chip_update = dot(left_rows, back_full, (1, 0)).astype(half)
    turns = taken(held(assign, numbers, owner), gathered).reshape(slot_cap, 2, row_num, col_num)
    for_second = jnp.concatenate(
        [chip_update[row_num:], own_grams[:, 1].reshape(-1, col_num)], 0
    )
    turn_rows = slot_cap * row_num
    for_first = jnp.where(first, for_second[:turn_rows], turns[:, 0].reshape(-1, col_num))
    came = swap_cores(jnp.concatenate([for_first, for_second[turn_rows:]], 0))
    update = jnp.where(first, chip_update[:row_num], came[:row_num])
    grams = jnp.where(first, own_grams[:, 0], came[row_num:].reshape(own_grams[:, 0].shape))
    grams = grams.reshape(slot_cap, 2, row_num, col_num).astype(jnp.float32)
    turns = jnp.where(first, came[:turn_rows].reshape(turns[:, 0].shape), turns[:, 1])
    turns = turns.astype(jnp.float32)

    new_left = beta_two * left_stat[0] + (1.0 - beta_two) * grams[:, 0]
    new_right = beta_two * right_stat[0] + (1.0 - beta_two) * grams[:, 1]
    new_moment = beta_one * moment[0] + (1.0 - beta_one) * turns
    new_second = beta_two * second[0] + (1.0 - beta_two) * turns * turns
    return (update[None], new_left[None], new_right[None], new_moment[None], new_second[None])


def solution(mesh):
    placed = (
        P("dp", "owner", None, None),
        P(),
        P("owner", None, "dp", None),
        P("owner", None, "dp", None),
        P("owner", None, "dp", None),
        P("owner", None, "dp", None),
        P("owner", None, "dp", None),
        P("owner", None, "dp", None),
    )
    return jax.shard_map(
        on_device,
        mesh=mesh,
        in_specs=placed,
        out_specs=(
            P("owner", "dp", None),
            P("owner", None, "dp", None),
            P("owner", None, "dp", None),
            P("owner", None, "dp", None),
            P("owner", None, "dp", None),
        ),
        check_vma=False,
    )
```

time: 126 us -> 155 us (1.23)
  Pallas kernels: 0.05 us -> 19.7 us
  starting transfers between devices: 40.8 us -> 56.8 us
  local copies, waits for them, and re-layouts: 7.74 us -> 3.1 us
  waiting for transfers between devices: 64.4 us -> 62.3 us
    all_to_all x1, waiting for transfers between devices: 24.1 us -> 0.01 us  [exchange(): lax.all_to_all(pieces, ('dp', 'owner'), 0, 0, axis_index_groups=groups)]
    pallas_call x1 -> x2, Pallas kernels: 0.05 us -> 19.7 us  [the longest x1 17.1 us: first_payload(): pl.pallas_call(first_payload_kernel, out_shape=jax.ShapeDtypeStruct(grads...]
    ppermute x0 -> x1, waiting for transfers between devices: none -> 9.18 us  [on_device(): own_grams = own_grams + lax.ppermute(beside_grams, 'owner', owners_beside)]
    all_to_all x0 -> x1, waiting for transfers between devices: none -> 9.08 us  [on_device(): states = lax.all_to_all(state_pieces(assign, moment, second), 'owner', 0, 0)]
    all_to_all x1 -> x2, starting transfers between devices: 7.07 us -> 13.8 us  [exchange_lines(): lax.all_to_all(pieces, ('dp', 'owner'), 0, 0, axis_index_groups=groups)]
    all_to_all x1 -> x2, waiting for transfers between devices: 14.6 us -> 21 us  [exchange_lines(): lax.all_to_all(pieces, ('dp', 'owner'), 0, 0, axis_index_groups=groups)]
    all_to_all x1, starting transfers between devices: 10 us -> 4.05 us  [exchange(): lax.all_to_all(pieces, ('dp', 'owner'), 0, 0, axis_index_groups=groups)]
    all_to_all x0 -> x1, starting transfers between devices: none -> 4.81 us  [on_device(): states = lax.all_to_all(state_pieces(assign, moment, second), 'owner', 0, 0)]
  transfers between devices with their start and end apart: 7 -> 10, of which waited for: 6 -> 8; matrix products, arithmetic and copies ran while one was open for 2% -> 4% of each run, Pallas kernels for 0% -> 2%
where the time goes in v4:
time: 155 us; the launch traced here: 154 us
  waiting for transfers between devices  62.3 us (40%)
  starting transfers between devices  56.8 us (37%)
  Pallas kernels  19.7 us (13%)
  other arithmetic  5.72 us (4%)
  between operations  5.22 us (3%)
  local copies, waits for them, and re-layouts  3.1 us (2%)
    all_to_all x2, waiting for transfers between devices, exchange_lines(): lax.all_to_all(pieces, ('dp', 'owner'), 0, 0, axis_index_groups=groups)  21 us
    pallas_call x1, Pallas kernels, first_payload(): pl.pallas_call(first_payload_kernel, out_shape=jax.ShapeDtypeStruct(grads...  17.1 us
    all_to_all x1, waiting for transfers between devices, exchange_dp(): return lax.all_to_all(pieces, 'dp', 0, 0, axis_index_groups=groups)  15.7 us
    all_to_all x2, starting transfers between devices, exchange_lines(): lax.all_to_all(pieces, ('dp', 'owner'), 0, 0, axis_index_groups=groups)  13.8 us
    all_to_all x1, starting transfers between devices, exchange_dp(): return lax.all_to_all(pieces, 'dp', 0, 0, axis_index_groups=groups)  12.8 us
    ppermute x3, starting transfers between devices, swap_cores(): lax.ppermute(value, 'dp', [(i, i ^ 1) for i in range(lax.axis_size('dp'))])  11.1 us
    ppermute x1, waiting for transfers between devices, on_device(): own_grams = own_grams + lax.ppermute(beside_grams, 'owner', owners_beside)  9.18 us
    all_to_all x1, waiting for transfers between devices, on_device(): states = lax.all_to_all(state_pieces(assign, moment, second), 'owner', 0, 0)  9.08 us
  transfers between devices with their start and end apart: 10, of which 8 were waited for; matrix products, arithmetic and copies ran while one was open for 4% of the time, Pallas kernels for 2%

profile of v4, /device:TPU:1, one launch (start us, length us, event | category | flops | bytes accessed | tf_op | source)
XLA Modules:
  0.0 154.3 jit_solution(12187576404513528973)
XLA Ops:
  0.7 17.1 %first_payload.1 = bf16[512,512]{1,0:T(8,128)(2,1)} custom-call(s32[1]{0:T(128)} %bitcast.1.core, bf16[1,1,512,512]{3,2,1,0:T(8,128)(2,1)} %grads.1, bf16[1,3,16,512]{3,2,1,0:T(8,128)(2,1)} %left.1, bf16[1,3,16,512]{3,2,1,0:T(8,128)(2,1)} %right.1), custom_call_target="tpu_custom_call" | custom-call | tf_op jit(solution)/shard_map/first_payload/pallas_call | solution.py:105
  17.8 1.9 %collective-permute-start = (bf16[512,512]{1,0:T(8,128)(2,1)}, bf16[512,512]{1,0:T(8,128)(2,1)S(1)}, u32[]{:S(2)}, u32[]{:S(2)}) collective-permute-start(bf16[512,512]{1,0:T(8,128)(2,1)} %first_payload.1), channel_id=1, source_target_pairs={{0,16},{16,0},{32,48},{48,32},{64,80},{80,64},{96,112},{112,96},{1... | collective-permute-start | bytes 1572872 | tf_op jit(solution)/shard_map/ppermute | solution.py:27
  20.5 1.2 collective-permute-done
  22.1 5.5 %collective-permute-start.1 = (bf16[256,512]{1,0:T(8,128)(2,1)S(1)}, bf16[256,512]{1,0:T(8,128)(2,1)S(1)}, u32[]{:S(2)}, u32[]{:S(2)}) collective-permute-start(bf16[256,512]{1,0:T(8,128)(2,1)S(1)} %pad_maximum_fusion.4), channel_id=1, source_target_pairs={{0,32},{16,17},{1,33},{17,16},{2,34},{18,19},{3,35},{19,18},{4,36}... | collective-permute-start | bytes 786440 | tf_op jit(solution)/shard_map/ppermute | solution.py:72
  27.6 5.1 %collective-permute-done.1 = bf16[256,512]{1,0:T(8,128)(2,1)S(1)} collective-permute-done((bf16[256,512]{1,0:T(8,128)(2,1)S(1)}, bf16[256,512]{1,0:T(8,128)(2,1)S(1)}, u32[]{:S(2)}, u32[]{:S(2)}) %collective-permute-start.1) | collective-permute-done | bytes 262176 | tf_op jit(solution)/shard_map/ppermute | solution.py:72
  33.3 0.8 pad_maximum_fusion.2
  34.2 10.3 %all-to-all-start = ((bf16[8,64,512]{2,1,0:T(8,128)(2,1)}), bf16[8,64,512]{2,1,0:T(8,128)(2,1)S(1)}, u32[]{:S(2)}, u32[]{:S(2)}) async-start(bf16[8,64,512]{2,1,0:T(8,128)(2,1)} %pad_maximum_fusion.2), calls=%async_computation | async-start | bytes 1048576 | tf_op jit(solution)/shard_map/all_to_all | solution.py:61
  44.5 2.7 %state_pieces.1 = bf16[16,2,16,512]{3,2,1,0:T(8,128)(2,1)} custom-call(s32[16]{0:T(128)} %assign.1, f32[1,3,16,512]{3,2,1,0:T(8,128)} %moment.1, f32[1,3,16,512]{3,2,1,0:T(8,128)} %second.1), custom_call_target="tpu_custom_call" | custom-call | tf_op jit(solution)/shard_map/state_pieces/pallas_call | solution.py:139
  47.2 9.4 %all-to-all-done = bf16[8,64,512]{2,1,0:T(8,128)(2,1)S(1)} async-done(((bf16[8,64,512]{2,1,0:T(8,128)(2,1)}), bf16[8,64,512]{2,1,0:T(8,128)(2,1)S(1)}, u32[]{:S(2)}, u32[]{:S(2)}) %all-to-all-start) | async-done | bytes 524320 | tf_op jit(solution)/shard_map/all_to_all | solution.py:61
  56.6 4.8 %all-to-all-start.2 = ((bf16[16,2,16,512]{3,2,1,0:T(8,128)(2,1)}), bf16[16,2,16,512]{3,2,1,0:T(8,128)(2,1)S(1)}, u32[]{:S(2)}, u32[]{:S(2)}) async-start(bf16[16,2,16,512]{3,2,1,0:T(8,128)(2,1)} %state_pieces.1), calls=%async_computation.2 | async-start | bytes 1048576 | tf_op jit(solution)/shard_map/all_to_all | solution.py:185
  64.8 0.9 pad_maximum_fusion.1
  65.7 9.1 %all-to-all-done.2 = bf16[16,2,16,512]{3,2,1,0:T(8,128)(2,1)S(1)} async-done(((bf16[16,2,16,512]{3,2,1,0:T(8,128)(2,1)}), bf16[16,2,16,512]{3,2,1,0:T(8,128)(2,1)S(1)}, u32[]{:S(2)}, u32[]{:S(2)}) %all-to-all-start.2) | async-done | bytes 524320 | tf_op jit(solution)/shard_map/all_to_all | solution.py:185
  74.8 12.8 %all-to-all-start.1 = ((bf16[16,32,640]{2,1,0:T(8,128)(2,1)}), bf16[16,32,640]{2,1,0:T(8,128)(2,1)S(1)}, u32[]{:S(2)}, u32[]{:S(2)}) async-start(bf16[16,32,640]{2,1,0:T(8,128)(2,1)} %pad_maximum_fusion.1), calls=%async_computation.1 | async-start | bytes 1310720 | tf_op jit(solution)/shard_map/all_to_all | solution.py:37
  89.0 15.7 %all-to-all-done.1 = bf16[16,32,640]{2,1,0:T(8,128)(2,1)S(1)} async-done(((bf16[16,32,640]{2,1,0:T(8,128)(2,1)}), bf16[16,32,640]{2,1,0:T(8,128)(2,1)S(1)}, u32[]{:S(2)}, u32[]{:S(2)}) %all-to-all-start.1) | async-done | bytes 655392 | tf_op jit(solution)/shard_map/all_to_all | solution.py:37
  104.9 5.9 %collective-permute-start.2 = (bf16[576,640]{1,0:T(8,128)(2,1)S(1)}, bf16[576,640]{1,0:T(8,128)(2,1)S(1)}, u32[]{:S(2)}, u32[]{:S(2)}) collective-permute-start(bf16[576,640]{1,0:T(8,128)(2,1)S(1)} %fusion.3), channel_id=1, source_target_pairs={{0,16},{16,0},{32,48},{48,32},{64,80},{80,64},{96,112},{112,96},{1... | collective-permute-start | bytes 2211848 | tf_op jit(solution)/shard_map/ppermute | solution.py:27
  111.3 0.8 broadcast_in_dim.196
  112.2 3.5 %all-to-all-start.3 = ((bf16[8,64,512]{2,1,0:T(8,128)(2,1)}), bf16[8,64,512]{2,1,0:T(8,128)(2,1)S(1)}, u32[]{:S(2)}, u32[]{:S(2)}) async-start(bf16[8,64,512]{2,1,0:T(8,128)(2,1)} %broadcast_in_dim.196), calls=%async_computation.3 | async-start | bytes 1048576 | tf_op jit(solution)/shard_map/all_to_all | solution.py:61
  116.5 11.5 %all-to-all-done.3 = bf16[8,64,512]{2,1,0:T(8,128)(2,1)S(1)} async-done(((bf16[8,64,512]{2,1,0:T(8,128)(2,1)}), bf16[8,64,512]{2,1,0:T(8,128)(2,1)S(1)}, u32[]{:S(2)}, u32[]{:S(2)}) %all-to-all-start.3) | async-done | bytes 524320 | tf_op jit(solution)/shard_map/all_to_all | solution.py:61
  128.0 0.8 broadcast_in_dim.195
  128.9 4.1 %all-to-all-start.4 = ((bf16[16,32,512]{2,1,0:T(8,128)(2,1)}), bf16[16,32,512]{2,1,0:T(8,128)(2,1)S(1)}, u32[]{:S(2)}, u32[]{:S(2)}) async-start(bf16[16,32,512]{2,1,0:T(8,128)(2,1)} %broadcast_in_dim.195), calls=%async_computation.4 | async-start | bytes 1048576 | tf_op jit(solution)/shard_map/all_to_all | solution.py:45
  133.8 4.8 %collective-permute-start.3 = (bf16[3,64,512]{2,1,0:T(8,128)(2,1)S(1)}, bf16[3,64,512]{2,1,0:T(8,128)(2,1)S(1)}, u32[]{:S(2)}, u32[]{:S(2)}) collective-permute-start(bf16[3,64,512]{2,1,0:T(8,128)(2,1)S(1)} %get-tuple-element.10), channel_id=1, source_target_pairs={{0,1},{1,0},{2,3},{3,2},{4,5},{5,4},{6,7},{7,6},{8,9},{9,8},{10,11... | collective-permute-start | bytes 589832 | tf_op jit(solution)/shard_map/ppermute | solution.py:275
  138.6 9.2 %collective-permute-done.3 = bf16[3,64,512]{2,1,0:T(8,128)(2,1)S(1)} collective-permute-done((bf16[3,64,512]{2,1,0:T(8,128)(2,1)S(1)}, bf16[3,64,512]{2,1,0:T(8,128)(2,1)S(1)}, u32[]{:S(2)}, u32[]{:S(2)}) %collective-permute-start.3) | collective-permute-done | bytes 196640 | tf_op jit(solution)/shard_map/ppermute | solution.py:275
  148.6 3.3 %collective-permute-start.4 = (bf16[112,512]{1,0:T(8,128)(2,1)S(1)}, bf16[112,512]{1,0:T(8,128)(2,1)S(1)}, u32[]{:S(2)}, u32[]{:S(2)}) collective-permute-start(bf16[112,512]{1,0:T(8,128)(2,1)S(1)} %pad_maximum_fusion.5), channel_id=1, source_target_pairs={{0,16},{16,0},{32,48},{48,32},{64,80},{80,64},{96,112},{112,96},{1... | collective-permute-start | bytes 344072 | tf_op jit(solution)/shard_map/ppermute | solution.py:27
  151.9 0.9 collective-permute-done.4
  (80 shorter events, 6.8 us)
Async XLA Ops:
  0.6 19.8 %copy-start.4 = (bf16[1,3,16,512]{3,2,1,0:T(8,128)(2,1)S(1)}, bf16[1,3,16,512]{3,2,1,0:T(8,128)(2,1)}, u32[]{:S(2)}) copy-start(bf16[1,3,16,512]{3,2,1,0:T(8,128)(2,1)} %right.1) | copy-start | bytes 147460
  0.6 19.8 %copy-start.3 = (bf16[1,3,16,512]{3,2,1,0:T(8,128)(2,1)S(1)}, bf16[1,3,16,512]{3,2,1,0:T(8,128)(2,1)}, u32[]{:S(2)}) copy-start(bf16[1,3,16,512]{3,2,1,0:T(8,128)(2,1)} %left.1) | copy-start | bytes 147460
  0.7 21.1 %copy-start = (bf16[1,1,512,512]{3,2,1,0:T(8,128)(2,1)S(1)}, bf16[1,1,512,512]{3,2,1,0:T(8,128)(2,1)}, u32[]{:S(2)}) copy-start(bf16[1,1,512,512]{3,2,1,0:T(8,128)(2,1)} %grads.1) | copy-start | bytes 1572868
  0.7 19.1 %copy-start.7 = (s32[16]{0:T(128)S(1)}, s32[16]{0:T(128)}, u32[]{:S(2)}) copy-start(s32[16]{0:T(128)} %assign.1) | copy-start | bytes 196
  17.8 4.0 %collective-permute-start = (bf16[512,512]{1,0:T(8,128)(2,1)}, bf16[512,512]{1,0:T(8,128)(2,1)S(1)}, u32[]{:S(2)}, u32[]{:S(2)}) collective-permute-start(bf16[512,512]{1,0:T(8,128)(2,1)} %first_payload.1), channel_id=1, source_target_pairs={{0,16},{16,0},{32,48},{48,32},{64,80},{80,64},{96,112},{112,96},{1... | collective-permute-start | bytes 1572872 | tf_op jit(solution)/shard_map/ppermute | solution.py:27
  22.1 10.7 %collective-permute-start.1 = (bf16[256,512]{1,0:T(8,128)(2,1)S(1)}, bf16[256,512]{1,0:T(8,128)(2,1)S(1)}, u32[]{:S(2)}, u32[]{:S(2)}) collective-permute-start(bf16[256,512]{1,0:T(8,128)(2,1)S(1)} %pad_maximum_fusion.4), channel_id=1, source_target_pairs={{0,32},{16,17},{1,33},{17,16},{2,34},{18,19},{3,35},{19,18},{4,36}... | collective-permute-start | bytes 786440 | tf_op jit(solution)/shard_map/ppermute | solution.py:72
  34.2 22.5 %all-to-all-start = ((bf16[8,64,512]{2,1,0:T(8,128)(2,1)}), bf16[8,64,512]{2,1,0:T(8,128)(2,1)S(1)}, u32[]{:S(2)}, u32[]{:S(2)}) async-start(bf16[8,64,512]{2,1,0:T(8,128)(2,1)} %pad_maximum_fusion.2), calls=%async_computation | async-start | bytes 1048576 | tf_op jit(solution)/shard_map/all_to_all | solution.py:61
  44.5 17.0 %copy-start.8 = (s32[16]{0:T(128)S(1)}, s32[16]{0:T(128)}, u32[]{:S(2)}) copy-start(s32[16]{0:T(128)} %assign.1) | copy-start | bytes 196
  56.6 18.2 %all-to-all-start.2 = ((bf16[16,2,16,512]{3,2,1,0:T(8,128)(2,1)}), bf16[16,2,16,512]{3,2,1,0:T(8,128)(2,1)S(1)}, u32[]{:S(2)}, u32[]{:S(2)}) async-start(bf16[16,2,16,512]{3,2,1,0:T(8,128)(2,1)} %state_pieces.1), calls=%async_computation.2 | async-start | bytes 1048576 | tf_op jit(solution)/shard_map/all_to_all | solution.py:185
  74.8 29.9 %all-to-all-start.1 = ((bf16[16,32,640]{2,1,0:T(8,128)(2,1)}), bf16[16,32,640]{2,1,0:T(8,128)(2,1)S(1)}, u32[]{:S(2)}, u32[]{:S(2)}) async-start(bf16[16,32,640]{2,1,0:T(8,128)(2,1)} %pad_maximum_fusion.1), calls=%async_computation.1 | async-start | bytes 1310720 | tf_op jit(solution)/shard_map/all_to_all | solution.py:37
  104.9 10.8 %collective-permute-start.2 = (bf16[576,640]{1,0:T(8,128)(2,1)S(1)}, bf16[576,640]{1,0:T(8,128)(2,1)S(1)}, u32[]{:S(2)}, u32[]{:S(2)}) collective-permute-start(bf16[576,640]{1,0:T(8,128)(2,1)S(1)} %fusion.3), channel_id=1, source_target_pairs={{0,16},{16,0},{32,48},{48,32},{64,80},{80,64},{96,112},{112,96},{1... | collective-permute-start | bytes 2211848 | tf_op jit(solution)/shard_map/ppermute | solution.py:27
  112.2 15.8 %all-to-all-start.3 = ((bf16[8,64,512]{2,1,0:T(8,128)(2,1)}), bf16[8,64,512]{2,1,0:T(8,128)(2,1)S(1)}, u32[]{:S(2)}, u32[]{:S(2)}) async-start(bf16[8,64,512]{2,1,0:T(8,128)(2,1)} %broadcast_in_dim.196), calls=%async_computation.3 | async-start | bytes 1048576 | tf_op jit(solution)/shard_map/all_to_all | solution.py:61
  128.9 19.0 %all-to-all-start.4 = ((bf16[16,32,512]{2,1,0:T(8,128)(2,1)}), bf16[16,32,512]{2,1,0:T(8,128)(2,1)S(1)}, u32[]{:S(2)}, u32[]{:S(2)}) async-start(bf16[16,32,512]{2,1,0:T(8,128)(2,1)} %broadcast_in_dim.195), calls=%async_computation.4 | async-start | bytes 1048576 | tf_op jit(solution)/shard_map/all_to_all | solution.py:45
  133.8 14.0 %collective-permute-start.3 = (bf16[3,64,512]{2,1,0:T(8,128)(2,1)S(1)}, bf16[3,64,512]{2,1,0:T(8,128)(2,1)S(1)}, u32[]{:S(2)}, u32[]{:S(2)}) collective-permute-start(bf16[3,64,512]{2,1,0:T(8,128)(2,1)S(1)} %get-tuple-element.10), channel_id=1, source_target_pairs={{0,1},{1,0},{2,3},{3,2},{4,5},{5,4},{6,7},{7,6},{8,9},{9,8},{10,11... | collective-permute-start | bytes 589832 | tf_op jit(solution)/shard_map/ppermute | solution.py:275
  148.2 4.7 %copy-start.1 = (f32[1,3,16,512]{3,2,1,0:T(8,128)S(1)}, f32[1,3,16,512]{3,2,1,0:T(8,128)}, u32[]{:S(2)}) copy-start(f32[1,3,16,512]{3,2,1,0:T(8,128)} %moment.1) | copy-start | bytes 294916
  148.2 4.7 %copy-start.2 = (f32[1,3,16,512]{3,2,1,0:T(8,128)S(1)}, f32[1,3,16,512]{3,2,1,0:T(8,128)}, u32[]{:S(2)}) copy-start(f32[1,3,16,512]{3,2,1,0:T(8,128)} %second.1) | copy-start | bytes 294916
  148.2 4.7 %copy-start.5 = (f32[1,3,16,512]{3,2,1,0:T(8,128)S(1)}, f32[1,3,16,512]{3,2,1,0:T(8,128)}, u32[]{:S(2)}) copy-start(f32[1,3,16,512]{3,2,1,0:T(8,128)} %param.12) | copy-start | bytes 294916
  148.3 4.7 %copy-start.6 = (f32[1,3,16,512]{3,2,1,0:T(8,128)S(1)}, f32[1,3,16,512]{3,2,1,0:T(8,128)}, u32[]{:S(2)}) copy-start(f32[1,3,16,512]{3,2,1,0:T(8,128)} %param.13) | copy-start | bytes 294916
  148.6 4.2 %collective-permute-start.4 = (bf16[112,512]{1,0:T(8,128)(2,1)S(1)}, bf16[112,512]{1,0:T(8,128)(2,1)S(1)}, u32[]{:S(2)}, u32[]{:S(2)}) collective-permute-start(bf16[112,512]{1,0:T(8,128)(2,1)S(1)} %pad_maximum_fusion.5), channel_id=1, source_target_pairs={{0,16},{16,0},{32,48},{48,32},{64,80},{80,64},{96,112},{112,96},{1... | collective-permute-start | bytes 344072 | tf_op jit(solution)/shard_map/ppermute | solution.py:27

commit v5 on v4

v5 whole, which is shorter than its diff:
```python
import jax
import jax.numpy as jnp
from jax import lax
from jax.experimental import pallas as pl
from jax.experimental.pallas import tpu as pltpu
from jax.sharding import PartitionSpec as P

beta_one = 0.9
beta_two = 0.95
step_count = 10.0
adam_eps = 1e-08
bias_one = 1.0 - beta_one**step_count
bias_two = 1.0 - beta_two**step_count

LANES = 128
half = jnp.bfloat16


def slot_numbers(assign):
    positions = jnp.arange(assign.shape[0], dtype=jnp.int32)
    matching = assign[:, None] == assign[None, :]
    earlier = positions[None, :] < positions[:, None]
    return jnp.sum((matching & earlier).astype(jnp.int32), axis=1)


def swap_cores(value):
    return lax.ppermute(value, "dp", [(i, i ^ 1) for i in range(lax.axis_size("dp"))])


def place(chip, core, owner):
    return (chip * 2 + core) * lax.axis_size("owner") + owner


def exchange_dp(pieces):
    chips = lax.axis_size("dp") // 2
    groups = [[chip * 2 + core for chip in range(chips)] for core in range(2)]
    return lax.all_to_all(pieces, "dp", 0, 0, axis_index_groups=groups)


def exchange(pieces):
    chips = lax.axis_size("dp") // 2
    owners = lax.axis_size("owner")
    groups = [[place(chip, 0, owner) for chip in range(chips)] for owner in range(owners)]
    groups += [[place(chip, 1, owner) for owner in range(owners)] for chip in range(chips)]
    return lax.all_to_all(pieces, ("dp", "owner"), 0, 0, axis_index_groups=groups)


def shift_z(value, step):
    owners = lax.axis_size("owner")
    return lax.ppermute(
        value, "owner", [(i, (i + 2 * step) % owners) for i in range(owners)]
    )


def swap_owners(value):
    return lax.ppermute(value, "owner", [(i, i ^ 1) for i in range(lax.axis_size("owner"))])


def z_order(value, z):
    return lax.dynamic_slice_in_dim(jnp.concatenate([value, value], 0), z, value.shape[0], 0)


def first_payload_kernel(core, grads, left, right, payload, sems):
    slot_cap, row_num = left.shape[1:3]

    @pl.when(core[0] == 0)
    def _():
        moves = []
        for slot in range(slot_cap):
            for kind, basis in enumerate((left, right)):
                place_of = slot * 2 + kind
                moves.append(
                    pltpu.make_async_copy(
                        basis.at[0, slot],
                        payload.at[pl.ds(place_of * row_num, row_num)],
                        sems.at[place_of],
                    )
                )
        for move in moves:
            move.start()
        for move in moves:
            move.wait()

    @pl.when(core[0] != 0)
    def _():
        move = pltpu.make_async_copy(grads.at[0, 0], payload, sems.at[0])
        move.start()
        move.wait()


def first_payload(core, grads, left, right):
    anywhere = pl.BlockSpec(memory_space=pl.ANY)
    return pl.pallas_call(
        first_payload_kernel,
        out_shape=jax.ShapeDtypeStruct(grads.shape[2:], half),
        in_specs=[pl.BlockSpec(memory_space=pltpu.SMEM)] + [anywhere] * 3,
        out_specs=pl.BlockSpec(memory_space=pltpu.VMEM),
        scratch_shapes=[pltpu.SemaphoreType.DMA((2 * left.shape[1],))],
        compiler_params=pltpu.CompilerParams(vmem_limit_bytes=60 * 1024 * 1024),
        name="first_payload",
    )(core, grads, left, right)


def copies(value, count):
    return jnp.broadcast_to(value[None], (count,) + value.shape)


def dot(left, right, contract):
    return lax.dot_general(
        left, right, ((contract[:1], contract[1:]), ((), ())), preferred_element_type=jnp.float32
    )


def on_device(grad_parts, assign, left_basis, right_basis, left_stat, right_stat, moment, second):
    row_index = lax.axis_index("dp")
    owner = lax.axis_index("owner")
    dp_num = lax.axis_size("dp")
    owner_num = lax.axis_size("owner")
    col_num = grad_parts.shape[3]
    row_num = col_num // dp_num
    slot_cap = left_basis.shape[1]
    chunk_num = col_num // LANES
    chips = dp_num // 2
    chip = row_index // 2
    first = row_index % 2 == 0
    chip_rows = 2 * row_num
    z_num = owner_num // 2
    z = owner // 2
    kinds = 2

    came = swap_cores(
        first_payload((row_index % 2).reshape(1), grad_parts, left_basis, right_basis)
    )
    numbers = slot_numbers(assign)
    chip_grads = jnp.stack(
        [grad_parts.reshape(chips, chip_rows, col_num), came.reshape(chips, chip_rows, col_num)], 1
    ).reshape(chips, 2 * chip_rows, col_num)
    slots = jnp.stack([left_basis[0], right_basis[0]], 1)
    slot_rows = slot_cap * kinds * row_num
    chip_slots = jnp.stack([came[:slot_rows].reshape(slots.shape), slots], 2)
    chip_slots = chip_slots.reshape(slot_cap, kinds * chip_rows, col_num)
    code = numbers[:, None, None]
    picked = chip_slots[0][None]
    for slot in range(1, slot_cap):
        picked = jnp.where(code == slot, chip_slots[slot][None], picked)

    parts = exchange(jnp.where(first, chip_grads, picked))
    grad_rows = jnp.sum(
        parts.reshape(2 * chips, chip_rows, col_num).astype(jnp.float32), axis=0
    ).astype(half)
    home = lax.dynamic_index_in_dim(parts, assign[owner], 0, keepdims=False)

    states = jnp.stack([moment[0], second[0]], 1).astype(half)
    states, came = lax.optimization_barrier((states, came))
    beside = swap_owners(states)
    owner_x = owner % 2
    from_owner = lax.dynamic_index_in_dim(assign.reshape(z_num, 2), owner_x, 1, keepdims=False)
    number = lax.dynamic_index_in_dim(numbers.reshape(z_num, 2), owner_x, 1, keepdims=False)
    code = number + slot_cap * (from_owner % 2 != owner_x)
    code = z_order(code, z)[:, None, None, None]
    states = jnp.concatenate([states, beside], 0)
    picked = states[0][None]
    for slot in range(1, 2 * slot_cap):
        picked = jnp.where(code == slot, states[slot][None], picked)
    picked, home = lax.optimization_barrier((picked, home))
    states = picked[0]
    distance = (z - assign[owner] // 2) % z_num
    for step in range(1, z_num):
        states = jnp.where(distance == step, shift_z(picked[step], step), states)

    left_rows, right_rows = home.reshape(kinds, chip_rows, col_num)
    left_chunks = left_rows.reshape(chip_rows, chunk_num, LANES).transpose(1, 0, 2)
    left_chunks = jnp.broadcast_to(
        left_chunks[:, None], (chunk_num, chips // chunk_num, chip_rows, LANES)
    ).reshape(chips, chip_rows, LANES)
    rows = copies(jnp.where(first, grad_rows, right_rows), chips)
    mine = exchange_dp(jnp.concatenate([rows, left_chunks], 2))
    mine = mine.reshape(col_num, col_num + LANES)

    extra = jnp.concatenate([left_rows, states.reshape(-1, col_num)], 0)
    extra = jnp.concatenate([extra, extra[:, :LANES]], 1)
    other = swap_cores(jnp.concatenate([mine, extra], 0))
    left_rows = other[col_num : col_num + chip_rows, :col_num]
    other_states = other[col_num + chip_rows :, :col_num].reshape(states.shape)
    states = jnp.concatenate([states, other_states], 1).astype(jnp.float32)
    other = other[:col_num]
    core_full = mine[:, :col_num]
    grad_full = jnp.where(first, core_full, other[:, :col_num])
    right_full = jnp.where(first, other[:, :col_num], core_full)
    left_cols = jnp.where(first, other[:, col_num:], mine[:, col_num:])

    chunk = row_index // (dp_num // chunk_num)
    in_chunk = (row_index % (dp_num // chunk_num)) * row_num
    grad_cols = lax.dynamic_slice_in_dim(grad_full, chunk * LANES, LANES, 1)
    grad_rows = lax.dynamic_slice_in_dim(grad_full, row_index * row_num, row_num, 0)
    left_term = dot(grad_rows, grad_full, (1, 1)).astype(half)
    right_term = dot(grad_cols, grad_full, (0, 0)).astype(half)
    right_term = lax.dynamic_slice_in_dim(right_term, in_chunk, row_num, 0)
    grams = jnp.stack([left_term, right_term])
    beside = swap_owners(grams)
    grams = jnp.where(
        owner_x == 0, jnp.stack([grams, beside], 0), jnp.stack([beside, grams], 0)
    )

    in_chunk = (chip % (chips // chunk_num)) * chip_rows
    turned = dot(left_cols, grad_full, (0, 0)).astype(half)
    turned = lax.dynamic_slice_in_dim(turned, in_chunk, chip_rows, 0)
    rotated = dot(turned, right_full, (1, 0))
    home_moment = beta_one * states[0] + (1.0 - beta_one) * rotated
    home_second = beta_two * states[1] + (1.0 - beta_two) * rotated * rotated
    direction = (home_moment / bias_one / (jnp.sqrt(home_second / bias_two) + adam_eps)).astype(half)
    back_rows = dot(direction, right_full, (1, 1)).astype(half)

    results = copies(jnp.where(first, back_rows, rotated.astype(half)), chips)
    results, grams = lax.optimization_barrier((results, grams))
    gathered = exchange(results)

    held = (assign == owner)[None, :] & (
        numbers[None, :] == jnp.arange(slot_cap, dtype=jnp.int32)[:, None]
    )
    held_z = held.reshape(slot_cap, z_num, 2)
    behind = lax.dynamic_slice_in_dim(
        jnp.concatenate([held_z[:, ::-1], held_z[:, ::-1]], 1), z_num - 1 - z, z_num, 1
    )
    all_grams = [grams] + [shift_z(grams, step) for step in range(1, z_num)]
    slot_grams = jnp.zeros((slot_cap,) + grams.shape[1:], half)
    for step, values in enumerate(all_grams):
        for x in range(2):
            mask = behind[:, step, x][:, None, None, None]
            slot_grams = jnp.where(mask, values[x][None], slot_grams)
    slot_grams = slot_grams.astype(jnp.float32)

    back_full = gathered.reshape(col_num, col_num)
    chip_update = dot(left_rows, back_full, (1, 0)).astype(half)
    turns = jnp.where(held[:, :, None, None], gathered[None].astype(jnp.float32), 0.0)
    turns = jnp.sum(turns, axis=1).astype(half).reshape(slot_cap, 2, row_num, col_num)
    for_second = jnp.concatenate([chip_update[row_num:], turns[1:, 0].reshape(-1, col_num)], 0)
    came = swap_cores(jnp.where(first, for_second, turns[:, 0].reshape(-1, col_num)))
    update = jnp.where(first, chip_update[:row_num], came[:row_num])
    turns = jnp.where(first, came.reshape(turns[:, 0].shape), turns[:, 1]).astype(jnp.float32)

    new_left = beta_two * left_stat[0] + (1.0 - beta_two) * slot_grams[:, 0]
    new_right = beta_two * right_stat[0] + (1.0 - beta_two) * slot_grams[:, 1]
    new_moment = beta_one * moment[0] + (1.0 - beta_one) * turns
    new_second = beta_two * second[0] + (1.0 - beta_two) * turns * turns
    return (update[None], new_left[None], new_right[None], new_moment[None], new_second[None])


def solution(mesh):
    placed = (
        P("dp", "owner", None, None),
        P(),
        P("owner", None, "dp", None),
        P("owner", None, "dp", None),
        P("owner", None, "dp", None),
        P("owner", None, "dp", None),
        P("owner", None, "dp", None),
        P("owner", None, "dp", None),
    )
    return jax.shard_map(
        on_device,
        mesh=mesh,
        in_specs=placed,
        out_specs=(
            P("owner", "dp", None),
            P("owner", None, "dp", None),
            P("owner", None, "dp", None),
            P("owner", None, "dp", None),
            P("owner", None, "dp", None),
        ),
        check_vma=False,
    )
```

time: 155 us -> 143 us (0.923)
  starting transfers between devices: 56.8 us -> 103 us
  waiting for transfers between devices: 62.3 us -> 20.8 us
  Pallas kernels: 19.7 us -> 1.96 us
    ppermute x2 -> x16, starting transfers between devices: 10.3 us -> 63.3 us  [the longest x14 55.3 us: shift_z(): lax.ppermute(value, 'owner', [(i, (i + 2 * step) % owners) for i in range...]
    all_to_all x3 -> x0, waiting for transfers between devices: 30 us -> none  [the longest x2 21 us: exchange_lines(): lax.all_to_all(pieces, ('dp', 'owner'), 0, 0, axis_index_groups=groups)]
    all_to_all x3 -> x0, starting transfers between devices: 18.6 us -> none  [the longest x2 13.8 us: exchange_lines(): lax.all_to_all(pieces, ('dp', 'owner'), 0, 0, axis_index_groups=groups)]
    all_to_all x1, waiting for transfers between devices: 15.7 us -> 0.01 us  [exchange_dp(): return lax.all_to_all(pieces, 'dp', 0, 0, axis_index_groups=groups)]
    pallas_call x1, Pallas kernels: 17.1 us -> 1.96 us  [first_payload(): pl.pallas_call(first_payload_kernel, out_shape=jax.ShapeDtypeStruct(grads...]
    all_to_all x1 -> x2, starting transfers between devices: 4.05 us -> 14.8 us  [exchange(): lax.all_to_all(pieces, ('dp', 'owner'), 0, 0, axis_index_groups=groups)]
    ppermute x3, starting transfers between devices: 11.1 us -> 18.3 us  [swap_cores(): lax.ppermute(value, 'dp', [(i, i ^ 1) for i in range(lax.axis_size('dp'))])]
    all_to_all x1, starting transfers between devices: 12.8 us -> 6.64 us  [exchange_dp(): return lax.all_to_all(pieces, 'dp', 0, 0, axis_index_groups=groups)]
  transfers between devices with their start and end apart: 10 -> 22, of which waited for: 8 -> 9; matrix products, arithmetic and copies ran while one was open for 4% -> 3% of each run, Pallas kernels for 2% -> 0%
where the time goes in v5:
time: 143 us; the launch traced here: 142 us
  starting transfers between devices  103 us (72%)
  waiting for transfers between devices  20.8 us (15%)
  other arithmetic  6.01 us (4%)
  between operations  5.33 us (4%)
  local copies, waits for them, and re-layouts  3.01 us (2%)
  Pallas kernels  1.96 us (1%)
    ppermute x14, starting transfers between devices, shift_z(): lax.ppermute(value, 'owner', [(i, (i + 2 * step) % owners) for i in range...  55.3 us
    ppermute x3, starting transfers between devices, swap_cores(): lax.ppermute(value, 'dp', [(i, i ^ 1) for i in range(lax.axis_size('dp'))])  18.3 us
    all_to_all x2, starting transfers between devices, exchange(): lax.all_to_all(pieces, ('dp', 'owner'), 0, 0, axis_index_groups=groups)  14.8 us
    ppermute x2, waiting for transfers between devices, swap_owners(): lax.ppermute(value, 'owner', [(i, i ^ 1) for i in range(lax.axis_size('ow...  13 us
    ppermute x2, starting transfers between devices, swap_owners(): lax.ppermute(value, 'owner', [(i, i ^ 1) for i in range(lax.axis_size('ow...  7.99 us
    all_to_all x1, starting transfers between devices, exchange_dp(): return lax.all_to_all(pieces, 'dp', 0, 0, axis_index_groups=groups)  6.64 us
    ppermute x14, waiting for transfers between devices, shift_z(): lax.ppermute(value, 'owner', [(i, (i + 2 * step) % owners) for i in range...  3.87 us
  transfers between devices with their start and end apart: 22, of which 9 were waited for; matrix products, arithmetic and copies ran while one was open for 3% of the time, Pallas kernels for 0%

profile of v5, /device:TPU:1, one launch (start us, length us, event | category | flops | bytes accessed | tf_op | source)
XLA Modules:
  0.0 141.6 jit_solution(7593686935384736864)
XLA Ops:
  2.7 8.5 %collective-permute-start = (bf16[512,512]{1,0:T(8,128)(2,1)}, bf16[512,512]{1,0:T(8,128)(2,1)S(1)}, u32[]{:S(2)}, u32[]{:S(2)}) collective-permute-start(bf16[512,512]{1,0:T(8,128)(2,1)} %first_payload.1), channel_id=1, source_target_pairs={{0,16},{16,0},{32,48},{48,32},{64,80},{80,64},{96,112},{112,96},{1... | collective-permute-start | bytes 1572872 | tf_op jit(solution)/shard_map/ppermute | solution.py:27
  14.4 7.4 %all-to-all-start = ((bf16[16,64,512]{2,1,0:T(8,128)(2,1)}), bf16[16,64,512]{2,1,0:T(8,128)(2,1)S(1)}, u32[]{:S(2)}, u32[]{:S(2)}) async-start(bf16[16,64,512]{2,1,0:T(8,128)(2,1)} %bitcast_select_fusion), calls=%async_computation | async-start | bytes 2097152 | tf_op jit(solution)/shard_map/all_to_all | solution.py:45
  25.1 4.8 %collective-permute-start.1 = (bf16[3,2,16,512]{3,2,0,1:T(8,128)(2,1)S(1)}, bf16[3,2,16,512]{3,2,0,1:T(8,128)(2,1)S(1)}, u32[]{:S(2)}, u32[]{:S(2)}) collective-permute-start(bf16[3,2,16,512]{3,2,0,1:T(8,128)(2,1)S(1)} %pad_maximum_fusion.3), channel_id=1, source_target_pairs={{0,1},{1,0},{2,3},{3,2},{4,5},{5,4},{6,7},{7,6},{8,9},{9,8},{10,11... | collective-permute-start | bytes 294920 | tf_op jit(solution)/shard_map/ppermute | solution.py:56
  29.9 10.8 %collective-permute-done.1 = bf16[3,2,16,512]{3,2,0,1:T(8,128)(2,1)S(1)} collective-permute-done((bf16[3,2,16,512]{3,2,0,1:T(8,128)(2,1)S(1)}, bf16[3,2,16,512]{3,2,0,1:T(8,128)(2,1)S(1)}, u32[]{:S(2)}, u32[]{:S(2)}) %collective-permute-start.1) | collective-permute-done | bytes 98336 | tf_op jit(solution)/shard_map/ppermute | solution.py:56
  42.1 6.6 %all-to-all-start.1 = ((bf16[16,32,640]{2,1,0:T(8,128)(2,1)}), bf16[16,32,640]{2,1,0:T(8,128)(2,1)S(1)}, u32[]{:S(2)}, u32[]{:S(2)}) async-start(bf16[16,32,640]{2,1,0:T(8,128)(2,1)} %pad_maximum_fusion.2), calls=%async_computation.1 | async-start | bytes 1310720 | tf_op jit(solution)/shard_map/all_to_all | solution.py:37
  48.8 6.2 %collective-permute-start.2 = (bf16[2,16,512]{2,1,0:T(8,128)(2,1)S(1)}, bf16[2,16,512]{2,1,0:T(8,128)(2,1)S(1)}, u32[]{:S(2)}, u32[]{:S(2)}) collective-permute-start(bf16[2,16,512]{2,1,0:T(8,128)(2,1)S(1)} %get-tuple-element.39), channel_id=1, source_target_pairs={{0,14},{1,15},{2,0},{3,1},{4,2},{5,3},{6,4},{7,5},{8,6},{9,7},{10,... | collective-permute-start | bytes 98312 | tf_op jit(solution)/shard_map/ppermute | solution.py:50
  55.0 4.7 %collective-permute-start.3 = (bf16[2,16,512]{2,1,0:T(8,128)(2,1)S(1)}, bf16[2,16,512]{2,1,0:T(8,128)(2,1)S(1)}, u32[]{:S(2)}, u32[]{:S(2)}) collective-permute-start(bf16[2,16,512]{2,1,0:T(8,128)(2,1)S(1)} %get-tuple-element.38), channel_id=1, source_target_pairs={{0,12},{1,13},{2,14},{3,15},{4,0},{5,1},{6,2},{7,3},{8,4},{9,5},{1... | collective-permute-start | bytes 98312 | tf_op jit(solution)/shard_map/ppermute | solution.py:50
  59.7 2.3 %collective-permute-start.4 = (bf16[2,16,512]{2,1,0:T(8,128)(2,1)S(1)}, bf16[2,16,512]{2,1,0:T(8,128)(2,1)S(1)}, u32[]{:S(2)}, u32[]{:S(2)}) collective-permute-start(bf16[2,16,512]{2,1,0:T(8,128)(2,1)S(1)} %get-tuple-element.37), channel_id=1, source_target_pairs={{0,10},{1,11},{2,12},{3,13},{4,14},{5,15},{6,0},{7,1},{8,2},{9,3},... | collective-permute-start | bytes 98312 | tf_op jit(solution)/shard_map/ppermute | solution.py:50
  62.0 5.2 %collective-permute-start.5 = (bf16[2,16,512]{2,1,0:T(8,128)(2,1)S(1)}, bf16[2,16,512]{2,1,0:T(8,128)(2,1)S(1)}, u32[]{:S(2)}, u32[]{:S(2)}) collective-permute-start(bf16[2,16,512]{2,1,0:T(8,128)(2,1)S(1)} %get-tuple-element.36), channel_id=1, source_target_pairs={{0,8},{1,9},{2,10},{3,11},{4,12},{5,13},{6,14},{7,15},{8,0},{9,1},... | collective-permute-start | bytes 98312 | tf_op jit(solution)/shard_map/ppermute | solution.py:50
  69.1 5.2 %collective-permute-start.7 = (bf16[2,16,512]{2,1,0:T(8,128)(2,1)S(1)}, bf16[2,16,512]{2,1,0:T(8,128)(2,1)S(1)}, u32[]{:S(2)}, u32[]{:S(2)}) collective-permute-start(bf16[2,16,512]{2,1,0:T(8,128)(2,1)S(1)} %get-tuple-element.34), channel_id=1, source_target_pairs={{0,4},{1,5},{2,6},{3,7},{4,8},{5,9},{6,10},{7,11},{8,12},{9,13},{1... | collective-permute-start | bytes 98312 | tf_op jit(solution)/shard_map/ppermute | solution.py:50
  74.3 3.4 %collective-permute-start.8 = (bf16[2,16,512]{2,1,0:T(8,128)(2,1)S(1)}, bf16[2,16,512]{2,1,0:T(8,128)(2,1)S(1)}, u32[]{:S(2)}, u32[]{:S(2)}) collective-permute-start(bf16[2,16,512]{2,1,0:T(8,128)(2,1)S(1)} %get-tuple-element.33), channel_id=1, source_target_pairs={{0,2},{1,3},{2,4},{3,5},{4,6},{5,7},{6,8},{7,9},{8,10},{9,11},{10,... | collective-permute-start | bytes 98312 | tf_op jit(solution)/shard_map/ppermute | solution.py:50
  80.3 5.2 %collective-permute-start.9 = (bf16[576,640]{1,0:T(8,128)(2,1)S(1)}, bf16[576,640]{1,0:T(8,128)(2,1)S(1)}, u32[]{:S(2)}, u32[]{:S(2)}) collective-permute-start(bf16[576,640]{1,0:T(8,128)(2,1)S(1)} %fusion.3), channel_id=1, source_target_pairs={{0,16},{16,0},{32,48},{48,32},{64,80},{80,64},{96,112},{112,96},{1... | collective-permute-start | bytes 2211848 | tf_op jit(solution)/shard_map/ppermute | solution.py:27
  87.9 3.2 %collective-permute-start.10 = (bf16[2,16,512]{2,1,0:T(8,128)(2,1)S(1)}, bf16[2,16,512]{2,1,0:T(8,128)(2,1)S(1)}, u32[]{:S(2)}, u32[]{:S(2)}) collective-permute-start(bf16[2,16,512]{2,1,0:T(8,128)(2,1)S(1)} %get-tuple-element.72), channel_id=1, source_target_pairs={{0,1},{1,0},{2,3},{3,2},{4,5},{5,4},{6,7},{7,6},{8,9},{9,8},{10,11... | collective-permute-start | bytes 98312 | tf_op jit(solution)/shard_map/ppermute | solution.py:56
  91.9 2.2 %collective-permute-done.10 = bf16[2,16,512]{2,1,0:T(8,128)(2,1)S(1)} collective-permute-done((bf16[2,16,512]{2,1,0:T(8,128)(2,1)S(1)}, bf16[2,16,512]{2,1,0:T(8,128)(2,1)S(1)}, u32[]{:S(2)}, u32[]{:S(2)}) %collective-permute-start.10) | collective-permute-done | bytes 32800 | tf_op jit(solution)/shard_map/ppermute | solution.py:56
  94.9 2.4 %collective-permute-start.18 = (bf16[2,2,16,512]{3,2,1,0:T(8,128)(2,1)S(1)}, bf16[2,2,16,512]{3,2,1,0:T(8,128)(2,1)S(1)}, u32[]{:S(2)}, u32[]{:S(2)}) collective-permute-start(bf16[2,2,16,512]{3,2,1,0:T(8,128)(2,1)S(1)} %maximum_select_fusion), channel_id=1, source_target_pairs={{0,2},{1,3},{2,4},{3,5},{4,6},{5,7},{6,8},{7,9},{8,10},{9,11},{10,... | collective-permute-start | bytes 196616 | tf_op jit(solution)/shard_map/ppermute | solution.py:50
  97.4 3.7 %collective-permute-start.17 = (bf16[2,2,16,512]{3,2,1,0:T(8,128)(2,1)S(1)}, bf16[2,2,16,512]{3,2,1,0:T(8,128)(2,1)S(1)}, u32[]{:S(2)}, u32[]{:S(2)}) collective-permute-start(bf16[2,2,16,512]{3,2,1,0:T(8,128)(2,1)S(1)} %maximum_select_fusion), channel_id=1, source_target_pairs={{0,4},{1,5},{2,6},{3,7},{4,8},{5,9},{6,10},{7,11},{8,12},{9,13},{1... | collective-permute-start | bytes 196616 | tf_op jit(solution)/shard_map/ppermute | solution.py:50
  101.1 3.6 %collective-permute-start.16 = (bf16[2,2,16,512]{3,2,1,0:T(8,128)(2,1)S(1)}, bf16[2,2,16,512]{3,2,1,0:T(8,128)(2,1)S(1)}, u32[]{:S(2)}, u32[]{:S(2)}) collective-permute-start(bf16[2,2,16,512]{3,2,1,0:T(8,128)(2,1)S(1)} %maximum_select_fusion), channel_id=1, source_target_pairs={{0,6},{1,7},{2,8},{3,9},{4,10},{5,11},{6,12},{7,13},{8,14},{9,15},... | collective-permute-start | bytes 196616 | tf_op jit(solution)/shard_map/ppermute | solution.py:50
  104.7 4.8 %collective-permute-start.15 = (bf16[2,2,16,512]{3,2,1,0:T(8,128)(2,1)S(1)}, bf16[2,2,16,512]{3,2,1,0:T(8,128)(2,1)S(1)}, u32[]{:S(2)}, u32[]{:S(2)}) collective-permute-start(bf16[2,2,16,512]{3,2,1,0:T(8,128)(2,1)S(1)} %maximum_select_fusion), channel_id=1, source_target_pairs={{0,8},{1,9},{2,10},{3,11},{4,12},{5,13},{6,14},{7,15},{8,0},{9,1},... | collective-permute-start | bytes 196616 | tf_op jit(solution)/shard_map/ppermute | solution.py:50
  109.5 3.5 %collective-permute-start.14 = (bf16[2,2,16,512]{3,2,1,0:T(8,128)(2,1)S(1)}, bf16[2,2,16,512]{3,2,1,0:T(8,128)(2,1)S(1)}, u32[]{:S(2)}, u32[]{:S(2)}) collective-permute-start(bf16[2,2,16,512]{3,2,1,0:T(8,128)(2,1)S(1)} %maximum_select_fusion), channel_id=1, source_target_pairs={{0,10},{1,11},{2,12},{3,13},{4,14},{5,15},{6,0},{7,1},{8,2},{9,3},... | collective-permute-start | bytes 196616 | tf_op jit(solution)/shard_map/ppermute | solution.py:50
  113.0 7.5 %all-to-all-start.2 = ((bf16[16,32,512]{2,1,0:T(8,128)(2,1)}), bf16[16,32,512]{2,1,0:T(8,128)(2,1)S(1)}, u32[]{:S(2)}, u32[]{:S(2)}) async-start(bf16[16,32,512]{2,1,0:T(8,128)(2,1)} %broadcast_in_dim.444), calls=%async_computation.2 | async-start | bytes 1048576 | tf_op jit(solution)/shard_map/all_to_all | solution.py:45
  120.4 5.4 %collective-permute-start.13 = (bf16[2,2,16,512]{3,2,1,0:T(8,128)(2,1)S(1)}, bf16[2,2,16,512]{3,2,1,0:T(8,128)(2,1)S(1)}, u32[]{:S(2)}, u32[]{:S(2)}) collective-permute-start(bf16[2,2,16,512]{3,2,1,0:T(8,128)(2,1)S(1)} %maximum_select_fusion), channel_id=1, source_target_pairs={{0,12},{1,13},{2,14},{3,15},{4,0},{5,1},{6,2},{7,3},{8,4},{9,5},{1... | collective-permute-start | bytes 196616 | tf_op jit(solution)/shard_map/ppermute | solution.py:50
  125.9 3.1 %collective-permute-start.12 = (bf16[2,2,16,512]{3,2,1,0:T(8,128)(2,1)S(1)}, bf16[2,2,16,512]{3,2,1,0:T(8,128)(2,1)S(1)}, u32[]{:S(2)}, u32[]{:S(2)}) collective-permute-start(bf16[2,2,16,512]{3,2,1,0:T(8,128)(2,1)S(1)} %maximum_select_fusion), channel_id=1, source_target_pairs={{0,14},{1,15},{2,0},{3,1},{4,2},{5,3},{6,4},{7,5},{8,6},{9,7},{10,... | collective-permute-start | bytes 196616 | tf_op jit(solution)/shard_map/ppermute | solution.py:50
  129.0 2.5 %collective-permute-done.13 = bf16[2,2,16,512]{3,2,1,0:T(8,128)(2,1)S(1)} collective-permute-done((bf16[2,2,16,512]{3,2,1,0:T(8,128)(2,1)S(1)}, bf16[2,2,16,512]{3,2,1,0:T(8,128)(2,1)S(1)}, u32[]{:S(2)}, u32[]{:S(2)}) %collective-permute-start.13) | collective-permute-done | bytes 65568 | tf_op jit(solution)/shard_map/ppermute | solution.py:50
  134.8 4.6 %collective-permute-start.11 = (bf16[48,512]{1,0:T(8,128)(2,1)S(1)}, bf16[48,512]{1,0:T(8,128)(2,1)S(1)}, u32[]{:S(2)}, u32[]{:S(2)}) collective-permute-start(bf16[48,512]{1,0:T(8,128)(2,1)S(1)} %maximum_select_fusion.1), channel_id=1, source_target_pairs={{0,16},{16,0},{32,48},{48,32},{64,80},{80,64},{96,112},{112,96},{1... | collective-permute-start | bytes 147464 | tf_op jit(solution)/shard_map/ppermute | solution.py:27
  (109 shorter events, 19.6 us)
Async XLA Ops:
  0.6 12.3 %copy-start = (bf16[1,1,512,512]{3,2,1,0:T(8,128)(2,1)S(1)}, bf16[1,1,512,512]{3,2,1,0:T(8,128)(2,1)}, u32[]{:S(2)}) copy-start(bf16[1,1,512,512]{3,2,1,0:T(8,128)(2,1)} %grads.1) | copy-start | bytes 1572868
  0.6 10.7 %copy-start.3 = (bf16[1,3,16,512]{3,2,1,0:T(8,128)(2,1)S(1)}, bf16[1,3,16,512]{3,2,1,0:T(8,128)(2,1)}, u32[]{:S(2)}) copy-start(bf16[1,3,16,512]{3,2,1,0:T(8,128)(2,1)} %left.1) | copy-start | bytes 147460
  2.7 10.3 %collective-permute-start = (bf16[512,512]{1,0:T(8,128)(2,1)}, bf16[512,512]{1,0:T(8,128)(2,1)S(1)}, u32[]{:S(2)}, u32[]{:S(2)}) collective-permute-start(bf16[512,512]{1,0:T(8,128)(2,1)} %first_payload.1), channel_id=1, source_target_pairs={{0,16},{16,0},{32,48},{48,32},{64,80},{80,64},{96,112},{112,96},{1... | collective-permute-start | bytes 1572872 | tf_op jit(solution)/shard_map/ppermute | solution.py:27
  14.4 26.4 %all-to-all-start = ((bf16[16,64,512]{2,1,0:T(8,128)(2,1)}), bf16[16,64,512]{2,1,0:T(8,128)(2,1)S(1)}, u32[]{:S(2)}, u32[]{:S(2)}) async-start(bf16[16,64,512]{2,1,0:T(8,128)(2,1)} %bitcast_select_fusion), calls=%async_computation | async-start | bytes 2097152 | tf_op jit(solution)/shard_map/all_to_all | solution.py:45
  25.1 15.6 %collective-permute-start.1 = (bf16[3,2,16,512]{3,2,0,1:T(8,128)(2,1)S(1)}, bf16[3,2,16,512]{3,2,0,1:T(8,128)(2,1)S(1)}, u32[]{:S(2)}, u32[]{:S(2)}) collective-permute-start(bf16[3,2,16,512]{3,2,0,1:T(8,128)(2,1)S(1)} %pad_maximum_fusion.3), channel_id=1, source_target_pairs={{0,1},{1,0},{2,3},{3,2},{4,5},{5,4},{6,7},{7,6},{8,9},{9,8},{10,11... | collective-permute-start | bytes 294920 | tf_op jit(solution)/shard_map/ppermute | solution.py:56
  42.1 38.1 %all-to-all-start.1 = ((bf16[16,32,640]{2,1,0:T(8,128)(2,1)}), bf16[16,32,640]{2,1,0:T(8,128)(2,1)S(1)}, u32[]{:S(2)}, u32[]{:S(2)}) async-start(bf16[16,32,640]{2,1,0:T(8,128)(2,1)} %pad_maximum_fusion.2), calls=%async_computation.1 | async-start | bytes 1310720 | tf_op jit(solution)/shard_map/all_to_all | solution.py:37
  48.8 20.4 %collective-permute-start.2 = (bf16[2,16,512]{2,1,0:T(8,128)(2,1)S(1)}, bf16[2,16,512]{2,1,0:T(8,128)(2,1)S(1)}, u32[]{:S(2)}, u32[]{:S(2)}) collective-permute-start(bf16[2,16,512]{2,1,0:T(8,128)(2,1)S(1)} %get-tuple-element.39), channel_id=1, source_target_pairs={{0,14},{1,15},{2,0},{3,1},{4,2},{5,3},{6,4},{7,5},{8,6},{9,7},{10,... | collective-permute-start | bytes 98312 | tf_op jit(solution)/shard_map/ppermute | solution.py:50
  55.0 19.3 %collective-permute-start.3 = (bf16[2,16,512]{2,1,0:T(8,128)(2,1)S(1)}, bf16[2,16,512]{2,1,0:T(8,128)(2,1)S(1)}, u32[]{:S(2)}, u32[]{:S(2)}) collective-permute-start(bf16[2,16,512]{2,1,0:T(8,128)(2,1)S(1)} %get-tuple-element.38), channel_id=1, source_target_pairs={{0,12},{1,13},{2,14},{3,15},{4,0},{5,1},{6,2},{7,3},{8,4},{9,5},{1... | collective-permute-start | bytes 98312 | tf_op jit(solution)/shard_map/ppermute | solution.py:50
  59.7 20.0 %collective-permute-start.4 = (bf16[2,16,512]{2,1,0:T(8,128)(2,1)S(1)}, bf16[2,16,512]{2,1,0:T(8,128)(2,1)S(1)}, u32[]{:S(2)}, u32[]{:S(2)}) collective-permute-start(bf16[2,16,512]{2,1,0:T(8,128)(2,1)S(1)} %get-tuple-element.37), channel_id=1, source_target_pairs={{0,10},{1,11},{2,12},{3,13},{4,14},{5,15},{6,0},{7,1},{8,2},{9,3},... | collective-permute-start | bytes 98312 | tf_op jit(solution)/shard_map/ppermute | solution.py:50
  62.0 17.7 %collective-permute-start.5 = (bf16[2,16,512]{2,1,0:T(8,128)(2,1)S(1)}, bf16[2,16,512]{2,1,0:T(8,128)(2,1)S(1)}, u32[]{:S(2)}, u32[]{:S(2)}) collective-permute-start(bf16[2,16,512]{2,1,0:T(8,128)(2,1)S(1)} %get-tuple-element.36), channel_id=1, source_target_pairs={{0,8},{1,9},{2,10},{3,11},{4,12},{5,13},{6,14},{7,15},{8,0},{9,1},... | collective-permute-start | bytes 98312 | tf_op jit(solution)/shard_map/ppermute | solution.py:50
  67.2 12.5 %collective-permute-start.6 = (bf16[2,16,512]{2,1,0:T(8,128)(2,1)S(1)}, bf16[2,16,512]{2,1,0:T(8,128)(2,1)S(1)}, u32[]{:S(2)}, u32[]{:S(2)}) collective-permute-start(bf16[2,16,512]{2,1,0:T(8,128)(2,1)S(1)} %get-tuple-element.35), channel_id=1, source_target_pairs={{0,6},{1,7},{2,8},{3,9},{4,10},{5,11},{6,12},{7,13},{8,14},{9,15},... | collective-permute-start | bytes 98312 | tf_op jit(solution)/shard_map/ppermute | solution.py:50
  69.1 10.6 %collective-permute-start.7 = (bf16[2,16,512]{2,1,0:T(8,128)(2,1)S(1)}, bf16[2,16,512]{2,1,0:T(8,128)(2,1)S(1)}, u32[]{:S(2)}, u32[]{:S(2)}) collective-permute-start(bf16[2,16,512]{2,1,0:T(8,128)(2,1)S(1)} %get-tuple-element.34), channel_id=1, source_target_pairs={{0,4},{1,5},{2,6},{3,7},{4,8},{5,9},{6,10},{7,11},{8,12},{9,13},{1... | collective-permute-start | bytes 98312 | tf_op jit(solution)/shard_map/ppermute | solution.py:50
  74.3 5.9 %collective-permute-start.8 = (bf16[2,16,512]{2,1,0:T(8,128)(2,1)S(1)}, bf16[2,16,512]{2,1,0:T(8,128)(2,1)S(1)}, u32[]{:S(2)}, u32[]{:S(2)}) collective-permute-start(bf16[2,16,512]{2,1,0:T(8,128)(2,1)S(1)} %get-tuple-element.33), channel_id=1, source_target_pairs={{0,2},{1,3},{2,4},{3,5},{4,6},{5,7},{6,8},{7,9},{8,10},{9,11},{10,... | collective-permute-start | bytes 98312 | tf_op jit(solution)/shard_map/ppermute | solution.py:50
  80.3 7.0 %collective-permute-start.9 = (bf16[576,640]{1,0:T(8,128)(2,1)S(1)}, bf16[576,640]{1,0:T(8,128)(2,1)S(1)}, u32[]{:S(2)}, u32[]{:S(2)}) collective-permute-start(bf16[576,640]{1,0:T(8,128)(2,1)S(1)} %fusion.3), channel_id=1, source_target_pairs={{0,16},{16,0},{32,48},{48,32},{64,80},{80,64},{96,112},{112,96},{1... | collective-permute-start | bytes 2211848 | tf_op jit(solution)/shard_map/ppermute | solution.py:27
  87.9 6.2 %collective-permute-start.10 = (bf16[2,16,512]{2,1,0:T(8,128)(2,1)S(1)}, bf16[2,16,512]{2,1,0:T(8,128)(2,1)S(1)}, u32[]{:S(2)}, u32[]{:S(2)}) collective-permute-start(bf16[2,16,512]{2,1,0:T(8,128)(2,1)S(1)} %get-tuple-element.72), channel_id=1, source_target_pairs={{0,1},{1,0},{2,3},{3,2},{4,5},{5,4},{6,7},{7,6},{8,9},{9,8},{10,11... | collective-permute-start | bytes 98312 | tf_op jit(solution)/shard_map/ppermute | solution.py:56
  94.9 25.5 %collective-permute-start.18 = (bf16[2,2,16,512]{3,2,1,0:T(8,128)(2,1)S(1)}, bf16[2,2,16,512]{3,2,1,0:T(8,128)(2,1)S(1)}, u32[]{:S(2)}, u32[]{:S(2)}) collective-permute-start(bf16[2,2,16,512]{3,2,1,0:T(8,128)(2,1)S(1)} %maximum_select_fusion), channel_id=1, source_target_pairs={{0,2},{1,3},{2,4},{3,5},{4,6},{5,7},{6,8},{7,9},{8,10},{9,11},{10,... | collective-permute-start | bytes 196616 | tf_op jit(solution)/shard_map/ppermute | solution.py:50
  97.4 28.5 %collective-permute-start.17 = (bf16[2,2,16,512]{3,2,1,0:T(8,128)(2,1)S(1)}, bf16[2,2,16,512]{3,2,1,0:T(8,128)(2,1)S(1)}, u32[]{:S(2)}, u32[]{:S(2)}) collective-permute-start(bf16[2,2,16,512]{3,2,1,0:T(8,128)(2,1)S(1)} %maximum_select_fusion), channel_id=1, source_target_pairs={{0,4},{1,5},{2,6},{3,7},{4,8},{5,9},{6,10},{7,11},{8,12},{9,13},{1... | collective-permute-start | bytes 196616 | tf_op jit(solution)/shard_map/ppermute | solution.py:50
  101.1 27.9 %collective-permute-start.16 = (bf16[2,2,16,512]{3,2,1,0:T(8,128)(2,1)S(1)}, bf16[2,2,16,512]{3,2,1,0:T(8,128)(2,1)S(1)}, u32[]{:S(2)}, u32[]{:S(2)}) collective-permute-start(bf16[2,2,16,512]{3,2,1,0:T(8,128)(2,1)S(1)} %maximum_select_fusion), channel_id=1, source_target_pairs={{0,6},{1,7},{2,8},{3,9},{4,10},{5,11},{6,12},{7,13},{8,14},{9,15},... | collective-permute-start | bytes 196616 | tf_op jit(solution)/shard_map/ppermute | solution.py:50
  104.7 24.3 %collective-permute-start.15 = (bf16[2,2,16,512]{3,2,1,0:T(8,128)(2,1)S(1)}, bf16[2,2,16,512]{3,2,1,0:T(8,128)(2,1)S(1)}, u32[]{:S(2)}, u32[]{:S(2)}) collective-permute-start(bf16[2,2,16,512]{3,2,1,0:T(8,128)(2,1)S(1)} %maximum_select_fusion), channel_id=1, source_target_pairs={{0,8},{1,9},{2,10},{3,11},{4,12},{5,13},{6,14},{7,15},{8,0},{9,1},... | collective-permute-start | bytes 196616 | tf_op jit(solution)/shard_map/ppermute | solution.py:50
  109.5 19.5 %collective-permute-start.14 = (bf16[2,2,16,512]{3,2,1,0:T(8,128)(2,1)S(1)}, bf16[2,2,16,512]{3,2,1,0:T(8,128)(2,1)S(1)}, u32[]{:S(2)}, u32[]{:S(2)}) collective-permute-start(bf16[2,2,16,512]{3,2,1,0:T(8,128)(2,1)S(1)} %maximum_select_fusion), channel_id=1, source_target_pairs={{0,10},{1,11},{2,12},{3,13},{4,14},{5,15},{6,0},{7,1},{8,2},{9,3},... | collective-permute-start | bytes 196616 | tf_op jit(solution)/shard_map/ppermute | solution.py:50
  113.0 21.1 %all-to-all-start.2 = ((bf16[16,32,512]{2,1,0:T(8,128)(2,1)}), bf16[16,32,512]{2,1,0:T(8,128)(2,1)S(1)}, u32[]{:S(2)}, u32[]{:S(2)}) async-start(bf16[16,32,512]{2,1,0:T(8,128)(2,1)} %broadcast_in_dim.444), calls=%async_computation.2 | async-start | bytes 1048576 | tf_op jit(solution)/shard_map/all_to_all | solution.py:45
  120.4 11.1 %collective-permute-start.13 = (bf16[2,2,16,512]{3,2,1,0:T(8,128)(2,1)S(1)}, bf16[2,2,16,512]{3,2,1,0:T(8,128)(2,1)S(1)}, u32[]{:S(2)}, u32[]{:S(2)}) collective-permute-start(bf16[2,2,16,512]{3,2,1,0:T(8,128)(2,1)S(1)} %maximum_select_fusion), channel_id=1, source_target_pairs={{0,12},{1,13},{2,14},{3,15},{4,0},{5,1},{6,2},{7,3},{8,4},{9,5},{1... | collective-permute-start | bytes 196616 | tf_op jit(solution)/shard_map/ppermute | solution.py:50
  125.9 6.6 %collective-permute-start.12 = (bf16[2,2,16,512]{3,2,1,0:T(8,128)(2,1)S(1)}, bf16[2,2,16,512]{3,2,1,0:T(8,128)(2,1)S(1)}, u32[]{:S(2)}, u32[]{:S(2)}) collective-permute-start(bf16[2,2,16,512]{3,2,1,0:T(8,128)(2,1)S(1)} %maximum_select_fusion), channel_id=1, source_target_pairs={{0,14},{1,15},{2,0},{3,1},{4,2},{5,3},{6,4},{7,5},{8,6},{9,7},{10,... | collective-permute-start | bytes 196616 | tf_op jit(solution)/shard_map/ppermute | solution.py:50
  134.8 5.5 %collective-permute-start.11 = (bf16[48,512]{1,0:T(8,128)(2,1)S(1)}, bf16[48,512]{1,0:T(8,128)(2,1)S(1)}, u32[]{:S(2)}, u32[]{:S(2)}) collective-permute-start(bf16[48,512]{1,0:T(8,128)(2,1)S(1)} %maximum_select_fusion.1), channel_id=1, source_target_pairs={{0,16},{16,0},{32,48},{48,32},{64,80},{80,64},{96,112},{112,96},{1... | collective-permute-start | bytes 147464 | tf_op jit(solution)/shard_map/ppermute | solution.py:27
  (6 other events, 52.9 us)

commit v6 on v5

--- a/solution.py
+++ b/solution.py
@@ -45,19 +45,20 @@
     return lax.all_to_all(pieces, ("dp", "owner"), 0, 0, axis_index_groups=groups)
 
 
-def shift_z(value, step):
-    owners = lax.axis_size("owner")
-    return lax.ppermute(
-        value, "owner", [(i, (i + 2 * step) % owners) for i in range(owners)]
-    )
-
-
-def swap_owners(value):
-    return lax.ppermute(value, "owner", [(i, i ^ 1) for i in range(lax.axis_size("owner"))])
-
-
-def z_order(value, z):
-    return lax.dynamic_slice_in_dim(jnp.concatenate([value, value], 0), z, value.shape[0], 0)
+def swap_owners(value, bit):
+    return lax.ppermute(value, "owner", [(i, i ^ bit) for i in range(lax.axis_size("owner"))])
+
+
+def halve(held, owner_z, z, step):
+    bit = (z >> step) % 2
+    pick = lambda value, index: lax.index_in_dim(value, index, 0, keepdims=False)
+    keep = jnp.where(bit == 0, pick(held, 0), pick(held, 1))
+    send = jnp.where(bit == 0, pick(held, 1), pick(held, 0))
+    owner_z = jnp.where(bit == 0, pick(owner_z, 0), pick(owner_z, 1))
+    came = swap_owners(send, 2 << step)
+    mask = ((owner_z >> step) % 2) == bit
+    mask = mask.reshape(mask.shape + (1,) * (keep.ndim - mask.ndim))
+    return jnp.where(mask, keep, came), owner_z
 
 
 def first_payload_kernel(core, grads, left, right, payload, sems):
@@ -152,21 +153,21 @@
 
     states = jnp.stack([moment[0], second[0]], 1).astype(half)
     states, came = lax.optimization_barrier((states, came))
-    beside = swap_owners(states)
+    beside = swap_owners(states, 1)
     owner_x = owner % 2
     from_owner = lax.dynamic_index_in_dim(assign.reshape(z_num, 2), owner_x, 1, keepdims=False)
     number = lax.dynamic_index_in_dim(numbers.reshape(z_num, 2), owner_x, 1, keepdims=False)
-    code = number + slot_cap * (from_owner % 2 != owner_x)
-    code = z_order(code, z)[:, None, None, None]
+    code = (number + slot_cap * (from_owner % 2 != owner_x))[:, None, None, None]
     states = jnp.concatenate([states, beside], 0)
     picked = states[0][None]
     for slot in range(1, 2 * slot_cap):
         picked = jnp.where(code == slot, states[slot][None], picked)
-    picked, home = lax.optimization_barrier((picked, home))
-    states = picked[0]
-    distance = (z - assign[owner] // 2) % z_num
-    for step in range(1, z_num):
-        states = jnp.where(distance == step, shift_z(picked[step], step), states)
+    states = picked.reshape((2, 2, 2) + picked.shape[1:]).transpose(2, 1, 0, 3, 4, 5)
+    owner_z = (from_owner // 2).reshape(2, 2, 2).transpose(2, 1, 0)
+    states, owner_z = halve(states, owner_z, z, 0)
+    states, home = lax.optimization_barrier((states, home))
+    states, owner_z = halve(states, owner_z, z, 1)
+    states, owner_z = halve(states, owner_z, z, 2)
 
     left_rows, right_rows = home.reshape(kinds, chip_rows, col_num)
     left_chunks = left_rows.reshape(chip_rows, chunk_num, LANES).transpose(1, 0, 2)
@@ -189,60 +190,45 @@
     right_full = jnp.where(first, other[:, :col_num], core_full)
     left_cols = jnp.where(first, other[:, col_num:], mine[:, col_num:])
 
-    chunk = row_index // (dp_num // chunk_num)
-    in_chunk = (row_index % (dp_num // chunk_num)) * row_num
-    grad_cols = lax.dynamic_slice_in_dim(grad_full, chunk * LANES, LANES, 1)
-    grad_rows = lax.dynamic_slice_in_dim(grad_full, row_index * row_num, row_num, 0)
-    left_term = dot(grad_rows, grad_full, (1, 1)).astype(half)
-    right_term = dot(grad_cols, grad_full, (0, 0)).astype(half)
-    right_term = lax.dynamic_slice_in_dim(right_term, in_chunk, row_num, 0)
-    grams = jnp.stack([left_term, right_term])
-    beside = swap_owners(grams)
-    grams = jnp.where(
-        owner_x == 0, jnp.stack([grams, beside], 0), jnp.stack([beside, grams], 0)
-    )
-
+    chunk = chip // (chips // chunk_num)
     in_chunk = (chip % (chips // chunk_num)) * chip_rows
-    turned = dot(left_cols, grad_full, (0, 0)).astype(half)
-    turned = lax.dynamic_slice_in_dim(turned, in_chunk, chip_rows, 0)
+    own_rows = lambda value: lax.dynamic_slice_in_dim(value, in_chunk, chip_rows, 0)
+    turned = own_rows(dot(left_cols, grad_full, (0, 0)).astype(half))
     rotated = dot(turned, right_full, (1, 0))
     home_moment = beta_one * states[0] + (1.0 - beta_one) * rotated
     home_second = beta_two * states[1] + (1.0 - beta_two) * rotated * rotated
     direction = (home_moment / bias_one / (jnp.sqrt(home_second / bias_two) + adam_eps)).astype(half)
     back_rows = dot(direction, right_full, (1, 1)).astype(half)
-
-    results = copies(jnp.where(first, back_rows, rotated.astype(half)), chips)
-    results, grams = lax.optimization_barrier((results, grams))
-    gathered = exchange(results)
-
+    grad_cols = lax.dynamic_slice_in_dim(grad_full, chunk * LANES, LANES, 1)
+    grad_rows = lax.dynamic_slice_in_dim(grad_full, chip * chip_rows, chip_rows, 0)
+    left_term = dot(grad_rows, grad_full, (1, 1)).astype(half)
+    right_term = own_rows(dot(grad_cols, grad_full, (0, 0)).astype(half))
+
+    results = jnp.concatenate(
+        [jnp.where(first, back_rows, left_term), right_term, rotated.astype(half)], 0
+    )
+    gathered = exchange(copies(results, chips))
+    back_full = gathered[:, :chip_rows].reshape(col_num, col_num)
+    chip_update = dot(left_rows, back_full, (1, 0)).astype(half)
     held = (assign == owner)[None, :] & (
         numbers[None, :] == jnp.arange(slot_cap, dtype=jnp.int32)[:, None]
     )
-    held_z = held.reshape(slot_cap, z_num, 2)
-    behind = lax.dynamic_slice_in_dim(
-        jnp.concatenate([held_z[:, ::-1], held_z[:, ::-1]], 1), z_num - 1 - z, z_num, 1
-    )
-    all_grams = [grams] + [shift_z(grams, step) for step in range(1, z_num)]
-    slot_grams = jnp.zeros((slot_cap,) + grams.shape[1:], half)
-    for step, values in enumerate(all_grams):
-        for x in range(2):
-            mask = behind[:, step, x][:, None, None, None]
-            slot_grams = jnp.where(mask, values[x][None], slot_grams)
-    slot_grams = slot_grams.astype(jnp.float32)
-
-    back_full = gathered.reshape(col_num, col_num)
-    chip_update = dot(left_rows, back_full, (1, 0)).astype(half)
-    turns = jnp.where(held[:, :, None, None], gathered[None].astype(jnp.float32), 0.0)
-    turns = jnp.sum(turns, axis=1).astype(half).reshape(slot_cap, 2, row_num, col_num)
-    for_second = jnp.concatenate([chip_update[row_num:], turns[1:, 0].reshape(-1, col_num)], 0)
-    came = swap_cores(jnp.where(first, for_second, turns[:, 0].reshape(-1, col_num)))
+    chip_results = jnp.sum(
+        jnp.where(held[:, :, None, None], gathered[None].astype(jnp.float32), 0.0), axis=1
+    ).astype(half)
+    chip_results = chip_results.reshape(slot_cap, 3, 2, row_num, col_num)
+    for_first = chip_results[:, :, 0].reshape(-1, col_num)
+    for_second = jnp.concatenate([chip_update[row_num:], for_first[row_num:]], 0)
+    came = swap_cores(jnp.where(first, for_second, for_first))
     update = jnp.where(first, chip_update[:row_num], came[:row_num])
-    turns = jnp.where(first, came.reshape(turns[:, 0].shape), turns[:, 1]).astype(jnp.float32)
-
-    new_left = beta_two * left_stat[0] + (1.0 - beta_two) * slot_grams[:, 0]
-    new_right = beta_two * right_stat[0] + (1.0 - beta_two) * slot_grams[:, 1]
-    new_moment = beta_one * moment[0] + (1.0 - beta_one) * turns
-    new_second = beta_two * second[0] + (1.0 - beta_two) * turns * turns
+    terms = jnp.where(
+        first, came.reshape(slot_cap, 3, row_num, col_num), chip_results[:, :, 1]
+    ).astype(jnp.float32)
+
+    new_left = beta_two * left_stat[0] + (1.0 - beta_two) * terms[:, 0]
+    new_right = beta_two * right_stat[0] + (1.0 - beta_two) * terms[:, 1]
+    new_moment = beta_one * moment[0] + (1.0 - beta_one) * terms[:, 2]
+    new_second = beta_two * second[0] + (1.0 - beta_two) * terms[:, 2] * terms[:, 2]
     return (update[None], new_left[None], new_right[None], new_moment[None], new_second[None])
 
 

time: 143 us -> 127 us (0.89)
  starting transfers between devices: 103 us -> 60.7 us
  waiting for transfers between devices: 20.8 us -> 45.4 us
  other arithmetic: 6.01 us -> 7.8 us
    ppermute x16 -> x4, starting transfers between devices: 63.3 us -> 21.2 us  [swap_owners(): lax.ppermute(value, 'owner', [(i, i ^ bit) for i in range(lax.axis_size('...]
    all_to_all x2, waiting for transfers between devices: 1.51 us -> 26 us  [exchange(): lax.all_to_all(pieces, ('dp', 'owner'), 0, 0, axis_index_groups=groups)]
    ppermute x3, starting transfers between devices: 18.3 us -> 15.2 us  [swap_cores(): lax.ppermute(value, 'dp', [(i, i ^ 1) for i in range(lax.axis_size('dp'))])]
    all_to_all x2, starting transfers between devices: 14.8 us -> 17.2 us  [exchange(): lax.all_to_all(pieces, ('dp', 'owner'), 0, 0, axis_index_groups=groups)]
    ppermute x16 -> x4, waiting for transfers between devices: 16.9 us -> 15.3 us  [swap_owners(): lax.ppermute(value, 'owner', [(i, i ^ bit) for i in range(lax.axis_size('...]
  transfers between devices with their start and end apart: 22 -> 10, of which waited for: 9 -> 7; matrix products, arithmetic and copies ran while one was open for 3% -> 4% of each run, Pallas kernels for 0% -> 0%
where the time goes in v6:
time: 127 us; the launch traced here: 126 us
  starting transfers between devices  60.7 us (48%)
  waiting for transfers between devices  45.4 us (36%)
  other arithmetic  7.8 us (6%)
  between operations  4.55 us (4%)
  local copies, waits for them, and re-layouts  4.28 us (3%)
  Pallas kernels  1.96 us (2%)
  matrix products  1.43 us (1%)
    all_to_all x2, waiting for transfers between devices, exchange(): lax.all_to_all(pieces, ('dp', 'owner'), 0, 0, axis_index_groups=groups)  26 us
    ppermute x4, starting transfers between devices, swap_owners(): lax.ppermute(value, 'owner', [(i, i ^ bit) for i in range(lax.axis_size('...  21.2 us
    all_to_all x2, starting transfers between devices, exchange(): lax.all_to_all(pieces, ('dp', 'owner'), 0, 0, axis_index_groups=groups)  17.2 us
    ppermute x4, waiting for transfers between devices, swap_owners(): lax.ppermute(value, 'owner', [(i, i ^ bit) for i in range(lax.axis_size('...  15.3 us
    ppermute x3, starting transfers between devices, swap_cores(): lax.ppermute(value, 'dp', [(i, i ^ 1) for i in range(lax.axis_size('dp'))])  15.2 us
    all_to_all x1, starting transfers between devices, exchange_dp(): return lax.all_to_all(pieces, 'dp', 0, 0, axis_index_groups=groups)  7.07 us
    ppermute x3, waiting for transfers between devices, swap_cores(): lax.ppermute(value, 'dp', [(i, i ^ 1) for i in range(lax.axis_size('dp'))])  3.1 us
  transfers between devices with their start and end apart: 10, of which 7 were waited for; matrix products, arithmetic and copies ran while one was open for 4% of the time, Pallas kernels for 0%

profile of v6, /device:TPU:1, one launch (start us, length us, event | category | flops | bytes accessed | tf_op | source)
XLA Modules:
  0.0 126.1 jit_solution(7725303515404080409)
XLA Ops:
  0.7 2.0 %first_payload.1 = bf16[512,512]{1,0:T(8,128)(2,1)} custom-call(s32[1]{0:T(128)} %bitcast.1.core, bf16[1,1,512,512]{3,2,1,0:T(8,128)(2,1)} %grads.1, bf16[1,3,16,512]{3,2,1,0:T(8,128)(2,1)} %left.1, bf16[1,3,16,512]{3,2,1,0:T(8,128)(2,1)} %right.1), custom_call_target="tpu_custom_call" | custom-call | tf_op jit(solution)/shard_map/first_payload/pallas_call | solution.py:94
  2.6 8.5 %collective-permute-start = (bf16[512,512]{1,0:T(8,128)(2,1)}, bf16[512,512]{1,0:T(8,128)(2,1)S(1)}, u32[]{:S(2)}, u32[]{:S(2)}) collective-permute-start(bf16[512,512]{1,0:T(8,128)(2,1)} %first_payload.1), channel_id=1, source_target_pairs={{0,16},{16,0},{32,48},{48,32},{64,80},{80,64},{96,112},{112,96},{1... | collective-permute-start | bytes 1572872 | tf_op jit(solution)/shard_map/ppermute | solution.py:27
  12.3 0.8 maximum_bitcast_fusion
  13.2 0.9 convert_reduce_fusion
  14.3 1.3 %bitcast_select_fusion = bf16[16,64,512]{2,1,0:T(8,128)(2,1)} fusion(bf16[16,2,32,512]{3,2,1,0:T(8,128)(2,1)S(1)} %pad_maximum_fusion, pred[16]{0:T(512)(128)(4,1)S(1)} %get-tuple-element.39, pred[16]{0:T(512)(128)(4,1)S(1)} %get-tuple-element.38, pred[]{:T(512)S(6)} %eq.148, bf16[64,512]{1,0:T(8,128)(2,1)S(1)} %bitcast.158, ...), kind=kLoop, calls=%fused_computation.6 | loop fusion | flops 1572864 | bytes 2293793 | tf_op jit(solution)/shard_map/jit(_where)/select_n | solution.py:148
  15.6 7.4 %all-to-all-start = ((bf16[16,64,512]{2,1,0:T(8,128)(2,1)}), bf16[16,64,512]{2,1,0:T(8,128)(2,1)S(1)}, u32[]{:S(2)}, u32[]{:S(2)}) async-start(bf16[16,64,512]{2,1,0:T(8,128)(2,1)} %bitcast_select_fusion), calls=%async_computation | async-start | bytes 2097152 | tf_op jit(solution)/shard_map/all_to_all | solution.py:45
  26.1 4.8 %collective-permute-start.1 = (bf16[3,2,16,512]{3,2,0,1:T(8,128)(2,1)S(1)}, bf16[3,2,16,512]{3,2,0,1:T(8,128)(2,1)S(1)}, u32[]{:S(2)}, u32[]{:S(2)}) collective-permute-start(bf16[3,2,16,512]{3,2,0,1:T(8,128)(2,1)S(1)} %pad_maximum_fusion.3), channel_id=1, source_target_pairs={{0,1},{1,0},{2,3},{3,2},{4,5},{5,4},{6,7},{7,6},{8,9},{9,8},{10,11... | collective-permute-start | bytes 294920 | tf_op jit(solution)/shard_map/ppermute | solution.py:49
  30.9 10.8 %collective-permute-done.1 = bf16[3,2,16,512]{3,2,0,1:T(8,128)(2,1)S(1)} collective-permute-done((bf16[3,2,16,512]{3,2,0,1:T(8,128)(2,1)S(1)}, bf16[3,2,16,512]{3,2,0,1:T(8,128)(2,1)S(1)}, u32[]{:S(2)}, u32[]{:S(2)}) %collective-permute-start.1) | collective-permute-done | bytes 98336 | tf_op jit(solution)/shard_map/ppermute | solution.py:49
  41.9 3.0 %collective-permute-start.2 = (bf16[2,2,2,16,512]{4,3,2,1,0:T(8,128)(2,1)S(1)}, bf16[2,2,2,16,512]{4,3,2,1,0:T(8,128)(2,1)S(1)}, u32[]{:S(2)}, u32[]{:S(2)}) collective-permute-start(bf16[2,2,2,16,512]{4,3,2,1,0:T(8,128)(2,1)S(1)} %select_bitcast_fusion), channel_id=1, source_target_pairs={{0,2},{1,3},{2,0},{3,1},{4,6},{5,7},{6,4},{7,5},{8,10},{9,11},{10,... | collective-permute-start | bytes 393224 | tf_op jit(solution)/shard_map/ppermute | solution.py:49
  44.9 2.7 %collective-permute-done.2 = bf16[2,2,2,16,512]{4,3,2,1,0:T(8,128)(2,1)S(1)} collective-permute-done((bf16[2,2,2,16,512]{4,3,2,1,0:T(8,128)(2,1)S(1)}, bf16[2,2,2,16,512]{4,3,2,1,0:T(8,128)(2,1)S(1)}, u32[]{:S(2)}, u32[]{:S(2)}) %collective-permute-start.2) | collective-permute-done | bytes 131104 | tf_op jit(solution)/shard_map/ppermute | solution.py:49
  48.0 0.9 pad_maximum_fusion.2
  48.9 7.1 %all-to-all-start.1 = ((bf16[16,32,640]{2,1,0:T(8,128)(2,1)}), bf16[16,32,640]{2,1,0:T(8,128)(2,1)S(1)}, u32[]{:S(2)}, u32[]{:S(2)}) async-start(bf16[16,32,640]{2,1,0:T(8,128)(2,1)} %pad_maximum_fusion.2), calls=%async_computation.1 | async-start | bytes 1310720 | tf_op jit(solution)/shard_map/all_to_all | solution.py:37
  56.0 5.5 %collective-permute-start.3 = (bf16[2,2,16,512]{3,2,1,0:T(8,128)(2,1)S(1)}, bf16[2,2,16,512]{3,2,1,0:T(8,128)(2,1)S(1)}, u32[]{:S(2)}, u32[]{:S(2)}) collective-permute-start(bf16[2,2,16,512]{3,2,1,0:T(8,128)(2,1)S(1)} %select_bitcast_fusion.1), channel_id=1, source_target_pairs={{0,4},{1,5},{2,6},{3,7},{4,0},{5,1},{6,2},{7,3},{8,12},{9,13},{10,... | collective-permute-start | bytes 196616 | tf_op jit(solution)/shard_map/ppermute | solution.py:49
  61.6 1.9 %collective-permute-done.3 = bf16[2,2,16,512]{3,2,1,0:T(8,128)(2,1)S(1)} collective-permute-done((bf16[2,2,16,512]{3,2,1,0:T(8,128)(2,1)S(1)}, bf16[2,2,16,512]{3,2,1,0:T(8,128)(2,1)S(1)}, u32[]{:S(2)}, u32[]{:S(2)}) %collective-permute-start.3) | collective-permute-done | bytes 65568 | tf_op jit(solution)/shard_map/ppermute | solution.py:49
  63.6 7.9 %collective-permute-start.4 = (bf16[2,16,512]{2,1,0:T(8,128)(2,1)S(1)}, bf16[2,16,512]{2,1,0:T(8,128)(2,1)S(1)}, u32[]{:S(2)}, u32[]{:S(2)}) collective-permute-start(bf16[2,16,512]{2,1,0:T(8,128)(2,1)S(1)} %select_bitcast_fusion.2), channel_id=1, source_target_pairs={{0,8},{1,9},{2,10},{3,11},{4,12},{5,13},{6,14},{7,15},{8,0},{9,1},... | collective-permute-start | bytes 98312 | tf_op jit(solution)/shard_map/ppermute | solution.py:49
  73.4 0.9 all-to-all-done.1
  74.4 4.8 %collective-permute-start.5 = (bf16[576,640]{1,0:T(8,128)(2,1)S(1)}, bf16[576,640]{1,0:T(8,128)(2,1)S(1)}, u32[]{:S(2)}, u32[]{:S(2)}) collective-permute-start(bf16[576,640]{1,0:T(8,128)(2,1)S(1)} %fusion.2), channel_id=1, source_target_pairs={{0,16},{16,0},{32,48},{48,32},{64,80},{80,64},{96,112},{112,96},{1... | collective-permute-start | bytes 2211848 | tf_op jit(solution)/shard_map/ppermute | solution.py:27
  79.3 1.8 %collective-permute-done.5 = bf16[576,640]{1,0:T(8,128)(2,1)S(1)} collective-permute-done((bf16[576,640]{1,0:T(8,128)(2,1)S(1)}, bf16[576,640]{1,0:T(8,128)(2,1)S(1)}, u32[]{:S(2)}, u32[]{:S(2)}) %collective-permute-start.5) | collective-permute-done | bytes 737312 | tf_op jit(solution)/shard_map/ppermute | solution.py:27
  82.4 1.3 %broadcast_in_dim.253 = bf16[16,96,512]{2,1,0:T(8,128)(2,1)} broadcast(bf16[96,512]{1,0:T(8,128)(2,1)S(1)} %pad_maximum_fusion.4), dimensions={1,2} | broadcast | bytes 1671168 | tf_op jit(solution)/shard_map/broadcast_in_dim | solution.py:106
  83.7 9.8 %all-to-all-start.2 = ((bf16[16,96,512]{2,1,0:T(8,128)(2,1)}), bf16[16,96,512]{2,1,0:T(8,128)(2,1)S(1)}, u32[]{:S(2)}, u32[]{:S(2)}) async-start(bf16[16,96,512]{2,1,0:T(8,128)(2,1)} %broadcast_in_dim.253), calls=%async_computation.2 | async-start | bytes 3145728 | tf_op jit(solution)/shard_map/all_to_all | solution.py:45
  93.6 26.0 %all-to-all-done.2 = bf16[16,96,512]{2,1,0:T(8,128)(2,1)S(1)} async-done(((bf16[16,96,512]{2,1,0:T(8,128)(2,1)}), bf16[16,96,512]{2,1,0:T(8,128)(2,1)S(1)}, u32[]{:S(2)}, u32[]{:S(2)}) %all-to-all-start.2) | async-done | bytes 1572896 | tf_op jit(solution)/shard_map/all_to_all | solution.py:45
  120.3 1.0 select_reduce_fusion
  121.4 1.9 %collective-permute-start.6 = (bf16[144,512]{1,0:T(8,128)(2,1)S(1)}, bf16[144,512]{1,0:T(8,128)(2,1)S(1)}, u32[]{:S(2)}, u32[]{:S(2)}) collective-permute-start(bf16[144,512]{1,0:T(8,128)(2,1)S(1)} %maximum_select_fusion), channel_id=1, source_target_pairs={{0,16},{16,0},{32,48},{48,32},{64,80},{80,64},{96,112},{112,96},{1... | collective-permute-start | bytes 442376 | tf_op jit(solution)/shard_map/ppermute | solution.py:27
  123.3 1.3 %collective-permute-done.6 = bf16[144,512]{1,0:T(8,128)(2,1)S(1)} collective-permute-done((bf16[144,512]{1,0:T(8,128)(2,1)S(1)}, bf16[144,512]{1,0:T(8,128)(2,1)S(1)}, u32[]{:S(2)}, u32[]{:S(2)}) %collective-permute-start.6) | collective-permute-done | bytes 147488 | tf_op jit(solution)/shard_map/ppermute | solution.py:27
  (75 shorter events, 7.2 us)
Async XLA Ops:
  0.6 13.5 %copy-start = (bf16[1,1,512,512]{3,2,1,0:T(8,128)(2,1)S(1)}, bf16[1,1,512,512]{3,2,1,0:T(8,128)(2,1)}, u32[]{:S(2)}) copy-start(bf16[1,1,512,512]{3,2,1,0:T(8,128)(2,1)} %grads.1) | copy-start | bytes 1572868
  0.6 13.4 %copy-start.1 = (f32[1,3,16,512]{3,2,1,0:T(8,128)S(1)}, f32[1,3,16,512]{3,2,1,0:T(8,128)}, u32[]{:S(2)}) copy-start(f32[1,3,16,512]{3,2,1,0:T(8,128)} %param.15) | copy-start | bytes 294916
  0.7 13.4 %copy-start.2 = (f32[1,3,16,512]{3,2,1,0:T(8,128)S(1)}, f32[1,3,16,512]{3,2,1,0:T(8,128)}, u32[]{:S(2)}) copy-start(f32[1,3,16,512]{3,2,1,0:T(8,128)} %param.14) | copy-start | bytes 294916
  2.6 11.5 %collective-permute-start = (bf16[512,512]{1,0:T(8,128)(2,1)}, bf16[512,512]{1,0:T(8,128)(2,1)S(1)}, u32[]{:S(2)}, u32[]{:S(2)}) collective-permute-start(bf16[512,512]{1,0:T(8,128)(2,1)} %first_payload.1), channel_id=1, source_target_pairs={{0,16},{16,0},{32,48},{48,32},{64,80},{80,64},{96,112},{112,96},{1... | collective-permute-start | bytes 1572872 | tf_op jit(solution)/shard_map/ppermute | solution.py:27
  15.6 7.4 %copy-start.5 = (s32[16]{0:T(128)S(1)}, s32[16]{0:T(128)}, u32[]{:S(2)}) copy-start(s32[16]{0:T(128)} %param.9) | copy-start | bytes 196
  15.6 32.1 %all-to-all-start = ((bf16[16,64,512]{2,1,0:T(8,128)(2,1)}), bf16[16,64,512]{2,1,0:T(8,128)(2,1)S(1)}, u32[]{:S(2)}, u32[]{:S(2)}) async-start(bf16[16,64,512]{2,1,0:T(8,128)(2,1)} %bitcast_select_fusion), calls=%async_computation | async-start | bytes 2097152 | tf_op jit(solution)/shard_map/all_to_all | solution.py:45
  26.1 15.6 %collective-permute-start.1 = (bf16[3,2,16,512]{3,2,0,1:T(8,128)(2,1)S(1)}, bf16[3,2,16,512]{3,2,0,1:T(8,128)(2,1)S(1)}, u32[]{:S(2)}, u32[]{:S(2)}) collective-permute-start(bf16[3,2,16,512]{3,2,0,1:T(8,128)(2,1)S(1)} %pad_maximum_fusion.3), channel_id=1, source_target_pairs={{0,1},{1,0},{2,3},{3,2},{4,5},{5,4},{6,7},{7,6},{8,9},{9,8},{10,11... | collective-permute-start | bytes 294920 | tf_op jit(solution)/shard_map/ppermute | solution.py:49
  41.9 5.7 %collective-permute-start.2 = (bf16[2,2,2,16,512]{4,3,2,1,0:T(8,128)(2,1)S(1)}, bf16[2,2,2,16,512]{4,3,2,1,0:T(8,128)(2,1)S(1)}, u32[]{:S(2)}, u32[]{:S(2)}) collective-permute-start(bf16[2,2,2,16,512]{4,3,2,1,0:T(8,128)(2,1)S(1)} %select_bitcast_fusion), channel_id=1, source_target_pairs={{0,2},{1,3},{2,0},{3,1},{4,6},{5,7},{6,4},{7,5},{8,10},{9,11},{10,... | collective-permute-start | bytes 393224 | tf_op jit(solution)/shard_map/ppermute | solution.py:49
  48.9 25.4 %all-to-all-start.1 = ((bf16[16,32,640]{2,1,0:T(8,128)(2,1)}), bf16[16,32,640]{2,1,0:T(8,128)(2,1)S(1)}, u32[]{:S(2)}, u32[]{:S(2)}) async-start(bf16[16,32,640]{2,1,0:T(8,128)(2,1)} %pad_maximum_fusion.2), calls=%async_computation.1 | async-start | bytes 1310720 | tf_op jit(solution)/shard_map/all_to_all | solution.py:37
  56.0 7.5 %collective-permute-start.3 = (bf16[2,2,16,512]{3,2,1,0:T(8,128)(2,1)S(1)}, bf16[2,2,16,512]{3,2,1,0:T(8,128)(2,1)S(1)}, u32[]{:S(2)}, u32[]{:S(2)}) collective-permute-start(bf16[2,2,16,512]{3,2,1,0:T(8,128)(2,1)S(1)} %select_bitcast_fusion.1), channel_id=1, source_target_pairs={{0,4},{1,5},{2,6},{3,7},{4,0},{5,1},{6,2},{7,3},{8,12},{9,13},{10,... | collective-permute-start | bytes 196616 | tf_op jit(solution)/shard_map/ppermute | solution.py:49
  63.6 9.8 %collective-permute-start.4 = (bf16[2,16,512]{2,1,0:T(8,128)(2,1)S(1)}, bf16[2,16,512]{2,1,0:T(8,128)(2,1)S(1)}, u32[]{:S(2)}, u32[]{:S(2)}) collective-permute-start(bf16[2,16,512]{2,1,0:T(8,128)(2,1)S(1)} %select_bitcast_fusion.2), channel_id=1, source_target_pairs={{0,8},{1,9},{2,10},{3,11},{4,12},{5,13},{6,14},{7,15},{8,0},{9,1},... | collective-permute-start | bytes 98312 | tf_op jit(solution)/shard_map/ppermute | solution.py:49
  74.4 6.6 %collective-permute-start.5 = (bf16[576,640]{1,0:T(8,128)(2,1)S(1)}, bf16[576,640]{1,0:T(8,128)(2,1)S(1)}, u32[]{:S(2)}, u32[]{:S(2)}) collective-permute-start(bf16[576,640]{1,0:T(8,128)(2,1)S(1)} %fusion.2), channel_id=1, source_target_pairs={{0,16},{16,0},{32,48},{48,32},{64,80},{80,64},{96,112},{112,96},{1... | collective-permute-start | bytes 2211848 | tf_op jit(solution)/shard_map/ppermute | solution.py:27
  83.7 35.9 %all-to-all-start.2 = ((bf16[16,96,512]{2,1,0:T(8,128)(2,1)}), bf16[16,96,512]{2,1,0:T(8,128)(2,1)S(1)}, u32[]{:S(2)}, u32[]{:S(2)}) async-start(bf16[16,96,512]{2,1,0:T(8,128)(2,1)} %broadcast_in_dim.253), calls=%async_computation.2 | async-start | bytes 3145728 | tf_op jit(solution)/shard_map/all_to_all | solution.py:45
  121.3 3.4 %copy-start.3 = (f32[1,3,16,512]{3,2,1,0:T(8,128)S(1)}, f32[1,3,16,512]{3,2,1,0:T(8,128)}, u32[]{:S(2)}) copy-start(f32[1,3,16,512]{3,2,1,0:T(8,128)} %param.12) | copy-start | bytes 294916
  121.3 3.4 %copy-start.4 = (f32[1,3,16,512]{3,2,1,0:T(8,128)S(1)}, f32[1,3,16,512]{3,2,1,0:T(8,128)}, u32[]{:S(2)}) copy-start(f32[1,3,16,512]{3,2,1,0:T(8,128)} %param.13) | copy-start | bytes 294916
  121.4 3.3 %collective-permute-start.6 = (bf16[144,512]{1,0:T(8,128)(2,1)S(1)}, bf16[144,512]{1,0:T(8,128)(2,1)S(1)}, u32[]{:S(2)}, u32[]{:S(2)}) collective-permute-start(bf16[144,512]{1,0:T(8,128)(2,1)S(1)} %maximum_select_fusion), channel_id=1, source_target_pairs={{0,16},{16,0},{32,48},{48,32},{64,80},{80,64},{96,112},{112,96},{1... | collective-permute-start | bytes 442376 | tf_op jit(solution)/shard_map/ppermute | solution.py:27

commit v7 on v4

--- a/solution.py
+++ b/solution.py
@@ -72,7 +72,18 @@
     return lax.ppermute(value, ("dp", "owner"), pairs)
 
 
-def first_payload_kernel(core, grads, left, right, payload, sems):
+def swap_owners_first(value):
+    chips = lax.axis_size("dp") // 2
+    owners = lax.axis_size("owner")
+    pairs = [
+        (place(chip, 0, owner), place(chip, 0, owner ^ 1))
+        for chip in range(chips)
+        for owner in range(owners)
+    ]
+    return lax.ppermute(value, ("dp", "owner"), pairs)
+
+
+def first_payload_kernel(core, grads, left, right, moment, second, payload, wide, sems):
     slot_cap, row_num = left.shape[1:3]
 
     @pl.when(core[0] == 0)
@@ -80,18 +91,28 @@
         moves = []
         for slot in range(slot_cap):
             for kind, basis in enumerate((left, right)):
-                place_of = slot * 2 + kind
                 moves.append(
                     pltpu.make_async_copy(
                         basis.at[0, slot],
-                        payload.at[pl.ds(place_of * row_num, row_num)],
-                        sems.at[place_of],
+                        payload.at[pl.ds((slot * 4 + kind) * row_num, row_num)],
+                        sems.at[slot * 2 + kind],
                     )
                 )
+        for kind, state in enumerate((moment, second)):
+            moves.append(
+                pltpu.make_async_copy(
+                    state.at[0], wide.at[kind], sems.at[2 * slot_cap + kind]
+                )
+            )
         for move in moves:
             move.start()
         for move in moves:
             move.wait()
+        for slot in range(slot_cap):
+            for kind in range(2):
+                payload[pl.ds((slot * 4 + 2 + kind) * row_num, row_num)] = wide[
+                    kind, slot
+                ].astype(half)
 
     @pl.when(core[0] != 0)
     def _():
@@ -100,54 +121,21 @@
         move.wait()
 
 
-def first_payload(core, grads, left, right):
+def first_payload(core, grads, left, right, moment, second):
+    slot_cap, row_num, col_num = left.shape[1:]
     anywhere = pl.BlockSpec(memory_space=pl.ANY)
     return pl.pallas_call(
         first_payload_kernel,
         out_shape=jax.ShapeDtypeStruct(grads.shape[2:], half),
-        in_specs=[pl.BlockSpec(memory_space=pltpu.SMEM)] + [anywhere] * 3,
-        out_specs=anywhere,
-        scratch_shapes=[pltpu.SemaphoreType.DMA((2 * left.shape[1],))],
-        compiler_params=pltpu.CompilerParams(vmem_limit_bytes=60 * 1024 * 1024),
-        name="first_payload",
-    )(core, grads, left, right)
-
-
-def state_pieces_kernel(assign, moment, second, pieces, wide, narrow, sems):
-    moves = [
-        pltpu.make_async_copy(source.at[0], wide.at[kind], sems.at[kind])
-        for kind, source in enumerate((moment, second))
-    ]
-    for move in moves:
-        move.start()
-    for move in moves:
-        move.wait()
-    slot_cap = moment.shape[1]
-    for slot in range(slot_cap):
-        for kind in range(2):
-            narrow[slot, kind] = wide[kind, slot].astype(half)
-    for block in range(assign.shape[0]):
-        number = jnp.int32(0)
-        for earlier in range(block):
-            number += (assign[earlier] == assign[block]).astype(jnp.int32)
-        pieces[block] = narrow[jnp.minimum(number, slot_cap - 1)]
-
-
-def state_pieces(assign, moment, second):
-    slot_cap, row_num, col_num = moment.shape[1:]
-    anywhere = pl.BlockSpec(memory_space=pl.ANY)
-    return pl.pallas_call(
-        state_pieces_kernel,
-        out_shape=jax.ShapeDtypeStruct((assign.shape[0], 2, row_num, col_num), half),
-        in_specs=[pl.BlockSpec(memory_space=pltpu.SMEM), anywhere, anywhere],
+        in_specs=[pl.BlockSpec(memory_space=pltpu.SMEM)] + [anywhere] * 5,
         out_specs=pl.BlockSpec(memory_space=pltpu.VMEM),
         scratch_shapes=[
             pltpu.VMEM((2, slot_cap, row_num, col_num), jnp.float32),
-            pltpu.VMEM((slot_cap, 2, row_num, col_num), half),
-            pltpu.SemaphoreType.DMA((2,)),
+            pltpu.SemaphoreType.DMA((2 * slot_cap + 2,)),
         ],
-        name="state_pieces",
-    )(assign, moment, second)
+        compiler_params=pltpu.CompilerParams(vmem_limit_bytes=60 * 1024 * 1024),
+        name="first_payload",
+    )(core, grads, left, right, moment, second)
 
 
 def copies(value, count):
@@ -173,32 +161,36 @@
     chip = row_index // 2
     first = row_index % 2 == 0
     chip_rows = 2 * row_num
+    kinds = 4
+
+    grads = grad_parts[0, 0]
+    came = swap_cores(
+        first_payload(
+            (row_index % 2).reshape(1), grad_parts, left_basis, right_basis, moment, second
+        )
+    )
+    slots = jnp.stack(
+        [left_basis[0], right_basis[0], moment[0].astype(half), second[0].astype(half)], 1
+    )
+    numbers = slot_numbers(assign)
+
     y_num = chips // 2
     z_num = owner_num // 2
-    kinds = 2
-
-    came = swap_cores(
-        first_payload((row_index % 2).reshape(1), grad_parts, left_basis, right_basis)
-    )
-
-    numbers = slot_numbers(assign)
-    states = lax.all_to_all(state_pieces(assign, moment, second), "owner", 0, 0)
-    states = lax.dynamic_index_in_dim(states, assign[owner], 0, keepdims=False)
-
-    pair = (grad_parts[0, 0].astype(jnp.float32) + came.astype(jnp.float32)).astype(half)
+    pair = (grads.astype(jnp.float32) + came.astype(jnp.float32)).astype(half)
     pair = pair.reshape(y_num, 2, chip_rows, col_num)
     even = chip % 2 == 0
     kept = jnp.where(even, pair[:, 0], pair[:, 1])
     sent = jnp.where(even, pair[:, 1], pair[:, 0]).reshape(-1, col_num)
-    slots = jnp.stack([left_basis[0], right_basis[0]], 1)
     slot_rows = slot_cap * kinds * row_num
     chip_slots = jnp.stack([came[:slot_rows].reshape(slots.shape), slots], 2)
     chip_slots = chip_slots.reshape(slot_cap * kinds * chip_rows, col_num)
-    slot_rows = chip_slots.shape[0]
+    sent_num = sent.shape[0]
     beside = swap_x(
-        jnp.concatenate([jnp.where(first, sent[:slot_rows], chip_slots), sent[slot_rows:]], 0)
-    )
-    sums = kept.astype(jnp.float32) + beside.reshape(kept.shape).astype(jnp.float32)
+        jnp.concatenate(
+            [jnp.where(first, sent, chip_slots[:sent_num]), chip_slots[sent_num:]], 0
+        )
+    )
+    sums = kept.astype(jnp.float32) + beside[:sent_num].reshape(kept.shape).astype(jnp.float32)
     sums = sums.astype(half)
 
     owner_x = owner % 2
@@ -206,7 +198,7 @@
     number = lax.dynamic_index_in_dim(numbers.reshape(z_num, 2), owner_x, 1, keepdims=False)
     code = (number + slot_cap * (from_owner % 2 != owner_x))[:, None, None]
     chip_slots = chip_slots.reshape(slot_cap, kinds * chip_rows, col_num)
-    beside = beside[:slot_rows].reshape(chip_slots.shape)
+    beside = beside.reshape(chip_slots.shape)
     picked = chip_slots[0][None]
     for slot in range(1, slot_cap):
         picked = jnp.where(code == slot, chip_slots[slot][None], picked)
@@ -222,7 +214,7 @@
     grad_rows = jnp.sum(parts[:, :chip_rows].astype(jnp.float32), axis=0).astype(half)
     home = lax.dynamic_index_in_dim(parts, assign[owner] // 2, 0, keepdims=False)
 
-    left_rows, right_rows = home.reshape(kinds, chip_rows, col_num)
+    left_rows, right_rows = home.reshape(kinds, chip_rows, col_num)[:2]
     left_chunks = left_rows.reshape(chip_rows, chunk_num, LANES).transpose(1, 0, 2)
     left_chunks = jnp.broadcast_to(
         left_chunks[:, None], (chunk_num, chips // chunk_num, chip_rows, LANES)
@@ -240,12 +232,9 @@
     right_term = own_rows(dot(grad_cols, core_full, (0, 0)).astype(half))
     grams = exchange_lines(copies(jnp.concatenate([left_term, right_term], 0), z_num), 1)
 
-    extra = jnp.concatenate([left_rows, states.reshape(-1, col_num)], 0)
-    extra = jnp.concatenate([extra, extra[:, :LANES]], 1)
-    other = swap_cores(jnp.concatenate([mine, extra], 0))
-    left_rows = other[col_num : col_num + chip_rows, :col_num]
-    other_states = other[col_num + chip_rows :, :col_num].reshape(states.shape)
-    states = jnp.concatenate([states, other_states], 1).astype(jnp.float32)
+    wide_home = jnp.concatenate([home, home[:, :LANES]], 1)
+    other = swap_cores(jnp.concatenate([mine, wide_home], 0))
+    home = jnp.where(first, other[col_num:, :col_num], home).reshape(kinds, chip_rows, col_num)
     other = other[:col_num]
     grad_full = jnp.where(first, core_full, other[:, :col_num])
     right_full = jnp.where(first, other[:, :col_num], core_full)
@@ -253,8 +242,8 @@
 
     turned = own_rows(dot(left_cols, grad_full, (0, 0)).astype(half))
     rotated = dot(turned, right_full, (1, 0))
-    home_moment = beta_one * states[0] + (1.0 - beta_one) * rotated
-    home_second = beta_two * states[1] + (1.0 - beta_two) * rotated * rotated
+    home_moment = beta_one * home[2].astype(jnp.float32) + (1.0 - beta_one) * rotated
+    home_second = beta_two * home[3].astype(jnp.float32) + (1.0 - beta_two) * rotated * rotated
     direction = (home_moment / bias_one / (jnp.sqrt(home_second / bias_two) + adam_eps)).astype(half)
     back_rows = dot(direction, right_full, (1, 1)).astype(half)
 
@@ -271,12 +260,11 @@
 
     own_grams = taken(held(from_owner, number, owner), grams)
     beside_grams = taken(held(from_owner, number, owner ^ 1), grams)
-    owners_beside = [(i, i ^ 1) for i in range(owner_num)]
-    own_grams = own_grams + lax.ppermute(beside_grams, "owner", owners_beside)
+    own_grams = own_grams + swap_owners_first(beside_grams)
     own_grams = own_grams.reshape(slot_cap * 2, 2, row_num, col_num)
 
     back_full = gathered.reshape(col_num, col_num)
-    chip_update = dot(left_rows, back_full, (1, 0)).astype(half)
+    chip_update = dot(home[0], back_full, (1, 0)).astype(half)
     turns = taken(held(assign, numbers, owner), gathered).reshape(slot_cap, 2, row_num, col_num)
     for_second = jnp.concatenate(
         [chip_update[row_num:], own_grams[:, 1].reshape(-1, col_num)], 0

time: 155 us -> 126 us (0.81)
  Pallas kernels: 19.7 us -> 2.01 us
  starting transfers between devices: 56.8 us -> 46.4 us
  waiting for transfers between devices: 62.3 us -> 57.8 us
  matrix products: 1.45 us -> 4.65 us
  other arithmetic: 5.72 us -> 7.64 us
    pallas_call x1, Pallas kernels: 17.1 us -> 2.01 us  [first_payload(): pl.pallas_call(first_payload_kernel, out_shape=jax.ShapeDtypeStruct(grads...]
    all_to_all x1, waiting for transfers between devices: 0.01 us -> 11.7 us  [exchange(): lax.all_to_all(pieces, ('dp', 'owner'), 0, 0, axis_index_groups=groups)]
    ppermute x1, waiting for transfers between devices: 9.18 us -> 0.01 us  [swap_owners_first(): return lax.ppermute(value, ('dp', 'owner'), pairs)]
    all_to_all x1 -> x0, waiting for transfers between devices: 9.08 us -> none  [on_device(): states = lax.all_to_all(state_pieces(assign, moment, second), 'owner', 0, 0)]
    all_to_all x1, starting transfers between devices: 4.05 us -> 10.5 us  [exchange(): lax.all_to_all(pieces, ('dp', 'owner'), 0, 0, axis_index_groups=groups)]
    all_to_all x1 -> x0, starting transfers between devices: 4.81 us -> none  [on_device(): states = lax.all_to_all(state_pieces(assign, moment, second), 'owner', 0, 0)]
    ppermute x1, starting transfers between devices: 4.77 us -> 0.67 us  [swap_owners_first(): return lax.ppermute(value, ('dp', 'owner'), pairs)]
    all_to_all x1, starting transfers between devices: 12.8 us -> 8.96 us  [exchange_dp(): return lax.all_to_all(pieces, 'dp', 0, 0, axis_index_groups=groups)]
  transfers between devices with their start and end apart: 10 -> 9, of which waited for: 8 -> 7; matrix products, arithmetic and copies ran while one was open for 4% -> 7% of each run, Pallas kernels for 2% -> 0%
where the time goes in v7:
time: 126 us; the launch traced here: 125 us
  waiting for transfers between devices  57.8 us (46%)
  starting transfers between devices  46.4 us (37%)
  other arithmetic  7.64 us (6%)
  matrix products  4.65 us (4%)
  between operations  3.88 us (3%)
  local copies, waits for them, and re-layouts  3.02 us (2%)
  Pallas kernels  2.01 us (2%)
    all_to_all x2, waiting for transfers between devices, exchange_lines(): lax.all_to_all(pieces, ('dp', 'owner'), 0, 0, axis_index_groups=groups)  21.7 us
    all_to_all x1, waiting for transfers between devices, exchange_dp(): return lax.all_to_all(pieces, 'dp', 0, 0, axis_index_groups=groups)  13.9 us
    ppermute x3, starting transfers between devices, swap_cores(): lax.ppermute(value, 'dp', [(i, i ^ 1) for i in range(lax.axis_size('dp'))])  13.7 us
    all_to_all x1, waiting for transfers between devices, exchange(): lax.all_to_all(pieces, ('dp', 'owner'), 0, 0, axis_index_groups=groups)  11.7 us
    all_to_all x2, starting transfers between devices, exchange_lines(): lax.all_to_all(pieces, ('dp', 'owner'), 0, 0, axis_index_groups=groups)  10.6 us
    all_to_all x1, starting transfers between devices, exchange(): lax.all_to_all(pieces, ('dp', 'owner'), 0, 0, axis_index_groups=groups)  10.5 us
    all_to_all x1, starting transfers between devices, exchange_dp(): return lax.all_to_all(pieces, 'dp', 0, 0, axis_index_groups=groups)  8.96 us
    ppermute x1, waiting for transfers between devices, swap_x(): return lax.ppermute(value, ('dp', 'owner'), pairs)  8.42 us
  transfers between devices with their start and end apart: 9, of which 7 were waited for; matrix products, arithmetic and copies ran while one was open for 7% of the time, Pallas kernels for 0%

profile of v7, /device:TPU:1, one launch (start us, length us, event | category | flops | bytes accessed | tf_op | source)
XLA Modules:
  0.0 125.4 jit_solution(10506992069972901670)
XLA Ops:
  0.7 2.0 %first_payload.1 = bf16[512,512]{1,0:T(8,128)(2,1)} custom-call(s32[1]{0:T(128)} %bitcast.1.core, bf16[1,1,512,512]{3,2,1,0:T(8,128)(2,1)} %grads.1, bf16[1,3,16,512]{3,2,1,0:T(8,128)(2,1)} %left.1, bf16[1,3,16,512]{3,2,1,0:T(8,128)(2,1)} %right.1, f32[1,3,16,512]{3,2,1,0:T(8,128)} %moment.1, f32[1,3,16,512]{3,2,1,0:T(8,128)} %second.1), custom_call_target="tpu_custom_call" | custom-call | tf_op jit(solution)/shard_map/first_payload/pallas_call | solution.py:127
  2.7 8.8 %collective-permute-start = (bf16[512,512]{1,0:T(8,128)(2,1)}, bf16[512,512]{1,0:T(8,128)(2,1)S(1)}, u32[]{:S(2)}, u32[]{:S(2)}) collective-permute-start(bf16[512,512]{1,0:T(8,128)(2,1)} %first_payload.1), channel_id=1, source_target_pairs={{0,16},{16,0},{32,48},{48,32},{64,80},{80,64},{96,112},{112,96},{1... | collective-permute-start | bytes 1572872 | tf_op jit(solution)/shard_map/ppermute | solution.py:27
  12.2 1.0 collective-permute-done
  13.6 1.9 %collective-permute-start.1 = (bf16[384,512]{1,0:T(8,128)(2,1)S(1)}, bf16[384,512]{1,0:T(8,128)(2,1)S(1)}, u32[]{:S(2)}, u32[]{:S(2)}) collective-permute-start(bf16[384,512]{1,0:T(8,128)(2,1)S(1)} %pad_maximum_fusion.2), channel_id=1, source_target_pairs={{0,32},{16,17},{1,33},{17,16},{2,34},{18,19},{3,35},{19,18},{4,36}... | collective-permute-start | bytes 1179656 | tf_op jit(solution)/shard_map/ppermute | solution.py:72
  15.6 8.4 %collective-permute-done.1 = bf16[384,512]{1,0:T(8,128)(2,1)S(1)} collective-permute-done((bf16[384,512]{1,0:T(8,128)(2,1)S(1)}, bf16[384,512]{1,0:T(8,128)(2,1)S(1)}, u32[]{:S(2)}, u32[]{:S(2)}) %collective-permute-start.1) | collective-permute-done | bytes 393248 | tf_op jit(solution)/shard_map/ppermute | solution.py:72
  24.7 1.0 pad_maximum_fusion
  25.8 7.1 %all-to-all-start = ((bf16[8,128,512]{2,1,0:T(8,128)(2,1)}), bf16[8,128,512]{2,1,0:T(8,128)(2,1)S(1)}, u32[]{:S(2)}, u32[]{:S(2)}) async-start(bf16[8,128,512]{2,1,0:T(8,128)(2,1)} %pad_maximum_fusion), calls=%async_computation | async-start | bytes 2097152 | tf_op jit(solution)/shard_map/all_to_all | solution.py:61
  36.1 14.6 %all-to-all-done = bf16[8,128,512]{2,1,0:T(8,128)(2,1)S(1)} async-done(((bf16[8,128,512]{2,1,0:T(8,128)(2,1)}), bf16[8,128,512]{2,1,0:T(8,128)(2,1)S(1)}, u32[]{:S(2)}, u32[]{:S(2)}) %all-to-all-start) | async-done | bytes 1048608 | tf_op jit(solution)/shard_map/all_to_all | solution.py:61
  50.9 0.9 pad_maximum_fusion.1
  51.8 9.0 %all-to-all-start.1 = ((bf16[16,32,640]{2,1,0:T(8,128)(2,1)}), bf16[16,32,640]{2,1,0:T(8,128)(2,1)S(1)}, u32[]{:S(2)}, u32[]{:S(2)}) async-start(bf16[16,32,640]{2,1,0:T(8,128)(2,1)} %pad_maximum_fusion.1), calls=%async_computation.1 | async-start | bytes 1310720 | tf_op jit(solution)/shard_map/all_to_all | solution.py:37
  60.8 13.9 %all-to-all-done.1 = bf16[16,32,640]{2,1,0:T(8,128)(2,1)S(1)} async-done(((bf16[16,32,640]{2,1,0:T(8,128)(2,1)}), bf16[16,32,640]{2,1,0:T(8,128)(2,1)S(1)}, u32[]{:S(2)}, u32[]{:S(2)}) %all-to-all-start.1) | async-done | bytes 655392 | tf_op jit(solution)/shard_map/all_to_all | solution.py:37
  74.8 1.9 %collective-permute-start.2 = (bf16[640,640]{1,0:T(8,128)(2,1)S(1)}, bf16[640,640]{1,0:T(8,128)(2,1)}, u32[]{:S(2)}, u32[]{:S(2)}) collective-permute-start(bf16[640,640]{1,0:T(8,128)(2,1)S(1)} %maximum_maximum_fusion), channel_id=1, source_target_pairs={{0,16},{16,0},{32,48},{48,32},{64,80},{80,64},{96,112},{112,96},{1... | collective-permute-start | bytes 2457608 | tf_op jit(solution)/shard_map/ppermute | solution.py:27
  77.4 0.8 broadcast_in_dim.193
  78.3 3.5 %all-to-all-start.2 = ((bf16[8,64,512]{2,1,0:T(8,128)(2,1)}), bf16[8,64,512]{2,1,0:T(8,128)(2,1)S(1)}, u32[]{:S(2)}, u32[]{:S(2)}) async-start(bf16[8,64,512]{2,1,0:T(8,128)(2,1)} %broadcast_in_dim.193), calls=%async_computation.2 | async-start | bytes 1048576 | tf_op jit(solution)/shard_map/all_to_all | solution.py:61
  81.8 0.9 slice_select_fusion.2
  82.7 1.4 %fusion.3 = bf16[128,512]{1,0:T(8,128)(2,1)S(1)} fusion(pred[]{:T(512)S(6)} %eq.137, bf16[640,640]{1,0:T(8,128)(2,1)} %collective-permute-done.2, bf16[512,640]{1,0:T(8,128)(2,1)S(1)} %bitcast.78), kind=kOutput, calls=%fused_computation.15 | convolution fusion | flops 67436544 | bytes 1442816 | tf_op jit(solution)/shard_map/dot_general | solution.py:146
  84.1 1.2 fusion.9
  85.4 1.3 %fusion = bf16[32,512]{1,0:T(8,128)(2,1)S(1)} fusion(pred[]{:T(512)S(6)} %eq.137, bf16[640,640]{1,0:T(8,128)(2,1)} %collective-permute-done.2, f32[32,512]{1,0:T(8,128)S(1)} %fusion.9, bf16[128,512]{1,0:T(8,128)(2,1)S(1)} %slice_select_fusion.2, bf16[512,640]{1,0:T(8,128)(2,1)S(1)} %bitcast.80), kind=kOutput, calls=%fused_computation.6 | convolution fusion | flops 17317888 | bytes 1278976 | tf_op jit(solution)/shard_map/dot_general | solution.py:146
  86.7 7.1 %all-to-all-done.2 = bf16[8,64,512]{2,1,0:T(8,128)(2,1)S(1)} async-done(((bf16[8,64,512]{2,1,0:T(8,128)(2,1)}), bf16[8,64,512]{2,1,0:T(8,128)(2,1)S(1)}, u32[]{:S(2)}, u32[]{:S(2)}) %all-to-all-start.2) | async-done | bytes 524320 | tf_op jit(solution)/shard_map/all_to_all | solution.py:61
  93.8 0.9 broadcast_in_dim.192
  94.7 10.5 %all-to-all-start.3 = ((bf16[16,32,512]{2,1,0:T(8,128)(2,1)}), bf16[16,32,512]{2,1,0:T(8,128)(2,1)S(1)}, u32[]{:S(2)}, u32[]{:S(2)}) async-start(bf16[16,32,512]{2,1,0:T(8,128)(2,1)} %broadcast_in_dim.192), calls=%async_computation.3 | async-start | bytes 1048576 | tf_op jit(solution)/shard_map/all_to_all | solution.py:45
  106.9 11.7 %all-to-all-done.3 = bf16[16,32,512]{2,1,0:T(8,128)(2,1)S(1)} async-done(((bf16[16,32,512]{2,1,0:T(8,128)(2,1)}), bf16[16,32,512]{2,1,0:T(8,128)(2,1)S(1)}, u32[]{:S(2)}, u32[]{:S(2)}) %all-to-all-start.3) | async-done | bytes 524320 | tf_op jit(solution)/shard_map/all_to_all | solution.py:45
  119.3 3.0 %collective-permute-start.4 = (bf16[112,512]{1,0:T(8,128)(2,1)S(1)}, bf16[112,512]{1,0:T(8,128)(2,1)S(1)}, u32[]{:S(2)}, u32[]{:S(2)}) collective-permute-start(bf16[112,512]{1,0:T(8,128)(2,1)S(1)} %pad_maximum_fusion.4), channel_id=1, source_target_pairs={{0,16},{16,0},{32,48},{48,32},{64,80},{80,64},{96,112},{112,96},{1... | collective-permute-start | bytes 344072 | tf_op jit(solution)/shard_map/ppermute | solution.py:27
  122.4 0.9 collective-permute-done.4
  (75 shorter events, 7.4 us)
Async XLA Ops:
  0.6 11.5 %copy-start.3 = (bf16[1,3,16,512]{3,2,1,0:T(8,128)(2,1)S(1)}, bf16[1,3,16,512]{3,2,1,0:T(8,128)(2,1)}, u32[]{:S(2)}) copy-start(bf16[1,3,16,512]{3,2,1,0:T(8,128)(2,1)} %left.1) | copy-start | bytes 147460
  0.6 11.5 %copy-start.4 = (bf16[1,3,16,512]{3,2,1,0:T(8,128)(2,1)S(1)}, bf16[1,3,16,512]{3,2,1,0:T(8,128)(2,1)}, u32[]{:S(2)}) copy-start(bf16[1,3,16,512]{3,2,1,0:T(8,128)(2,1)} %right.1) | copy-start | bytes 147460
  0.7 11.5 %copy-start.1 = (f32[1,3,16,512]{3,2,1,0:T(8,128)S(1)}, f32[1,3,16,512]{3,2,1,0:T(8,128)}, u32[]{:S(2)}) copy-start(f32[1,3,16,512]{3,2,1,0:T(8,128)} %moment.1) | copy-start | bytes 294916
  0.7 11.5 %copy-start.2 = (f32[1,3,16,512]{3,2,1,0:T(8,128)S(1)}, f32[1,3,16,512]{3,2,1,0:T(8,128)}, u32[]{:S(2)}) copy-start(f32[1,3,16,512]{3,2,1,0:T(8,128)} %second.1) | copy-start | bytes 294916
  0.7 10.9 %copy-start.7 = (s32[16]{0:T(128)S(1)}, s32[16]{0:T(128)}, u32[]{:S(2)}) copy-start(s32[16]{0:T(128)} %param.9) | copy-start | bytes 196
  2.7 10.5 %collective-permute-start = (bf16[512,512]{1,0:T(8,128)(2,1)}, bf16[512,512]{1,0:T(8,128)(2,1)S(1)}, u32[]{:S(2)}, u32[]{:S(2)}) collective-permute-start(bf16[512,512]{1,0:T(8,128)(2,1)} %first_payload.1), channel_id=1, source_target_pairs={{0,16},{16,0},{32,48},{48,32},{64,80},{80,64},{96,112},{112,96},{1... | collective-permute-start | bytes 1572872 | tf_op jit(solution)/shard_map/ppermute | solution.py:27
  12.2 1.1 copy-start
  13.6 10.4 %collective-permute-start.1 = (bf16[384,512]{1,0:T(8,128)(2,1)S(1)}, bf16[384,512]{1,0:T(8,128)(2,1)S(1)}, u32[]{:S(2)}, u32[]{:S(2)}) collective-permute-start(bf16[384,512]{1,0:T(8,128)(2,1)S(1)} %pad_maximum_fusion.2), channel_id=1, source_target_pairs={{0,32},{16,17},{1,33},{17,16},{2,34},{18,19},{3,35},{19,18},{4,36}... | collective-permute-start | bytes 1179656 | tf_op jit(solution)/shard_map/ppermute | solution.py:72
  25.8 25.0 %all-to-all-start = ((bf16[8,128,512]{2,1,0:T(8,128)(2,1)}), bf16[8,128,512]{2,1,0:T(8,128)(2,1)S(1)}, u32[]{:S(2)}, u32[]{:S(2)}) async-start(bf16[8,128,512]{2,1,0:T(8,128)(2,1)} %pad_maximum_fusion), calls=%async_computation | async-start | bytes 2097152 | tf_op jit(solution)/shard_map/all_to_all | solution.py:61
  51.8 22.9 %all-to-all-start.1 = ((bf16[16,32,640]{2,1,0:T(8,128)(2,1)}), bf16[16,32,640]{2,1,0:T(8,128)(2,1)S(1)}, u32[]{:S(2)}, u32[]{:S(2)}) async-start(bf16[16,32,640]{2,1,0:T(8,128)(2,1)} %pad_maximum_fusion.1), calls=%async_computation.1 | async-start | bytes 1310720 | tf_op jit(solution)/shard_map/all_to_all | solution.py:37
  74.8 6.9 %collective-permute-start.2 = (bf16[640,640]{1,0:T(8,128)(2,1)S(1)}, bf16[640,640]{1,0:T(8,128)(2,1)}, u32[]{:S(2)}, u32[]{:S(2)}) collective-permute-start(bf16[640,640]{1,0:T(8,128)(2,1)S(1)} %maximum_maximum_fusion), channel_id=1, source_target_pairs={{0,16},{16,0},{32,48},{48,32},{64,80},{80,64},{96,112},{112,96},{1... | collective-permute-start | bytes 2457608 | tf_op jit(solution)/shard_map/ppermute | solution.py:27
  78.3 15.6 %all-to-all-start.2 = ((bf16[8,64,512]{2,1,0:T(8,128)(2,1)}), bf16[8,64,512]{2,1,0:T(8,128)(2,1)S(1)}, u32[]{:S(2)}, u32[]{:S(2)}) async-start(bf16[8,64,512]{2,1,0:T(8,128)(2,1)} %broadcast_in_dim.193), calls=%async_computation.2 | async-start | bytes 1048576 | tf_op jit(solution)/shard_map/all_to_all | solution.py:61
  94.7 23.9 %all-to-all-start.3 = ((bf16[16,32,512]{2,1,0:T(8,128)(2,1)}), bf16[16,32,512]{2,1,0:T(8,128)(2,1)S(1)}, u32[]{:S(2)}, u32[]{:S(2)}) async-start(bf16[16,32,512]{2,1,0:T(8,128)(2,1)} %broadcast_in_dim.192), calls=%async_computation.3 | async-start | bytes 1048576 | tf_op jit(solution)/shard_map/all_to_all | solution.py:45
  106.1 0.7 collective-permute-start.3
  119.3 4.8 %copy-start.5 = (f32[1,3,16,512]{3,2,1,0:T(8,128)S(1)}, f32[1,3,16,512]{3,2,1,0:T(8,128)}, u32[]{:S(2)}) copy-start(f32[1,3,16,512]{3,2,1,0:T(8,128)} %param.13) | copy-start | bytes 294916
  119.3 4.8 %copy-start.6 = (f32[1,3,16,512]{3,2,1,0:T(8,128)S(1)}, f32[1,3,16,512]{3,2,1,0:T(8,128)}, u32[]{:S(2)}) copy-start(f32[1,3,16,512]{3,2,1,0:T(8,128)} %param.12) | copy-start | bytes 294916
  119.3 4.0 %collective-permute-start.4 = (bf16[112,512]{1,0:T(8,128)(2,1)S(1)}, bf16[112,512]{1,0:T(8,128)(2,1)S(1)}, u32[]{:S(2)}, u32[]{:S(2)}) collective-permute-start(bf16[112,512]{1,0:T(8,128)(2,1)S(1)} %pad_maximum_fusion.4), channel_id=1, source_target_pairs={{0,16},{16,0},{32,48},{48,32},{64,80},{80,64},{96,112},{112,96},{1... | collective-permute-start | bytes 344072 | tf_op jit(solution)/shard_map/ppermute | solution.py:27

commit v8 on v7

--- a/solution.py
+++ b/solution.py
@@ -37,24 +37,26 @@
     return lax.all_to_all(pieces, "dp", 0, 0, axis_index_groups=groups)
 
 
-def exchange(pieces):
+def exchange(pieces, dp_core):
     chips = lax.axis_size("dp") // 2
     owners = lax.axis_size("owner")
-    groups = [[place(chip, 0, owner) for chip in range(chips)] for owner in range(owners)]
-    groups += [[place(chip, 1, owner) for owner in range(owners)] for chip in range(chips)]
+    groups = [[place(chip, dp_core, owner) for chip in range(chips)] for owner in range(owners)]
+    groups += [
+        [place(chip, 1 - dp_core, owner) for owner in range(owners)] for chip in range(chips)
+    ]
     return lax.all_to_all(pieces, ("dp", "owner"), 0, 0, axis_index_groups=groups)
 
 
-def exchange_lines(pieces, y_core):
+def exchange_lines(pieces):
     chips = lax.axis_size("dp") // 2
     owners = lax.axis_size("owner")
     groups = [
-        [place(2 * y + x, y_core, owner) for y in range(chips // 2)]
+        [place(2 * y + x, 0, owner) for y in range(chips // 2)]
         for owner in range(owners)
         for x in range(2)
     ]
     groups += [
-        [place(chip, 1 - y_core, 2 * z + x) for z in range(owners // 2)]
+        [place(chip, 1, 2 * z + x) for z in range(owners // 2)]
         for chip in range(chips)
         for x in range(2)
     ]
@@ -69,17 +71,6 @@
         for owner in range(owners):
             pairs.append((place(chip, 0, owner), place(chip ^ 1, 0, owner)))
             pairs.append((place(chip, 1, owner), place(chip, 1, owner ^ 1)))
-    return lax.ppermute(value, ("dp", "owner"), pairs)
-
-
-def swap_owners_first(value):
-    chips = lax.axis_size("dp") // 2
-    owners = lax.axis_size("owner")
-    pairs = [
-        (place(chip, 0, owner), place(chip, 0, owner ^ 1))
-        for chip in range(chips)
-        for owner in range(owners)
-    ]
     return lax.ppermute(value, ("dp", "owner"), pairs)
 
 
@@ -208,8 +199,7 @@
     parts = exchange_lines(
         jnp.concatenate(
             [jnp.where(first, sums, picked[:, :chip_rows]), picked[:, chip_rows:]], 1
-        ),
-        0,
+        )
     )
     grad_rows = jnp.sum(parts[:, :chip_rows].astype(jnp.float32), axis=0).astype(half)
     home = lax.dynamic_index_in_dim(parts, assign[owner] // 2, 0, keepdims=False)
@@ -230,7 +220,9 @@
     grad_cols = lax.dynamic_slice_in_dim(core_full, chunk * LANES, LANES, 1)
     left_term = dot(grad_rows, core_full, (1, 1)).astype(half)
     right_term = own_rows(dot(grad_cols, core_full, (0, 0)).astype(half))
-    grams = exchange_lines(copies(jnp.concatenate([left_term, right_term], 0), z_num), 1)
+    grams = copies(jnp.concatenate([left_term, right_term], 0), owner_num)
+    grams, home = lax.optimization_barrier((grams, home))
+    grams = exchange(grams, 1)
 
     wide_home = jnp.concatenate([home, home[:, :LANES]], 1)
     other = swap_cores(jnp.concatenate([mine, wide_home], 0))
@@ -249,7 +241,7 @@
 
     results = copies(jnp.where(first, back_rows, rotated.astype(half)), chips)
     results, grams = lax.optimization_barrier((results, grams))
-    gathered = exchange(results)
+    gathered = exchange(results, 0)
     held = lambda blocks, counts, target: (blocks == target)[None, :] & (
         counts[None, :] == jnp.arange(slot_cap, dtype=jnp.int32)[:, None]
     )
@@ -258,9 +250,7 @@
         values = jnp.where(mask[:, :, None, None], values[None].astype(jnp.float32), 0.0)
         return jnp.sum(values, axis=1).astype(half)
 
-    own_grams = taken(held(from_owner, number, owner), grams)
-    beside_grams = taken(held(from_owner, number, owner ^ 1), grams)
-    own_grams = own_grams + swap_owners_first(beside_grams)
+    own_grams = taken(held(assign, numbers, owner), grams)
     own_grams = own_grams.reshape(slot_cap * 2, 2, row_num, col_num)
 
     back_full = gathered.reshape(col_num, col_num)

time: 126 us -> 133 us (1.056)
  starting transfers between devices: 46.4 us -> 54.5 us
  matrix products: 4.65 us -> 1.49 us
  other arithmetic: 7.64 us -> 9.24 us
    ppermute x3, starting transfers between devices: 13.7 us -> 22.8 us  [swap_cores(): lax.ppermute(value, 'dp', [(i, i ^ 1) for i in range(lax.axis_size('dp'))])]
    all_to_all x2 -> x1, waiting for transfers between devices: 21.7 us -> 14.6 us  [exchange_lines(): lax.all_to_all(pieces, ('dp', 'owner'), 0, 0, axis_index_groups=groups)]
    all_to_all x1 -> x2, waiting for transfers between devices: 11.7 us -> 17.4 us  [exchange(): lax.all_to_all(pieces, ('dp', 'owner'), 0, 0, axis_index_groups=groups)]
    all_to_all x2 -> x1, starting transfers between devices: 10.6 us -> 7.07 us  [exchange_lines(): lax.all_to_all(pieces, ('dp', 'owner'), 0, 0, axis_index_groups=groups)]
    all_to_all x1 -> x2, starting transfers between devices: 10.5 us -> 13.8 us  [exchange(): lax.all_to_all(pieces, ('dp', 'owner'), 0, 0, axis_index_groups=groups)]
    dot_general x6, matrix products: 4.65 us -> 1.49 us  [dot(): lax.dot_general(left, right, ((contract[:1], contract[1:]), ((), ())), pr...]
  transfers between devices with their start and end apart: 9 -> 8, of which waited for: 7 -> 7; matrix products, arithmetic and copies ran while one was open for 7% -> 5% of each run, Pallas kernels for 0% -> 0%
where the time goes in v8:
time: 133 us; the launch traced here: 132 us
  waiting for transfers between devices  57.1 us (43%)
  starting transfers between devices  54.5 us (41%)
  other arithmetic  9.24 us (7%)
  local copies, waits for them, and re-layouts  3.93 us (3%)
  between operations  3.81 us (3%)
  Pallas kernels  1.97 us (1%)
  matrix products  1.49 us (1%)
    ppermute x3, starting transfers between devices, swap_cores(): lax.ppermute(value, 'dp', [(i, i ^ 1) for i in range(lax.axis_size('dp'))])  22.8 us
    all_to_all x2, waiting for transfers between devices, exchange(): lax.all_to_all(pieces, ('dp', 'owner'), 0, 0, axis_index_groups=groups)  17.4 us
    all_to_all x1, waiting for transfers between devices, exchange_lines(): lax.all_to_all(pieces, ('dp', 'owner'), 0, 0, axis_index_groups=groups)  14.6 us
    all_to_all x2, starting transfers between devices, exchange(): lax.all_to_all(pieces, ('dp', 'owner'), 0, 0, axis_index_groups=groups)  13.8 us
    all_to_all x1, waiting for transfers between devices, exchange_dp(): return lax.all_to_all(pieces, 'dp', 0, 0, axis_index_groups=groups)  13.5 us
    all_to_all x1, starting transfers between devices, exchange_dp(): return lax.all_to_all(pieces, 'dp', 0, 0, axis_index_groups=groups)  8.94 us
    ppermute x1, waiting for transfers between devices, swap_x(): return lax.ppermute(value, ('dp', 'owner'), pairs)  8.68 us
    all_to_all x1, starting transfers between devices, exchange_lines(): lax.all_to_all(pieces, ('dp', 'owner'), 0, 0, axis_index_groups=groups)  7.07 us
  transfers between devices with their start and end apart: 8, of which 7 were waited for; matrix products, arithmetic and copies ran while one was open for 5% of the time, Pallas kernels for 0%

profile of v8, /device:TPU:1, one launch (start us, length us, event | category | flops | bytes accessed | tf_op | source)
XLA Modules:
  0.0 132.0 jit_solution(10646915716157425867)
XLA Ops:
  0.7 2.0 %first_payload.1 = bf16[512,512]{1,0:T(8,128)(2,1)} custom-call(s32[1]{0:T(128)} %bitcast.1.core, bf16[1,1,512,512]{3,2,1,0:T(8,128)(2,1)} %grads.1, bf16[1,3,16,512]{3,2,1,0:T(8,128)(2,1)} %left.1, bf16[1,3,16,512]{3,2,1,0:T(8,128)(2,1)} %right.1, f32[1,3,16,512]{3,2,1,0:T(8,128)} %moment.1, f32[1,3,16,512]{3,2,1,0:T(8,128)} %second.1), custom_call_target="tpu_custom_call" | custom-call | tf_op jit(solution)/shard_map/first_payload/pallas_call | solution.py:118
  2.6 8.8 %collective-permute-start = (bf16[512,512]{1,0:T(8,128)(2,1)}, bf16[512,512]{1,0:T(8,128)(2,1)S(1)}, u32[]{:S(2)}, u32[]{:S(2)}) collective-permute-start(bf16[512,512]{1,0:T(8,128)(2,1)} %first_payload.1), channel_id=1, source_target_pairs={{0,16},{16,0},{32,48},{48,32},{64,80},{80,64},{96,112},{112,96},{1... | collective-permute-start | bytes 1572872 | tf_op jit(solution)/shard_map/ppermute | solution.py:27
  11.5 0.7 reshape.295
  12.2 0.9 convert_reduce_fusion
  13.4 1.0 convert_bitcast_fusion
  14.4 0.9 maximum_bitcast_fusion
  15.7 1.9 %collective-permute-start.1 = (bf16[384,512]{1,0:T(8,128)(2,1)S(1)}, bf16[384,512]{1,0:T(8,128)(2,1)S(1)}, u32[]{:S(2)}, u32[]{:S(2)}) collective-permute-start(bf16[384,512]{1,0:T(8,128)(2,1)S(1)} %pad_maximum_fusion.2), channel_id=1, source_target_pairs={{0,32},{16,17},{1,33},{17,16},{2,34},{18,19},{3,35},{19,18},{4,36}... | collective-permute-start | bytes 1179656 | tf_op jit(solution)/shard_map/ppermute | solution.py:74
  17.6 8.7 %collective-permute-done.1 = bf16[384,512]{1,0:T(8,128)(2,1)S(1)} collective-permute-done((bf16[384,512]{1,0:T(8,128)(2,1)S(1)}, bf16[384,512]{1,0:T(8,128)(2,1)S(1)}, u32[]{:S(2)}, u32[]{:S(2)}) %collective-permute-start.1) | collective-permute-done | bytes 393248 | tf_op jit(solution)/shard_map/ppermute | solution.py:74
  27.1 1.0 pad_maximum_fusion
  28.1 7.1 %all-to-all-start = ((bf16[8,128,512]{2,1,0:T(8,128)(2,1)}), bf16[8,128,512]{2,1,0:T(8,128)(2,1)S(1)}, u32[]{:S(2)}, u32[]{:S(2)}) async-start(bf16[8,128,512]{2,1,0:T(8,128)(2,1)} %pad_maximum_fusion), calls=%async_computation | async-start | bytes 2097152 | tf_op jit(solution)/shard_map/all_to_all | solution.py:63
  38.4 14.6 %all-to-all-done = bf16[8,128,512]{2,1,0:T(8,128)(2,1)S(1)} async-done(((bf16[8,128,512]{2,1,0:T(8,128)(2,1)}), bf16[8,128,512]{2,1,0:T(8,128)(2,1)S(1)}, u32[]{:S(2)}, u32[]{:S(2)}) %all-to-all-start) | async-done | bytes 1048608 | tf_op jit(solution)/shard_map/all_to_all | solution.py:63
  53.2 0.9 pad_maximum_fusion.1
  54.1 8.9 %all-to-all-start.1 = ((bf16[16,32,640]{2,1,0:T(8,128)(2,1)}), bf16[16,32,640]{2,1,0:T(8,128)(2,1)S(1)}, u32[]{:S(2)}, u32[]{:S(2)}) async-start(bf16[16,32,640]{2,1,0:T(8,128)(2,1)} %pad_maximum_fusion.1), calls=%async_computation.1 | async-start | bytes 1310720 | tf_op jit(solution)/shard_map/all_to_all | solution.py:37
  63.1 13.5 %all-to-all-done.1 = bf16[16,32,640]{2,1,0:T(8,128)(2,1)S(1)} async-done(((bf16[16,32,640]{2,1,0:T(8,128)(2,1)}), bf16[16,32,640]{2,1,0:T(8,128)(2,1)S(1)}, u32[]{:S(2)}, u32[]{:S(2)}) %all-to-all-start.1) | async-done | bytes 655392 | tf_op jit(solution)/shard_map/all_to_all | solution.py:37
  77.2 1.1 broadcast_in_dim.178
  78.3 3.7 %all-to-all-start.2 = ((bf16[16,64,512]{2,1,0:T(8,128)(2,1)}), bf16[16,64,512]{2,1,0:T(8,128)(2,1)S(1)}, u32[]{:S(2)}, u32[]{:S(2)}) async-start(bf16[16,64,512]{2,1,0:T(8,128)(2,1)} %broadcast_in_dim.178), calls=%async_computation.2 | async-start | bytes 2097152 | tf_op jit(solution)/shard_map/all_to_all | solution.py:47
  82.0 8.9 %collective-permute-start.2 = (bf16[640,640]{1,0:T(8,128)(2,1)S(1)}, bf16[640,640]{1,0:T(8,128)(2,1)S(1)}, u32[]{:S(2)}, u32[]{:S(2)}) collective-permute-start(bf16[640,640]{1,0:T(8,128)(2,1)S(1)} %maximum_maximum_fusion), channel_id=1, source_target_pairs={{0,16},{16,0},{32,48},{48,32},{64,80},{80,64},{96,112},{112,96},{1... | collective-permute-start | bytes 2457608 | tf_op jit(solution)/shard_map/ppermute | solution.py:27
  91.0 1.9 %collective-permute-done.2 = bf16[640,640]{1,0:T(8,128)(2,1)S(1)} collective-permute-done((bf16[640,640]{1,0:T(8,128)(2,1)S(1)}, bf16[640,640]{1,0:T(8,128)(2,1)S(1)}, u32[]{:S(2)}, u32[]{:S(2)}) %collective-permute-start.2) | collective-permute-done | bytes 819232 | tf_op jit(solution)/shard_map/ppermute | solution.py:27
  93.8 5.0 %all-to-all-done.2 = bf16[16,64,512]{2,1,0:T(8,128)(2,1)S(1)} async-done(((bf16[16,64,512]{2,1,0:T(8,128)(2,1)}), bf16[16,64,512]{2,1,0:T(8,128)(2,1)S(1)}, u32[]{:S(2)}, u32[]{:S(2)}) %all-to-all-start.2) | async-done | bytes 1048608 | tf_op jit(solution)/shard_map/all_to_all | solution.py:47
  98.8 0.8 broadcast_in_dim.179
  99.6 10.1 %all-to-all-start.3 = ((bf16[16,32,512]{2,1,0:T(8,128)(2,1)}), bf16[16,32,512]{2,1,0:T(8,128)(2,1)S(1)}, u32[]{:S(2)}, u32[]{:S(2)}) async-start(bf16[16,32,512]{2,1,0:T(8,128)(2,1)} %broadcast_in_dim.179), calls=%async_computation.3 | async-start | bytes 1048576 | tf_op jit(solution)/shard_map/all_to_all | solution.py:47
  110.8 12.4 %all-to-all-done.3 = bf16[16,32,512]{2,1,0:T(8,128)(2,1)S(1)} async-done(((bf16[16,32,512]{2,1,0:T(8,128)(2,1)}), bf16[16,32,512]{2,1,0:T(8,128)(2,1)S(1)}, u32[]{:S(2)}, u32[]{:S(2)}) %all-to-all-start.3) | async-done | bytes 524320 | tf_op jit(solution)/shard_map/all_to_all | solution.py:47
  123.8 5.0 %collective-permute-start.3 = (bf16[112,512]{1,0:T(8,128)(2,1)S(1)}, bf16[112,512]{1,0:T(8,128)(2,1)S(1)}, u32[]{:S(2)}, u32[]{:S(2)}) collective-permute-start(bf16[112,512]{1,0:T(8,128)(2,1)S(1)} %pad_maximum_fusion.4), channel_id=1, source_target_pairs={{0,16},{16,0},{32,48},{48,32},{64,80},{80,64},{96,112},{112,96},{1... | collective-permute-start | bytes 344072 | tf_op jit(solution)/shard_map/ppermute | solution.py:27
  128.9 0.9 collective-permute-done.3
  (67 shorter events, 7.3 us)
Async XLA Ops:
  0.6 14.8 %copy-start = (bf16[1,1,512,512]{3,2,1,0:T(8,128)(2,1)S(1)}, bf16[1,1,512,512]{3,2,1,0:T(8,128)(2,1)}, u32[]{:S(2)}) copy-start(bf16[1,1,512,512]{3,2,1,0:T(8,128)(2,1)} %grads.1) | copy-start | bytes 1572868
  2.6 12.6 %collective-permute-start = (bf16[512,512]{1,0:T(8,128)(2,1)}, bf16[512,512]{1,0:T(8,128)(2,1)S(1)}, u32[]{:S(2)}, u32[]{:S(2)}) collective-permute-start(bf16[512,512]{1,0:T(8,128)(2,1)} %first_payload.1), channel_id=1, source_target_pairs={{0,16},{16,0},{32,48},{48,32},{64,80},{80,64},{96,112},{112,96},{1... | collective-permute-start | bytes 1572872 | tf_op jit(solution)/shard_map/ppermute | solution.py:27
  15.7 10.6 %collective-permute-start.1 = (bf16[384,512]{1,0:T(8,128)(2,1)S(1)}, bf16[384,512]{1,0:T(8,128)(2,1)S(1)}, u32[]{:S(2)}, u32[]{:S(2)}) collective-permute-start(bf16[384,512]{1,0:T(8,128)(2,1)S(1)} %pad_maximum_fusion.2), channel_id=1, source_target_pairs={{0,32},{16,17},{1,33},{17,16},{2,34},{18,19},{3,35},{19,18},{4,36}... | collective-permute-start | bytes 1179656 | tf_op jit(solution)/shard_map/ppermute | solution.py:74
  27.0 8.1 %copy-start.5 = (s32[16]{0:T(128)S(1)}, s32[16]{0:T(128)}, u32[]{:S(2)}) copy-start(s32[16]{0:T(128)} %param.9) | copy-start | bytes 196
  28.1 24.9 %all-to-all-start = ((bf16[8,128,512]{2,1,0:T(8,128)(2,1)}), bf16[8,128,512]{2,1,0:T(8,128)(2,1)S(1)}, u32[]{:S(2)}, u32[]{:S(2)}) async-start(bf16[8,128,512]{2,1,0:T(8,128)(2,1)} %pad_maximum_fusion), calls=%async_computation | async-start | bytes 2097152 | tf_op jit(solution)/shard_map/all_to_all | solution.py:63
  54.1 22.5 %all-to-all-start.1 = ((bf16[16,32,640]{2,1,0:T(8,128)(2,1)}), bf16[16,32,640]{2,1,0:T(8,128)(2,1)S(1)}, u32[]{:S(2)}, u32[]{:S(2)}) async-start(bf16[16,32,640]{2,1,0:T(8,128)(2,1)} %pad_maximum_fusion.1), calls=%async_computation.1 | async-start | bytes 1310720 | tf_op jit(solution)/shard_map/all_to_all | solution.py:37
  78.3 20.5 %all-to-all-start.2 = ((bf16[16,64,512]{2,1,0:T(8,128)(2,1)}), bf16[16,64,512]{2,1,0:T(8,128)(2,1)S(1)}, u32[]{:S(2)}, u32[]{:S(2)}) async-start(bf16[16,64,512]{2,1,0:T(8,128)(2,1)} %broadcast_in_dim.178), calls=%async_computation.2 | async-start | bytes 2097152 | tf_op jit(solution)/shard_map/all_to_all | solution.py:47
  82.0 10.9 %collective-permute-start.2 = (bf16[640,640]{1,0:T(8,128)(2,1)S(1)}, bf16[640,640]{1,0:T(8,128)(2,1)S(1)}, u32[]{:S(2)}, u32[]{:S(2)}) collective-permute-start(bf16[640,640]{1,0:T(8,128)(2,1)S(1)} %maximum_maximum_fusion), channel_id=1, source_target_pairs={{0,16},{16,0},{32,48},{48,32},{64,80},{80,64},{96,112},{112,96},{1... | collective-permute-start | bytes 2457608 | tf_op jit(solution)/shard_map/ppermute | solution.py:27
  99.6 23.5 %all-to-all-start.3 = ((bf16[16,32,512]{2,1,0:T(8,128)(2,1)}), bf16[16,32,512]{2,1,0:T(8,128)(2,1)S(1)}, u32[]{:S(2)}, u32[]{:S(2)}) async-start(bf16[16,32,512]{2,1,0:T(8,128)(2,1)} %broadcast_in_dim.179), calls=%async_computation.3 | async-start | bytes 1048576 | tf_op jit(solution)/shard_map/all_to_all | solution.py:47
  110.7 19.1 %copy-start.1 = (f32[1,3,16,512]{3,2,1,0:T(8,128)S(1)}, f32[1,3,16,512]{3,2,1,0:T(8,128)}, u32[]{:S(2)}) copy-start(f32[1,3,16,512]{3,2,1,0:T(8,128)} %moment.1) | copy-start | bytes 294916
  110.7 19.1 %copy-start.2 = (f32[1,3,16,512]{3,2,1,0:T(8,128)S(1)}, f32[1,3,16,512]{3,2,1,0:T(8,128)}, u32[]{:S(2)}) copy-start(f32[1,3,16,512]{3,2,1,0:T(8,128)} %second.1) | copy-start | bytes 294916
  123.3 7.3 %copy-start.3 = (f32[1,3,16,512]{3,2,1,0:T(8,128)S(1)}, f32[1,3,16,512]{3,2,1,0:T(8,128)}, u32[]{:S(2)}) copy-start(f32[1,3,16,512]{3,2,1,0:T(8,128)} %param.13) | copy-start | bytes 294916
  123.3 7.3 %copy-start.4 = (f32[1,3,16,512]{3,2,1,0:T(8,128)S(1)}, f32[1,3,16,512]{3,2,1,0:T(8,128)}, u32[]{:S(2)}) copy-start(f32[1,3,16,512]{3,2,1,0:T(8,128)} %param.12) | copy-start | bytes 294916
  123.8 6.0 %collective-permute-start.3 = (bf16[112,512]{1,0:T(8,128)(2,1)S(1)}, bf16[112,512]{1,0:T(8,128)(2,1)S(1)}, u32[]{:S(2)}, u32[]{:S(2)}) collective-permute-start(bf16[112,512]{1,0:T(8,128)(2,1)S(1)} %pad_maximum_fusion.4), channel_id=1, source_target_pairs={{0,16},{16,0},{32,48},{48,32},{64,80},{80,64},{96,112},{112,96},{1... | collective-permute-start | bytes 344072 | tf_op jit(solution)/shard_map/ppermute | solution.py:27

commit v9 on v8

--- a/solution.py
+++ b/solution.py
@@ -35,16 +35,6 @@
     chips = lax.axis_size("dp") // 2
     groups = [[chip * 2 + core for chip in range(chips)] for core in range(2)]
     return lax.all_to_all(pieces, "dp", 0, 0, axis_index_groups=groups)
-
-
-def exchange(pieces, dp_core):
-    chips = lax.axis_size("dp") // 2
-    owners = lax.axis_size("owner")
-    groups = [[place(chip, dp_core, owner) for chip in range(chips)] for owner in range(owners)]
-    groups += [
-        [place(chip, 1 - dp_core, owner) for owner in range(owners)] for chip in range(chips)
-    ]
-    return lax.all_to_all(pieces, ("dp", "owner"), 0, 0, axis_index_groups=groups)
 
 
 def exchange_lines(pieces):
@@ -212,66 +202,68 @@
     rows = copies(jnp.where(first, grad_rows, right_rows), chips)
     mine = exchange_dp(jnp.concatenate([rows, left_chunks], 2))
     mine = mine.reshape(col_num, col_num + LANES)
-
-    chunk = chip // (chips // chunk_num)
-    in_chunk = (chip % (chips // chunk_num)) * chip_rows
-    own_rows = lambda value: lax.dynamic_slice_in_dim(value, in_chunk, chip_rows, 0)
-    core_full = mine[:, :col_num]
-    grad_cols = lax.dynamic_slice_in_dim(core_full, chunk * LANES, LANES, 1)
-    left_term = dot(grad_rows, core_full, (1, 1)).astype(half)
-    right_term = own_rows(dot(grad_cols, core_full, (0, 0)).astype(half))
-    grams = copies(jnp.concatenate([left_term, right_term], 0), owner_num)
-    grams, home = lax.optimization_barrier((grams, home))
-    grams = exchange(grams, 1)
-
     wide_home = jnp.concatenate([home, home[:, :LANES]], 1)
     other = swap_cores(jnp.concatenate([mine, wide_home], 0))
     home = jnp.where(first, other[col_num:, :col_num], home).reshape(kinds, chip_rows, col_num)
     other = other[:col_num]
-    grad_full = jnp.where(first, core_full, other[:, :col_num])
-    right_full = jnp.where(first, other[:, :col_num], core_full)
+    grad_full = jnp.where(first, mine[:, :col_num], other[:, :col_num])
+    right_full = jnp.where(first, other[:, :col_num], mine[:, :col_num])
     left_cols = jnp.where(first, other[:, col_num:], mine[:, col_num:])
 
+    chunk = chip // (chips // chunk_num)
+    in_chunk = (chip % (chips // chunk_num)) * chip_rows
+    own_rows = lambda value: lax.dynamic_slice_in_dim(value, in_chunk, chip_rows, 0)
     turned = own_rows(dot(left_cols, grad_full, (0, 0)).astype(half))
     rotated = dot(turned, right_full, (1, 0))
     home_moment = beta_one * home[2].astype(jnp.float32) + (1.0 - beta_one) * rotated
     home_second = beta_two * home[3].astype(jnp.float32) + (1.0 - beta_two) * rotated * rotated
     direction = (home_moment / bias_one / (jnp.sqrt(home_second / bias_two) + adam_eps)).astype(half)
     back_rows = dot(direction, right_full, (1, 1)).astype(half)
-
-    results = copies(jnp.where(first, back_rows, rotated.astype(half)), chips)
-    results, grams = lax.optimization_barrier((results, grams))
-    gathered = exchange(results, 0)
-    held = lambda blocks, counts, target: (blocks == target)[None, :] & (
-        counts[None, :] == jnp.arange(slot_cap, dtype=jnp.int32)[:, None]
-    )
-
-    def taken(mask, values):
-        values = jnp.where(mask[:, :, None, None], values[None].astype(jnp.float32), 0.0)
+    grad_cols = lax.dynamic_slice_in_dim(grad_full, chunk * LANES, LANES, 1)
+    chip_grad_rows = lax.dynamic_slice_in_dim(grad_full, chip * chip_rows, chip_rows, 0)
+    left_term = dot(chip_grad_rows, grad_full, (1, 1)).astype(half)
+    right_term = own_rows(dot(grad_cols, grad_full, (0, 0)).astype(half))
+
+    results = jnp.concatenate(
+        [jnp.where(first, back_rows, left_term), right_term, rotated.astype(half)], 0
+    )
+    gathered = exchange_lines(copies(results, y_num))
+
+    def taken(target):
+        mask = (from_owner == target)[None, :] & (
+            number[None, :] == jnp.arange(slot_cap, dtype=jnp.int32)[:, None]
+        )
+        values = jnp.where(mask[:, :, None, None], gathered[None].astype(jnp.float32), 0.0)
         return jnp.sum(values, axis=1).astype(half)
 
-    own_grams = taken(held(assign, numbers, owner), grams)
-    own_grams = own_grams.reshape(slot_cap * 2, 2, row_num, col_num)
-
-    back_full = gathered.reshape(col_num, col_num)
+    back_half = gathered[:, :chip_rows].reshape(-1, col_num)
+    half_rows = back_half.shape[0]
+    for_beside = taken(owner ^ 1).reshape(-1, col_num)
+    beside = swap_x(
+        jnp.concatenate(
+            [jnp.where(first, back_half, for_beside[:half_rows]), for_beside[half_rows:]], 0
+        )
+    )
+    chip_results = taken(owner) + beside.reshape(slot_cap, -1, col_num)
+    back_half = back_half.reshape(y_num, chip_rows, col_num)
+    beside = beside[:half_rows].reshape(back_half.shape)
+    back_full = jnp.where(
+        even, jnp.stack([back_half, beside], 1), jnp.stack([beside, back_half], 1)
+    ).reshape(col_num, col_num)
     chip_update = dot(home[0], back_full, (1, 0)).astype(half)
-    turns = taken(held(assign, numbers, owner), gathered).reshape(slot_cap, 2, row_num, col_num)
-    for_second = jnp.concatenate(
-        [chip_update[row_num:], own_grams[:, 1].reshape(-1, col_num)], 0
-    )
-    turn_rows = slot_cap * row_num
-    for_first = jnp.where(first, for_second[:turn_rows], turns[:, 0].reshape(-1, col_num))
-    came = swap_cores(jnp.concatenate([for_first, for_second[turn_rows:]], 0))
+    chip_results = chip_results.reshape(slot_cap, 3, 2, row_num, col_num)
+    for_first = chip_results[:, :, 0].reshape(-1, col_num)
+    for_second = jnp.concatenate([chip_update[row_num:], for_first[row_num:]], 0)
+    came = swap_cores(jnp.where(first, for_second, for_first))
     update = jnp.where(first, chip_update[:row_num], came[:row_num])
-    grams = jnp.where(first, own_grams[:, 0], came[row_num:].reshape(own_grams[:, 0].shape))
-    grams = grams.reshape(slot_cap, 2, row_num, col_num).astype(jnp.float32)
-    turns = jnp.where(first, came[:turn_rows].reshape(turns[:, 0].shape), turns[:, 1])
-    turns = turns.astype(jnp.float32)
-
-    new_left = beta_two * left_stat[0] + (1.0 - beta_two) * grams[:, 0]
-    new_right = beta_two * right_stat[0] + (1.0 - beta_two) * grams[:, 1]
-    new_moment = beta_one * moment[0] + (1.0 - beta_one) * turns
-    new_second = beta_two * second[0] + (1.0 - beta_two) * turns * turns
+    terms = jnp.where(
+        first, came.reshape(slot_cap, 3, row_num, col_num), chip_results[:, :, 1]
+    ).astype(jnp.float32)
+
+    new_left = beta_two * left_stat[0] + (1.0 - beta_two) * terms[:, 0]
+    new_right = beta_two * right_stat[0] + (1.0 - beta_two) * terms[:, 1]
+    new_moment = beta_one * moment[0] + (1.0 - beta_one) * terms[:, 2]
+    new_second = beta_two * second[0] + (1.0 - beta_two) * terms[:, 2] * terms[:, 2]
     return (update[None], new_left[None], new_right[None], new_moment[None], new_second[None])
 
 

time: 133 us -> 123 us (0.925)
  starting transfers between devices: 54.5 us -> 42.9 us
  waiting for transfers between devices: 57.1 us -> 61.1 us
    all_to_all x2 -> x0, waiting for transfers between devices: 17.4 us -> none  [exchange(): lax.all_to_all(pieces, ('dp', 'owner'), 0, 0, axis_index_groups=groups)]
    all_to_all x1 -> x2, waiting for transfers between devices: 14.6 us -> 29.6 us  [exchange_lines(): lax.all_to_all(pieces, ('dp', 'owner'), 0, 0, axis_index_groups=groups)]
    all_to_all x2 -> x0, starting transfers between devices: 13.8 us -> none  [exchange(): lax.all_to_all(pieces, ('dp', 'owner'), 0, 0, axis_index_groups=groups)]
    ppermute x3, starting transfers between devices: 22.8 us -> 12.8 us  [swap_cores(): lax.ppermute(value, 'dp', [(i, i ^ 1) for i in range(lax.axis_size('dp'))])]
    all_to_all x1 -> x2, starting transfers between devices: 7.07 us -> 15.9 us  [exchange_lines(): lax.all_to_all(pieces, ('dp', 'owner'), 0, 0, axis_index_groups=groups)]
    ppermute x1 -> x2, waiting for transfers between devices: 8.68 us -> 14.4 us  [swap_x(): return lax.ppermute(value, ('dp', 'owner'), pairs)]
    ppermute x1 -> x2, starting transfers between devices: 1.92 us -> 5.31 us  [swap_x(): return lax.ppermute(value, ('dp', 'owner'), pairs)]
  transfers between devices with their start and end apart: 8 -> 8, of which waited for: 7 -> 7; matrix products, arithmetic and copies ran while one was open for 5% -> 3% of each run, Pallas kernels for 0% -> 0%
where the time goes in v9:
time: 123 us; the launch traced here: 122 us
  waiting for transfers between devices  61.1 us (50%)
  starting transfers between devices  42.9 us (35%)
  other arithmetic  8.02 us (7%)
  between operations  3.85 us (3%)
  local copies, waits for them, and re-layouts  2.96 us (2%)
  Pallas kernels  1.92 us (2%)
  matrix products  1.44 us (1%)
    all_to_all x2, waiting for transfers between devices, exchange_lines(): lax.all_to_all(pieces, ('dp', 'owner'), 0, 0, axis_index_groups=groups)  29.6 us
    all_to_all x2, starting transfers between devices, exchange_lines(): lax.all_to_all(pieces, ('dp', 'owner'), 0, 0, axis_index_groups=groups)  15.9 us
    ppermute x2, waiting for transfers between devices, swap_x(): return lax.ppermute(value, ('dp', 'owner'), pairs)  14.4 us
    all_to_all x1, waiting for transfers between devices, exchange_dp(): return lax.all_to_all(pieces, 'dp', 0, 0, axis_index_groups=groups)  13.5 us
    ppermute x3, starting transfers between devices, swap_cores(): lax.ppermute(value, 'dp', [(i, i ^ 1) for i in range(lax.axis_size('dp'))])  12.8 us
    all_to_all x1, starting transfers between devices, exchange_dp(): return lax.all_to_all(pieces, 'dp', 0, 0, axis_index_groups=groups)  8.94 us
    ppermute x2, starting transfers between devices, swap_x(): return lax.ppermute(value, ('dp', 'owner'), pairs)  5.31 us
    ppermute x3, waiting for transfers between devices, swap_cores(): lax.ppermute(value, 'dp', [(i, i ^ 1) for i in range(lax.axis_size('dp'))])  3.59 us
  transfers between devices with their start and end apart: 8, of which 7 were waited for; matrix products, arithmetic and copies ran while one was open for 3% of the time, Pallas kernels for 0%

profile of v9, /device:TPU:1, one launch (start us, length us, event | category | flops | bytes accessed | tf_op | source)
XLA Modules:
  0.0 122.2 jit_solution(13559064127167194631)
XLA Ops:
  0.7 1.9 %first_payload.1 = bf16[512,512]{1,0:T(8,128)(2,1)} custom-call(s32[1]{0:T(128)} %bitcast.1.core, bf16[1,1,512,512]{3,2,1,0:T(8,128)(2,1)} %grads.1, bf16[1,3,16,512]{3,2,1,0:T(8,128)(2,1)} %left.1, bf16[1,3,16,512]{3,2,1,0:T(8,128)(2,1)} %right.1, f32[1,3,16,512]{3,2,1,0:T(8,128)} %moment.1, f32[1,3,16,512]{3,2,1,0:T(8,128)} %second.1), custom_call_target="tpu_custom_call" | custom-call | tf_op jit(solution)/shard_map/first_payload/pallas_call | solution.py:108
  2.6 8.9 %collective-permute-start = (bf16[512,512]{1,0:T(8,128)(2,1)}, bf16[512,512]{1,0:T(8,128)(2,1)S(1)}, u32[]{:S(2)}, u32[]{:S(2)}) collective-permute-start(bf16[512,512]{1,0:T(8,128)(2,1)} %first_payload.1), channel_id=1, source_target_pairs={{0,16},{16,0},{32,48},{48,32},{64,80},{80,64},{96,112},{112,96},{1... | collective-permute-start | bytes 1572872 | tf_op jit(solution)/shard_map/ppermute | solution.py:27
  11.6 0.7 reshape.333
  12.3 0.9 convert_reduce_fusion
  13.6 1.0 convert_bitcast_fusion
  15.0 1.9 %collective-permute-start.1 = (bf16[384,512]{1,0:T(8,128)(2,1)S(1)}, bf16[384,512]{1,0:T(8,128)(2,1)S(1)}, u32[]{:S(2)}, u32[]{:S(2)}) collective-permute-start(bf16[384,512]{1,0:T(8,128)(2,1)S(1)} %pad_maximum_fusion.2), channel_id=1, source_target_pairs={{0,32},{16,17},{1,33},{17,16},{2,34},{18,19},{3,35},{19,18},{4,36}... | collective-permute-start | bytes 1179656 | tf_op jit(solution)/shard_map/ppermute | solution.py:64
  17.0 8.7 %collective-permute-done.1 = bf16[384,512]{1,0:T(8,128)(2,1)S(1)} collective-permute-done((bf16[384,512]{1,0:T(8,128)(2,1)S(1)}, bf16[384,512]{1,0:T(8,128)(2,1)S(1)}, u32[]{:S(2)}, u32[]{:S(2)}) %collective-permute-start.1) | collective-permute-done | bytes 393248 | tf_op jit(solution)/shard_map/ppermute | solution.py:64
  26.3 1.0 pad_maximum_fusion
  27.4 7.2 %all-to-all-start = ((bf16[8,128,512]{2,1,0:T(8,128)(2,1)}), bf16[8,128,512]{2,1,0:T(8,128)(2,1)S(1)}, u32[]{:S(2)}, u32[]{:S(2)}) async-start(bf16[8,128,512]{2,1,0:T(8,128)(2,1)} %pad_maximum_fusion), calls=%async_computation | async-start | bytes 2097152 | tf_op jit(solution)/shard_map/all_to_all | solution.py:53
  37.8 14.6 %all-to-all-done = bf16[8,128,512]{2,1,0:T(8,128)(2,1)S(1)} async-done(((bf16[8,128,512]{2,1,0:T(8,128)(2,1)}), bf16[8,128,512]{2,1,0:T(8,128)(2,1)S(1)}, u32[]{:S(2)}, u32[]{:S(2)}) %all-to-all-start) | async-done | bytes 1048608 | tf_op jit(solution)/shard_map/all_to_all | solution.py:53
  52.6 0.9 pad_maximum_fusion.1
  53.5 8.9 %all-to-all-start.1 = ((bf16[16,32,640]{2,1,0:T(8,128)(2,1)}), bf16[16,32,640]{2,1,0:T(8,128)(2,1)S(1)}, u32[]{:S(2)}, u32[]{:S(2)}) async-start(bf16[16,32,640]{2,1,0:T(8,128)(2,1)} %pad_maximum_fusion.1), calls=%async_computation.1 | async-start | bytes 1310720 | tf_op jit(solution)/shard_map/all_to_all | solution.py:37
  62.5 13.5 %all-to-all-done.1 = bf16[16,32,640]{2,1,0:T(8,128)(2,1)S(1)} async-done(((bf16[16,32,640]{2,1,0:T(8,128)(2,1)}), bf16[16,32,640]{2,1,0:T(8,128)(2,1)S(1)}, u32[]{:S(2)}, u32[]{:S(2)}) %all-to-all-start.1) | async-done | bytes 655392 | tf_op jit(solution)/shard_map/all_to_all | solution.py:37
  76.1 1.9 %collective-permute-start.2 = (bf16[640,640]{1,0:T(8,128)(2,1)S(1)}, bf16[640,640]{1,0:T(8,128)(2,1)S(1)}, u32[]{:S(2)}, u32[]{:S(2)}) collective-permute-start(bf16[640,640]{1,0:T(8,128)(2,1)S(1)} %maximum_maximum_fusion), channel_id=1, source_target_pairs={{0,16},{16,0},{32,48},{48,32},{64,80},{80,64},{96,112},{112,96},{1... | collective-permute-start | bytes 2457608 | tf_op jit(solution)/shard_map/ppermute | solution.py:27
  78.1 2.3 %collective-permute-done.2 = bf16[640,640]{1,0:T(8,128)(2,1)S(1)} collective-permute-done((bf16[640,640]{1,0:T(8,128)(2,1)S(1)}, bf16[640,640]{1,0:T(8,128)(2,1)S(1)}, u32[]{:S(2)}, u32[]{:S(2)}) %collective-permute-start.2) | collective-permute-done | bytes 819232 | tf_op jit(solution)/shard_map/ppermute | solution.py:27
  81.7 1.0 broadcast_in_dim.161
  82.7 8.7 %all-to-all-start.2 = ((bf16[8,96,512]{2,1,0:T(8,128)(2,1)}), bf16[8,96,512]{2,1,0:T(8,128)(2,1)S(1)}, u32[]{:S(2)}, u32[]{:S(2)}) async-start(bf16[8,96,512]{2,1,0:T(8,128)(2,1)} %broadcast_in_dim.161), calls=%async_computation.2 | async-start | bytes 1572864 | tf_op jit(solution)/shard_map/all_to_all | solution.py:53
  91.4 15.0 %all-to-all-done.2 = bf16[8,96,512]{2,1,0:T(8,128)(2,1)S(1)} async-done(((bf16[8,96,512]{2,1,0:T(8,128)(2,1)}), bf16[8,96,512]{2,1,0:T(8,128)(2,1)S(1)}, u32[]{:S(2)}, u32[]{:S(2)}) %all-to-all-start.2) | async-done | bytes 786464 | tf_op jit(solution)/shard_map/all_to_all | solution.py:53
  106.6 1.1 select_reduce_fusion.1
  107.9 3.4 %collective-permute-start.3 = (bf16[288,512]{1,0:T(8,128)(2,1)S(1)}, bf16[288,512]{1,0:T(8,128)(2,1)S(1)}, u32[]{:S(2)}, u32[]{:S(2)}) collective-permute-start(bf16[288,512]{1,0:T(8,128)(2,1)S(1)} %pad_maximum_fusion.3), channel_id=1, source_target_pairs={{0,32},{16,17},{1,33},{17,16},{2,34},{18,19},{3,35},{19,18},{4,36}... | collective-permute-start | bytes 884744 | tf_op jit(solution)/shard_map/ppermute | solution.py:64
  111.3 5.7 %collective-permute-done.3 = bf16[288,512]{1,0:T(8,128)(2,1)S(1)} collective-permute-done((bf16[288,512]{1,0:T(8,128)(2,1)S(1)}, bf16[288,512]{1,0:T(8,128)(2,1)S(1)}, u32[]{:S(2)}, u32[]{:S(2)}) %collective-permute-start.3) | collective-permute-done | bytes 294944 | tf_op jit(solution)/shard_map/ppermute | solution.py:64
  117.5 1.9 %collective-permute-start.4 = (bf16[144,512]{1,0:T(8,128)(2,1)S(1)}, bf16[144,512]{1,0:T(8,128)(2,1)S(1)}, u32[]{:S(2)}, u32[]{:S(2)}) collective-permute-start(bf16[144,512]{1,0:T(8,128)(2,1)S(1)} %maximum_select_fusion.1), channel_id=1, source_target_pairs={{0,16},{16,0},{32,48},{48,32},{64,80},{80,64},{96,112},{112,96},{1... | collective-permute-start | bytes 442376 | tf_op jit(solution)/shard_map/ppermute | solution.py:27
  119.4 1.3 %collective-permute-done.4 = bf16[144,512]{1,0:T(8,128)(2,1)S(1)} collective-permute-done((bf16[144,512]{1,0:T(8,128)(2,1)S(1)}, bf16[144,512]{1,0:T(8,128)(2,1)S(1)}, u32[]{:S(2)}, u32[]{:S(2)}) %collective-permute-start.4) | collective-permute-done | bytes 147488 | tf_op jit(solution)/shard_map/ppermute | solution.py:27
  120.8 0.8 fusion.14
  (69 shorter events, 5.0 us)
Async XLA Ops:
  0.6 13.9 %copy-start.4 = (bf16[1,3,16,512]{3,2,1,0:T(8,128)(2,1)S(1)}, bf16[1,3,16,512]{3,2,1,0:T(8,128)(2,1)}, u32[]{:S(2)}) copy-start(bf16[1,3,16,512]{3,2,1,0:T(8,128)(2,1)} %right.1) | copy-start | bytes 147460
  0.6 13.9 %copy-start.3 = (bf16[1,3,16,512]{3,2,1,0:T(8,128)(2,1)S(1)}, bf16[1,3,16,512]{3,2,1,0:T(8,128)(2,1)}, u32[]{:S(2)}) copy-start(bf16[1,3,16,512]{3,2,1,0:T(8,128)(2,1)} %left.1) | copy-start | bytes 147460
  2.6 12.1 %copy-start = (bf16[1,1,512,512]{3,2,1,0:T(8,128)(2,1)S(1)}, bf16[1,1,512,512]{3,2,1,0:T(8,128)(2,1)}, u32[]{:S(2)}) copy-start(bf16[1,1,512,512]{3,2,1,0:T(8,128)(2,1)} %grads.1) | copy-start | bytes 1572868
  2.6 12.0 %collective-permute-start = (bf16[512,512]{1,0:T(8,128)(2,1)}, bf16[512,512]{1,0:T(8,128)(2,1)S(1)}, u32[]{:S(2)}, u32[]{:S(2)}) collective-permute-start(bf16[512,512]{1,0:T(8,128)(2,1)} %first_payload.1), channel_id=1, source_target_pairs={{0,16},{16,0},{32,48},{48,32},{64,80},{80,64},{96,112},{112,96},{1... | collective-permute-start | bytes 1572872 | tf_op jit(solution)/shard_map/ppermute | solution.py:27
  15.0 10.6 %collective-permute-start.1 = (bf16[384,512]{1,0:T(8,128)(2,1)S(1)}, bf16[384,512]{1,0:T(8,128)(2,1)S(1)}, u32[]{:S(2)}, u32[]{:S(2)}) collective-permute-start(bf16[384,512]{1,0:T(8,128)(2,1)S(1)} %pad_maximum_fusion.2), channel_id=1, source_target_pairs={{0,32},{16,17},{1,33},{17,16},{2,34},{18,19},{3,35},{19,18},{4,36}... | collective-permute-start | bytes 1179656 | tf_op jit(solution)/shard_map/ppermute | solution.py:64
  27.4 7.2 %copy-start.7 = (s32[16]{0:T(128)S(1)}, s32[16]{0:T(128)}, u32[]{:S(2)}) copy-start(s32[16]{0:T(128)} %param.9) | copy-start | bytes 196
  27.4 25.0 %all-to-all-start = ((bf16[8,128,512]{2,1,0:T(8,128)(2,1)}), bf16[8,128,512]{2,1,0:T(8,128)(2,1)S(1)}, u32[]{:S(2)}, u32[]{:S(2)}) async-start(bf16[8,128,512]{2,1,0:T(8,128)(2,1)} %pad_maximum_fusion), calls=%async_computation | async-start | bytes 2097152 | tf_op jit(solution)/shard_map/all_to_all | solution.py:53
  53.5 22.5 %all-to-all-start.1 = ((bf16[16,32,640]{2,1,0:T(8,128)(2,1)}), bf16[16,32,640]{2,1,0:T(8,128)(2,1)S(1)}, u32[]{:S(2)}, u32[]{:S(2)}) async-start(bf16[16,32,640]{2,1,0:T(8,128)(2,1)} %pad_maximum_fusion.1), calls=%async_computation.1 | async-start | bytes 1310720 | tf_op jit(solution)/shard_map/all_to_all | solution.py:37
  76.1 4.2 %collective-permute-start.2 = (bf16[640,640]{1,0:T(8,128)(2,1)S(1)}, bf16[640,640]{1,0:T(8,128)(2,1)S(1)}, u32[]{:S(2)}, u32[]{:S(2)}) collective-permute-start(bf16[640,640]{1,0:T(8,128)(2,1)S(1)} %maximum_maximum_fusion), channel_id=1, source_target_pairs={{0,16},{16,0},{32,48},{48,32},{64,80},{80,64},{96,112},{112,96},{1... | collective-permute-start | bytes 2457608 | tf_op jit(solution)/shard_map/ppermute | solution.py:27
  82.7 23.7 %all-to-all-start.2 = ((bf16[8,96,512]{2,1,0:T(8,128)(2,1)}), bf16[8,96,512]{2,1,0:T(8,128)(2,1)S(1)}, u32[]{:S(2)}, u32[]{:S(2)}) async-start(bf16[8,96,512]{2,1,0:T(8,128)(2,1)} %broadcast_in_dim.161), calls=%async_computation.2 | async-start | bytes 1572864 | tf_op jit(solution)/shard_map/all_to_all | solution.py:53
  107.9 9.1 %collective-permute-start.3 = (bf16[288,512]{1,0:T(8,128)(2,1)S(1)}, bf16[288,512]{1,0:T(8,128)(2,1)S(1)}, u32[]{:S(2)}, u32[]{:S(2)}) collective-permute-start(bf16[288,512]{1,0:T(8,128)(2,1)S(1)} %pad_maximum_fusion.3), channel_id=1, source_target_pairs={{0,32},{16,17},{1,33},{17,16},{2,34},{18,19},{3,35},{19,18},{4,36}... | collective-permute-start | bytes 884744 | tf_op jit(solution)/shard_map/ppermute | solution.py:64
  117.1 3.7 %copy-start.1 = (f32[1,3,16,512]{3,2,1,0:T(8,128)S(1)}, f32[1,3,16,512]{3,2,1,0:T(8,128)}, u32[]{:S(2)}) copy-start(f32[1,3,16,512]{3,2,1,0:T(8,128)} %moment.1) | copy-start | bytes 294916
  117.1 3.7 %copy-start.2 = (f32[1,3,16,512]{3,2,1,0:T(8,128)S(1)}, f32[1,3,16,512]{3,2,1,0:T(8,128)}, u32[]{:S(2)}) copy-start(f32[1,3,16,512]{3,2,1,0:T(8,128)} %second.1) | copy-start | bytes 294916
  117.1 3.7 %copy-start.5 = (f32[1,3,16,512]{3,2,1,0:T(8,128)S(1)}, f32[1,3,16,512]{3,2,1,0:T(8,128)}, u32[]{:S(2)}) copy-start(f32[1,3,16,512]{3,2,1,0:T(8,128)} %param.12) | copy-start | bytes 294916
  117.1 3.7 %copy-start.6 = (f32[1,3,16,512]{3,2,1,0:T(8,128)S(1)}, f32[1,3,16,512]{3,2,1,0:T(8,128)}, u32[]{:S(2)}) copy-start(f32[1,3,16,512]{3,2,1,0:T(8,128)} %param.13) | copy-start | bytes 294916
  117.5 3.3 %collective-permute-start.4 = (bf16[144,512]{1,0:T(8,128)(2,1)S(1)}, bf16[144,512]{1,0:T(8,128)(2,1)S(1)}, u32[]{:S(2)}, u32[]{:S(2)}) collective-permute-start(bf16[144,512]{1,0:T(8,128)(2,1)S(1)} %maximum_select_fusion.1), channel_id=1, source_target_pairs={{0,16},{16,0},{32,48},{48,32},{64,80},{80,64},{96,112},{112,96},{1... | collective-permute-start | bytes 442376 | tf_op jit(solution)/shard_map/ppermute | solution.py:27

commit v10 on v9

--- a/solution.py
+++ b/solution.py
@@ -61,6 +61,17 @@
         for owner in range(owners):
             pairs.append((place(chip, 0, owner), place(chip ^ 1, 0, owner)))
             pairs.append((place(chip, 1, owner), place(chip, 1, owner ^ 1)))
+    return lax.ppermute(value, ("dp", "owner"), pairs)
+
+
+def swap_across(value):
+    chips = lax.axis_size("dp") // 2
+    owners = lax.axis_size("owner")
+    pairs = []
+    for chip in range(chips):
+        for owner in range(owners):
+            pairs.append((place(chip, 0, owner), place(chip ^ 1, 1, owner)))
+            pairs.append((place(chip, 1, owner), place(chip, 0, owner ^ 1)))
     return lax.ppermute(value, ("dp", "owner"), pairs)
 
 
@@ -237,28 +248,32 @@
         return jnp.sum(values, axis=1).astype(half)
 
     back_half = gathered[:, :chip_rows].reshape(-1, col_num)
-    half_rows = back_half.shape[0]
-    for_beside = taken(owner ^ 1).reshape(-1, col_num)
-    beside = swap_x(
-        jnp.concatenate(
-            [jnp.where(first, back_half, for_beside[:half_rows]), for_beside[half_rows:]], 0
-        )
-    )
-    chip_results = taken(owner) + beside.reshape(slot_cap, -1, col_num)
-    back_half = back_half.reshape(y_num, chip_rows, col_num)
-    beside = beside[:half_rows].reshape(back_half.shape)
+    own = taken(owner).reshape(slot_cap, 3, 2, row_num, col_num)
+    of_beside = taken(owner ^ 1).reshape(own.shape)
+    result_rows = slot_cap * 3 * row_num
+
+    def either(values):
+        values = values.reshape(-1, col_num)
+        return jnp.concatenate(
+            [jnp.where(first, back_half[:result_rows], values), back_half[result_rows:]], 0
+        )
+
+    beside = swap_x(either(of_beside[:, :, 1]))
+    across = swap_across(either(of_beside[:, :, 0]))
+    came = swap_cores(either(own[:, :, 0]))
+    terms = jnp.where(
+        first,
+        came[:result_rows] + across[:result_rows],
+        own[:, :, 1].reshape(-1, col_num) + beside[:result_rows],
+    )
+    terms = terms.reshape(slot_cap, 3, row_num, col_num).astype(jnp.float32)
+    back_half = jnp.where(first, back_half, came).reshape(y_num, chip_rows, col_num)
+    beside = jnp.where(first, beside, across).reshape(back_half.shape)
     back_full = jnp.where(
         even, jnp.stack([back_half, beside], 1), jnp.stack([beside, back_half], 1)
     ).reshape(col_num, col_num)
-    chip_update = dot(home[0], back_full, (1, 0)).astype(half)
-    chip_results = chip_results.reshape(slot_cap, 3, 2, row_num, col_num)
-    for_first = chip_results[:, :, 0].reshape(-1, col_num)
-    for_second = jnp.concatenate([chip_update[row_num:], for_first[row_num:]], 0)
-    came = swap_cores(jnp.where(first, for_second, for_first))
-    update = jnp.where(first, chip_update[:row_num], came[:row_num])
-    terms = jnp.where(
-        first, came.reshape(slot_cap, 3, row_num, col_num), chip_results[:, :, 1]
-    ).astype(jnp.float32)
+    left_rows = jnp.where(first, home[0, :row_num], home[0, row_num:])
+    update = dot(left_rows, back_full, (1, 0)).astype(half)
 
     new_left = beta_two * left_stat[0] + (1.0 - beta_two) * terms[:, 0]
     new_right = beta_two * right_stat[0] + (1.0 - beta_two) * terms[:, 1]

time: 123 us -> 128 us (1.041)
  starting transfers between devices: 42.9 us -> 45.6 us
  waiting for transfers between devices: 61.1 us -> 63.3 us
    ppermute x0 -> x1, waiting for transfers between devices: none -> 4 us  [swap_across(): return lax.ppermute(value, ('dp', 'owner'), pairs)]
    ppermute x0 -> x1, starting transfers between devices: none -> 2.67 us  [swap_across(): return lax.ppermute(value, ('dp', 'owner'), pairs)]
    ppermute x3, waiting for transfers between devices: 3.59 us -> 2.26 us  [swap_cores(): lax.ppermute(value, 'dp', [(i, i ^ 1) for i in range(lax.axis_size('dp'))])]
  transfers between devices with their start and end apart: 8 -> 9, of which waited for: 7 -> 7; matrix products, arithmetic and copies ran while one was open for 3% -> 3% of each run, Pallas kernels for 0% -> 0%
where the time goes in v10:
time: 128 us; the launch traced here: 127 us
  waiting for transfers between devices  63.3 us (49%)
  starting transfers between devices  45.6 us (36%)
  other arithmetic  7.44 us (6%)
  between operations  3.82 us (3%)
  local copies, waits for them, and re-layouts  2.98 us (2%)
  matrix products  2.05 us (2%)
  Pallas kernels  1.92 us (2%)
    all_to_all x2, waiting for transfers between devices, exchange_lines(): lax.all_to_all(pieces, ('dp', 'owner'), 0, 0, axis_index_groups=groups)  29.6 us
    all_to_all x2, starting transfers between devices, exchange_lines(): lax.all_to_all(pieces, ('dp', 'owner'), 0, 0, axis_index_groups=groups)  15.9 us
    ppermute x2, waiting for transfers between devices, swap_x(): return lax.ppermute(value, ('dp', 'owner'), pairs)  13.9 us
    all_to_all x1, waiting for transfers between devices, exchange_dp(): return lax.all_to_all(pieces, 'dp', 0, 0, axis_index_groups=groups)  13.5 us
    ppermute x3, starting transfers between devices, swap_cores(): lax.ppermute(value, 'dp', [(i, i ^ 1) for i in range(lax.axis_size('dp'))])  12.8 us
    all_to_all x1, starting transfers between devices, exchange_dp(): return lax.all_to_all(pieces, 'dp', 0, 0, axis_index_groups=groups)  8.94 us
    ppermute x2, starting transfers between devices, swap_x(): return lax.ppermute(value, ('dp', 'owner'), pairs)  5.31 us
    ppermute x1, waiting for transfers between devices, swap_across(): return lax.ppermute(value, ('dp', 'owner'), pairs)  4 us
  transfers between devices with their start and end apart: 9, of which 7 were waited for; matrix products, arithmetic and copies ran while one was open for 3% of the time, Pallas kernels for 0%

profile of v10, /device:TPU:1, one launch (start us, length us, event | category | flops | bytes accessed | tf_op | source)
XLA Modules:
  0.0 127.1 jit_solution(3655819017481671532)
XLA Ops:
  0.7 1.9 %first_payload.1 = bf16[512,512]{1,0:T(8,128)(2,1)} custom-call(s32[1]{0:T(128)} %bitcast.1.core, bf16[1,1,512,512]{3,2,1,0:T(8,128)(2,1)} %grads.1, bf16[1,3,16,512]{3,2,1,0:T(8,128)(2,1)} %left.1, bf16[1,3,16,512]{3,2,1,0:T(8,128)(2,1)} %right.1, f32[1,3,16,512]{3,2,1,0:T(8,128)} %moment.1, f32[1,3,16,512]{3,2,1,0:T(8,128)} %second.1), custom_call_target="tpu_custom_call" | custom-call | tf_op jit(solution)/shard_map/first_payload/pallas_call | solution.py:119
  2.6 8.9 %collective-permute-start = (bf16[512,512]{1,0:T(8,128)(2,1)}, bf16[512,512]{1,0:T(8,128)(2,1)S(1)}, u32[]{:S(2)}, u32[]{:S(2)}) collective-permute-start(bf16[512,512]{1,0:T(8,128)(2,1)} %first_payload.1), channel_id=1, source_target_pairs={{0,16},{16,0},{32,48},{48,32},{64,80},{80,64},{96,112},{112,96},{1... | collective-permute-start | bytes 1572872 | tf_op jit(solution)/shard_map/ppermute | solution.py:27
  12.3 0.9 convert_reduce_fusion
  13.5 1.0 convert_bitcast_fusion
  15.0 1.9 %collective-permute-start.1 = (bf16[384,512]{1,0:T(8,128)(2,1)S(1)}, bf16[384,512]{1,0:T(8,128)(2,1)S(1)}, u32[]{:S(2)}, u32[]{:S(2)}) collective-permute-start(bf16[384,512]{1,0:T(8,128)(2,1)S(1)} %pad_maximum_fusion.2), channel_id=1, source_target_pairs={{0,32},{16,17},{1,33},{17,16},{2,34},{18,19},{3,35},{19,18},{4,36}... | collective-permute-start | bytes 1179656 | tf_op jit(solution)/shard_map/ppermute | solution.py:64
  16.9 8.7 %collective-permute-done.1 = bf16[384,512]{1,0:T(8,128)(2,1)S(1)} collective-permute-done((bf16[384,512]{1,0:T(8,128)(2,1)S(1)}, bf16[384,512]{1,0:T(8,128)(2,1)S(1)}, u32[]{:S(2)}, u32[]{:S(2)}) %collective-permute-start.1) | collective-permute-done | bytes 393248 | tf_op jit(solution)/shard_map/ppermute | solution.py:64
  26.3 1.1 pad_maximum_fusion
  27.4 7.2 %all-to-all-start = ((bf16[8,128,512]{2,1,0:T(8,128)(2,1)}), bf16[8,128,512]{2,1,0:T(8,128)(2,1)S(1)}, u32[]{:S(2)}, u32[]{:S(2)}) async-start(bf16[8,128,512]{2,1,0:T(8,128)(2,1)} %pad_maximum_fusion), calls=%async_computation | async-start | bytes 2097152 | tf_op jit(solution)/shard_map/all_to_all | solution.py:53
  37.8 14.6 %all-to-all-done = bf16[8,128,512]{2,1,0:T(8,128)(2,1)S(1)} async-done(((bf16[8,128,512]{2,1,0:T(8,128)(2,1)}), bf16[8,128,512]{2,1,0:T(8,128)(2,1)S(1)}, u32[]{:S(2)}, u32[]{:S(2)}) %all-to-all-start) | async-done | bytes 1048608 | tf_op jit(solution)/shard_map/all_to_all | solution.py:53
  52.6 0.9 pad_maximum_fusion.1
  53.5 8.9 %all-to-all-start.1 = ((bf16[16,32,640]{2,1,0:T(8,128)(2,1)}), bf16[16,32,640]{2,1,0:T(8,128)(2,1)S(1)}, u32[]{:S(2)}, u32[]{:S(2)}) async-start(bf16[16,32,640]{2,1,0:T(8,128)(2,1)} %pad_maximum_fusion.1), calls=%async_computation.1 | async-start | bytes 1310720 | tf_op jit(solution)/shard_map/all_to_all | solution.py:37
  62.5 13.5 %all-to-all-done.1 = bf16[16,32,640]{2,1,0:T(8,128)(2,1)S(1)} async-done(((bf16[16,32,640]{2,1,0:T(8,128)(2,1)}), bf16[16,32,640]{2,1,0:T(8,128)(2,1)S(1)}, u32[]{:S(2)}, u32[]{:S(2)}) %all-to-all-start.1) | async-done | bytes 655392 | tf_op jit(solution)/shard_map/all_to_all | solution.py:37
  76.1 1.9 %collective-permute-start.2 = (bf16[640,640]{1,0:T(8,128)(2,1)S(1)}, bf16[640,640]{1,0:T(8,128)(2,1)S(1)}, u32[]{:S(2)}, u32[]{:S(2)}) collective-permute-start(bf16[640,640]{1,0:T(8,128)(2,1)S(1)} %maximum_maximum_fusion), channel_id=1, source_target_pairs={{0,16},{16,0},{32,48},{48,32},{64,80},{80,64},{96,112},{112,96},{1... | collective-permute-start | bytes 2457608 | tf_op jit(solution)/shard_map/ppermute | solution.py:27
  78.1 2.3 %collective-permute-done.2 = bf16[640,640]{1,0:T(8,128)(2,1)S(1)} collective-permute-done((bf16[640,640]{1,0:T(8,128)(2,1)S(1)}, bf16[640,640]{1,0:T(8,128)(2,1)S(1)}, u32[]{:S(2)}, u32[]{:S(2)}) %collective-permute-start.2) | collective-permute-done | bytes 819232 | tf_op jit(solution)/shard_map/ppermute | solution.py:27
  81.7 1.0 broadcast_in_dim.161
  82.7 8.7 %all-to-all-start.2 = ((bf16[8,96,512]{2,1,0:T(8,128)(2,1)}), bf16[8,96,512]{2,1,0:T(8,128)(2,1)S(1)}, u32[]{:S(2)}, u32[]{:S(2)}) async-start(bf16[8,96,512]{2,1,0:T(8,128)(2,1)} %broadcast_in_dim.161), calls=%async_computation.2 | async-start | bytes 1572864 | tf_op jit(solution)/shard_map/all_to_all | solution.py:53
  91.4 15.0 %all-to-all-done.2 = bf16[8,96,512]{2,1,0:T(8,128)(2,1)S(1)} async-done(((bf16[8,96,512]{2,1,0:T(8,128)(2,1)}), bf16[8,96,512]{2,1,0:T(8,128)(2,1)S(1)}, u32[]{:S(2)}, u32[]{:S(2)}) %all-to-all-start.2) | async-done | bytes 786464 | tf_op jit(solution)/shard_map/all_to_all | solution.py:53
  106.7 1.1 select_reduce_fusion.1
  108.0 1.9 %collective-permute-start.3 = (bf16[256,512]{1,0:T(8,128)(2,1)S(1)}, bf16[256,512]{1,0:T(8,128)(2,1)S(1)}, u32[]{:S(2)}, u32[]{:S(2)}) collective-permute-start(bf16[256,512]{1,0:T(8,128)(2,1)S(1)} %get-tuple-element.28), channel_id=1, source_target_pairs={{0,16},{16,0},{32,48},{48,32},{64,80},{80,64},{96,112},{112,96},{1... | collective-permute-start | bytes 786440 | tf_op jit(solution)/shard_map/ppermute | solution.py:27
  109.9 3.4 %collective-permute-start.4 = (bf16[256,512]{1,0:T(8,128)(2,1)S(1)}, bf16[256,512]{1,0:T(8,128)(2,1)S(1)}, u32[]{:S(2)}, u32[]{:S(2)}) collective-permute-start(bf16[256,512]{1,0:T(8,128)(2,1)S(1)} %get-tuple-element.29), channel_id=1, source_target_pairs={{0,32},{16,17},{1,33},{17,16},{2,34},{18,19},{3,35},{19,18},{4,36}... | collective-permute-start | bytes 786440 | tf_op jit(solution)/shard_map/ppermute | solution.py:64
  113.3 2.7 %collective-permute-start.5 = (bf16[256,512]{1,0:T(8,128)(2,1)S(1)}, bf16[256,512]{1,0:T(8,128)(2,1)S(1)}, u32[]{:S(2)}, u32[]{:S(2)}) collective-permute-start(bf16[256,512]{1,0:T(8,128)(2,1)S(1)} %get-tuple-element.30), channel_id=1, source_target_pairs={{0,48},{16,1},{1,49},{17,0},{2,50},{18,3},{3,51},{19,2},{4,52},{20... | collective-permute-start | bytes 786440 | tf_op jit(solution)/shard_map/ppermute | solution.py:75
  116.0 5.3 %collective-permute-done.4 = bf16[256,512]{1,0:T(8,128)(2,1)S(1)} collective-permute-done((bf16[256,512]{1,0:T(8,128)(2,1)S(1)}, bf16[256,512]{1,0:T(8,128)(2,1)S(1)}, u32[]{:S(2)}, u32[]{:S(2)}) %collective-permute-start.4) | collective-permute-done | bytes 262176 | tf_op jit(solution)/shard_map/ppermute | solution.py:64
  121.2 4.0 %collective-permute-done.5 = bf16[256,512]{1,0:T(8,128)(2,1)S(1)} collective-permute-done((bf16[256,512]{1,0:T(8,128)(2,1)S(1)}, bf16[256,512]{1,0:T(8,128)(2,1)S(1)}, u32[]{:S(2)}, u32[]{:S(2)}) %collective-permute-start.5) | collective-permute-done | bytes 262176 | tf_op jit(solution)/shard_map/ppermute | solution.py:75
  125.5 0.8 fusion.1
  (69 shorter events, 5.8 us)
Async XLA Ops:
  0.6 13.9 %copy-start.4 = (bf16[1,3,16,512]{3,2,1,0:T(8,128)(2,1)S(1)}, bf16[1,3,16,512]{3,2,1,0:T(8,128)(2,1)}, u32[]{:S(2)}) copy-start(bf16[1,3,16,512]{3,2,1,0:T(8,128)(2,1)} %right.1) | copy-start | bytes 147460
  0.6 13.9 %copy-start.3 = (bf16[1,3,16,512]{3,2,1,0:T(8,128)(2,1)S(1)}, bf16[1,3,16,512]{3,2,1,0:T(8,128)(2,1)}, u32[]{:S(2)}) copy-start(bf16[1,3,16,512]{3,2,1,0:T(8,128)(2,1)} %left.1) | copy-start | bytes 147460
  2.6 12.1 %copy-start = (bf16[1,1,512,512]{3,2,1,0:T(8,128)(2,1)S(1)}, bf16[1,1,512,512]{3,2,1,0:T(8,128)(2,1)}, u32[]{:S(2)}) copy-start(bf16[1,1,512,512]{3,2,1,0:T(8,128)(2,1)} %grads.1) | copy-start | bytes 1572868
  2.6 12.0 %collective-permute-start = (bf16[512,512]{1,0:T(8,128)(2,1)}, bf16[512,512]{1,0:T(8,128)(2,1)S(1)}, u32[]{:S(2)}, u32[]{:S(2)}) collective-permute-start(bf16[512,512]{1,0:T(8,128)(2,1)} %first_payload.1), channel_id=1, source_target_pairs={{0,16},{16,0},{32,48},{48,32},{64,80},{80,64},{96,112},{112,96},{1... | collective-permute-start | bytes 1572872 | tf_op jit(solution)/shard_map/ppermute | solution.py:27
  15.0 10.6 %collective-permute-start.1 = (bf16[384,512]{1,0:T(8,128)(2,1)S(1)}, bf16[384,512]{1,0:T(8,128)(2,1)S(1)}, u32[]{:S(2)}, u32[]{:S(2)}) collective-permute-start(bf16[384,512]{1,0:T(8,128)(2,1)S(1)} %pad_maximum_fusion.2), channel_id=1, source_target_pairs={{0,32},{16,17},{1,33},{17,16},{2,34},{18,19},{3,35},{19,18},{4,36}... | collective-permute-start | bytes 1179656 | tf_op jit(solution)/shard_map/ppermute | solution.py:64
  27.4 7.2 %copy-start.7 = (s32[16]{0:T(128)S(1)}, s32[16]{0:T(128)}, u32[]{:S(2)}) copy-start(s32[16]{0:T(128)} %param.9) | copy-start | bytes 196
  27.4 25.0 %all-to-all-start = ((bf16[8,128,512]{2,1,0:T(8,128)(2,1)}), bf16[8,128,512]{2,1,0:T(8,128)(2,1)S(1)}, u32[]{:S(2)}, u32[]{:S(2)}) async-start(bf16[8,128,512]{2,1,0:T(8,128)(2,1)} %pad_maximum_fusion), calls=%async_computation | async-start | bytes 2097152 | tf_op jit(solution)/shard_map/all_to_all | solution.py:53
  53.5 22.5 %all-to-all-start.1 = ((bf16[16,32,640]{2,1,0:T(8,128)(2,1)}), bf16[16,32,640]{2,1,0:T(8,128)(2,1)S(1)}, u32[]{:S(2)}, u32[]{:S(2)}) async-start(bf16[16,32,640]{2,1,0:T(8,128)(2,1)} %pad_maximum_fusion.1), calls=%async_computation.1 | async-start | bytes 1310720 | tf_op jit(solution)/shard_map/all_to_all | solution.py:37
  76.1 4.2 %collective-permute-start.2 = (bf16[640,640]{1,0:T(8,128)(2,1)S(1)}, bf16[640,640]{1,0:T(8,128)(2,1)S(1)}, u32[]{:S(2)}, u32[]{:S(2)}) collective-permute-start(bf16[640,640]{1,0:T(8,128)(2,1)S(1)} %maximum_maximum_fusion), channel_id=1, source_target_pairs={{0,16},{16,0},{32,48},{48,32},{64,80},{80,64},{96,112},{112,96},{1... | collective-permute-start | bytes 2457608 | tf_op jit(solution)/shard_map/ppermute | solution.py:27
  82.7 23.7 %all-to-all-start.2 = ((bf16[8,96,512]{2,1,0:T(8,128)(2,1)}), bf16[8,96,512]{2,1,0:T(8,128)(2,1)S(1)}, u32[]{:S(2)}, u32[]{:S(2)}) async-start(bf16[8,96,512]{2,1,0:T(8,128)(2,1)} %broadcast_in_dim.161), calls=%async_computation.2 | async-start | bytes 1572864 | tf_op jit(solution)/shard_map/all_to_all | solution.py:53
  108.0 8.0 %collective-permute-start.3 = (bf16[256,512]{1,0:T(8,128)(2,1)S(1)}, bf16[256,512]{1,0:T(8,128)(2,1)S(1)}, u32[]{:S(2)}, u32[]{:S(2)}) collective-permute-start(bf16[256,512]{1,0:T(8,128)(2,1)S(1)} %get-tuple-element.28), channel_id=1, source_target_pairs={{0,16},{16,0},{32,48},{48,32},{64,80},{80,64},{96,112},{112,96},{1... | collective-permute-start | bytes 786440 | tf_op jit(solution)/shard_map/ppermute | solution.py:27
  109.9 11.3 %collective-permute-start.4 = (bf16[256,512]{1,0:T(8,128)(2,1)S(1)}, bf16[256,512]{1,0:T(8,128)(2,1)S(1)}, u32[]{:S(2)}, u32[]{:S(2)}) collective-permute-start(bf16[256,512]{1,0:T(8,128)(2,1)S(1)} %get-tuple-element.29), channel_id=1, source_target_pairs={{0,32},{16,17},{1,33},{17,16},{2,34},{18,19},{3,35},{19,18},{4,36}... | collective-permute-start | bytes 786440 | tf_op jit(solution)/shard_map/ppermute | solution.py:64
  113.3 11.9 %collective-permute-start.5 = (bf16[256,512]{1,0:T(8,128)(2,1)S(1)}, bf16[256,512]{1,0:T(8,128)(2,1)S(1)}, u32[]{:S(2)}, u32[]{:S(2)}) collective-permute-start(bf16[256,512]{1,0:T(8,128)(2,1)S(1)} %get-tuple-element.30), channel_id=1, source_target_pairs={{0,48},{16,1},{1,49},{17,0},{2,50},{18,3},{3,51},{19,2},{4,52},{20... | collective-permute-start | bytes 786440 | tf_op jit(solution)/shard_map/ppermute | solution.py:75
  125.3 1.0 copy-start.1
  125.3 1.0 copy-start.2
  125.3 1.0 copy-start.5
  125.4 1.0 copy-start.6

commit v11 on v9

--- a/solution.py
+++ b/solution.py
@@ -64,55 +64,57 @@
     return lax.ppermute(value, ("dp", "owner"), pairs)
 
 
-def first_payload_kernel(core, grads, left, right, moment, second, payload, wide, sems):
+def first_payload_kernel(core, grads, left, right, moment, second, slots, payload, wide, sems):
     slot_cap, row_num = left.shape[1:3]
+    moves = []
+    for slot in range(slot_cap):
+        for kind, basis in enumerate((left, right)):
+            moves.append(
+                pltpu.make_async_copy(
+                    basis.at[0, slot], slots.at[slot, kind], sems.at[slot * 2 + kind]
+                )
+            )
+    for kind, state in enumerate((moment, second)):
+        moves.append(
+            pltpu.make_async_copy(state.at[0], wide.at[kind], sems.at[2 * slot_cap + kind])
+        )
+    for move in moves:
+        move.start()
+
+    @pl.when(core[0] != 0)
+    def _():
+        move = pltpu.make_async_copy(grads.at[0, 0], payload, sems.at[2 * slot_cap + 2])
+        move.start()
+        move.wait()
+
+    for move in moves:
+        move.wait()
+    for slot in range(slot_cap):
+        for kind in range(2):
+            slots[slot, 2 + kind] = wide[kind, slot].astype(half)
 
     @pl.when(core[0] == 0)
     def _():
-        moves = []
         for slot in range(slot_cap):
-            for kind, basis in enumerate((left, right)):
-                moves.append(
-                    pltpu.make_async_copy(
-                        basis.at[0, slot],
-                        payload.at[pl.ds((slot * 4 + kind) * row_num, row_num)],
-                        sems.at[slot * 2 + kind],
-                    )
-                )
-        for kind, state in enumerate((moment, second)):
-            moves.append(
-                pltpu.make_async_copy(
-                    state.at[0], wide.at[kind], sems.at[2 * slot_cap + kind]
-                )
-            )
-        for move in moves:
-            move.start()
-        for move in moves:
-            move.wait()
-        for slot in range(slot_cap):
-            for kind in range(2):
-                payload[pl.ds((slot * 4 + 2 + kind) * row_num, row_num)] = wide[
-                    kind, slot
-                ].astype(half)
-
-    @pl.when(core[0] != 0)
-    def _():
-        move = pltpu.make_async_copy(grads.at[0, 0], payload, sems.at[0])
-        move.start()
-        move.wait()
+            for kind in range(4):
+                payload[pl.ds((slot * 4 + kind) * row_num, row_num)] = slots[slot, kind]
 
 
 def first_payload(core, grads, left, right, moment, second):
     slot_cap, row_num, col_num = left.shape[1:]
     anywhere = pl.BlockSpec(memory_space=pl.ANY)
+    vmem = pl.BlockSpec(memory_space=pltpu.VMEM)
     return pl.pallas_call(
         first_payload_kernel,
-        out_shape=jax.ShapeDtypeStruct(grads.shape[2:], half),
+        out_shape=(
+            jax.ShapeDtypeStruct((slot_cap, 4, row_num, col_num), half),
+            jax.ShapeDtypeStruct(grads.shape[2:], half),
+        ),
         in_specs=[pl.BlockSpec(memory_space=pltpu.SMEM)] + [anywhere] * 5,
-        out_specs=pl.BlockSpec(memory_space=pltpu.VMEM),
+        out_specs=(vmem, vmem),
         scratch_shapes=[
             pltpu.VMEM((2, slot_cap, row_num, col_num), jnp.float32),
-            pltpu.SemaphoreType.DMA((2 * slot_cap + 2,)),
+            pltpu.SemaphoreType.DMA((2 * slot_cap + 3,)),
         ],
         compiler_params=pltpu.CompilerParams(vmem_limit_bytes=60 * 1024 * 1024),
         name="first_payload",
@@ -145,15 +147,10 @@
     kinds = 4
 
     grads = grad_parts[0, 0]
-    came = swap_cores(
-        first_payload(
-            (row_index % 2).reshape(1), grad_parts, left_basis, right_basis, moment, second
-        )
-    )
-    slots = jnp.stack(
-        [left_basis[0], right_basis[0], moment[0].astype(half), second[0].astype(half)], 1
-    )
-    numbers = slot_numbers(assign)
+    slots, payload = first_payload(
+        (row_index % 2).reshape(1), grad_parts, left_basis, right_basis, moment, second
+    )
+    came = swap_cores(payload)
 
     y_num = chips // 2
     z_num = owner_num // 2
@@ -166,11 +163,12 @@
     chip_slots = jnp.stack([came[:slot_rows].reshape(slots.shape), slots], 2)
     chip_slots = chip_slots.reshape(slot_cap * kinds * chip_rows, col_num)
     sent_num = sent.shape[0]
-    beside = swap_x(
-        jnp.concatenate(
-            [jnp.where(first, sent, chip_slots[:sent_num]), chip_slots[sent_num:]], 0
-        )
-    )
+    payload = jnp.concatenate(
+        [jnp.where(first, sent, chip_slots[:sent_num]), chip_slots[sent_num:]], 0
+    )
+    payload, assign = lax.optimization_barrier((payload, assign))
+    beside = swap_x(payload)
+    numbers = slot_numbers(assign)
     sums = kept.astype(jnp.float32) + beside[:sent_num].reshape(kept.shape).astype(jnp.float32)
     sums = sums.astype(half)
 
@@ -233,8 +231,10 @@
         mask = (from_owner == target)[None, :] & (
             number[None, :] == jnp.arange(slot_cap, dtype=jnp.int32)[:, None]
         )
-        values = jnp.where(mask[:, :, None, None], gathered[None].astype(jnp.float32), 0.0)
-        return jnp.sum(values, axis=1).astype(half)
+        values = jnp.zeros((slot_cap,) + gathered.shape[1:], half)
+        for home_z in range(z_num):
+            values = jnp.where(mask[:, home_z, None, None], gathered[home_z][None], values)
+        return values
 
     back_half = gathered[:, :chip_rows].reshape(-1, col_num)
     half_rows = back_half.shape[0]

time: 123 us -> 123 us (level)
  other arithmetic: 8.02 us -> 6.54 us
  local copies, waits for them, and re-layouts: 2.96 us -> 4.29 us
    ppermute x3, waiting for transfers between devices: 3.59 us -> 5.26 us  [swap_cores(): lax.ppermute(value, 'dp', [(i, i ^ 1) for i in range(lax.axis_size('dp'))])]
    all_to_all x2, waiting for transfers between devices: 29.6 us -> 28.2 us  [exchange_lines(): lax.all_to_all(pieces, ('dp', 'owner'), 0, 0, axis_index_groups=groups)]
    broadcast_in_dim x0 -> x18, local copies, waits for them, and re-layouts: none -> 1.31 us  [taken(): jnp.where(mask[:, home_z, None, None], gathered[home_z][None], values)]
  transfers between devices with their start and end apart: 8 -> 8, of which waited for: 7 -> 8; matrix products, arithmetic and copies ran while one was open for 3% -> 2% of each run, Pallas kernels for 0% -> 0%
where the time goes in v11:
time: 123 us; the launch traced here: 122 us
  waiting for transfers between devices  61 us (50%)
  starting transfers between devices  43 us (35%)
  other arithmetic  6.54 us (5%)
  local copies, waits for them, and re-layouts  4.29 us (3%)
  between operations  3.86 us (3%)
  Pallas kernels  2.21 us (2%)
  matrix products  1.44 us (1%)
    all_to_all x2, waiting for transfers between devices, exchange_lines(): lax.all_to_all(pieces, ('dp', 'owner'), 0, 0, axis_index_groups=groups)  28.2 us
    all_to_all x2, starting transfers between devices, exchange_lines(): lax.all_to_all(pieces, ('dp', 'owner'), 0, 0, axis_index_groups=groups)  15.5 us
    all_to_all x1, waiting for transfers between devices, exchange_dp(): return lax.all_to_all(pieces, 'dp', 0, 0, axis_index_groups=groups)  13.9 us
    ppermute x2, waiting for transfers between devices, swap_x(): return lax.ppermute(value, ('dp', 'owner'), pairs)  13.6 us
    ppermute x3, starting transfers between devices, swap_cores(): lax.ppermute(value, 'dp', [(i, i ^ 1) for i in range(lax.axis_size('dp'))])  12.7 us
    all_to_all x1, starting transfers between devices, exchange_dp(): return lax.all_to_all(pieces, 'dp', 0, 0, axis_index_groups=groups)  8.96 us
    ppermute x2, starting transfers between devices, swap_x(): return lax.ppermute(value, ('dp', 'owner'), pairs)  5.87 us
    ppermute x3, waiting for transfers between devices, swap_cores(): lax.ppermute(value, 'dp', [(i, i ^ 1) for i in range(lax.axis_size('dp'))])  5.26 us
  transfers between devices with their start and end apart: 8, of which 8 were waited for; matrix products, arithmetic and copies ran while one was open for 2% of the time, Pallas kernels for 0%

profile of v11, /device:TPU:1, one launch (start us, length us, event | category | flops | bytes accessed | tf_op | source)
XLA Modules:
  0.0 122.3 jit_solution(6760059944981280170)
XLA Ops:
  0.6 2.2 %first_payload.1 = (bf16[3,4,16,512]{3,2,1,0:T(8,128)(2,1)}, bf16[512,512]{1,0:T(8,128)(2,1)}) custom-call(s32[1]{0:T(128)} %bitcast.1.core, bf16[1,1,512,512]{3,2,1,0:T(8,128)(2,1)} %grads.1, bf16[1,3,16,512]{3,2,1,0:T(8,128)(2,1)} %left.1, bf16[1,3,16,512]{3,2,1,0:T(8,128)(2,1)} %right.1, f32[1,3,16,512]{3,2,1,0:T(8,128)} %moment.1, f32[1,3,16,512]{3,2,1,0:T(8,128)} %second.1), custom_call_target="tpu_custom_call" | custom-call | tf_op jit(solution)/shard_map/first_payload/pallas_call | solution.py:107
  2.9 8.7 %collective-permute-start = (bf16[512,512]{1,0:T(8,128)(2,1)}, bf16[512,512]{1,0:T(8,128)(2,1)S(1)}, u32[]{:S(2)}, u32[]{:S(2)}) collective-permute-start(bf16[512,512]{1,0:T(8,128)(2,1)} %get-tuple-element.9), channel_id=1, source_target_pairs={{0,16},{16,0},{32,48},{48,32},{64,80},{80,64},{96,112},{112,96},{1... | collective-permute-start | bytes 1572872 | tf_op jit(solution)/shard_map/ppermute | solution.py:27
  11.7 1.7 %collective-permute-done = bf16[512,512]{1,0:T(8,128)(2,1)S(1)} collective-permute-done((bf16[512,512]{1,0:T(8,128)(2,1)}, bf16[512,512]{1,0:T(8,128)(2,1)S(1)}, u32[]{:S(2)}, u32[]{:S(2)}) %collective-permute-start) | collective-permute-done | bytes 524320 | tf_op jit(solution)/shard_map/ppermute | solution.py:27
  13.4 1.0 fusion.10
  15.5 1.9 %collective-permute-start.1 = (bf16[384,512]{1,0:T(8,128)(2,1)S(1)}, bf16[384,512]{1,0:T(8,128)(2,1)S(1)}, u32[]{:S(2)}, u32[]{:S(2)}) collective-permute-start(bf16[384,512]{1,0:T(8,128)(2,1)S(1)} %pad_maximum_fusion.2), channel_id=1, source_target_pairs={{0,32},{16,17},{1,33},{17,16},{2,34},{18,19},{3,35},{19,18},{4,36}... | collective-permute-start | bytes 1179656 | tf_op jit(solution)/shard_map/ppermute | solution.py:64
  17.8 8.1 %collective-permute-done.1 = bf16[384,512]{1,0:T(8,128)(2,1)S(1)} collective-permute-done((bf16[384,512]{1,0:T(8,128)(2,1)S(1)}, bf16[384,512]{1,0:T(8,128)(2,1)S(1)}, u32[]{:S(2)}, u32[]{:S(2)}) %collective-permute-start.1) | collective-permute-done | bytes 393248 | tf_op jit(solution)/shard_map/ppermute | solution.py:64
  26.6 1.1 pad_maximum_fusion
  27.7 7.1 %all-to-all-start = ((bf16[8,128,512]{2,1,0:T(8,128)(2,1)}), bf16[8,128,512]{2,1,0:T(8,128)(2,1)S(1)}, u32[]{:S(2)}, u32[]{:S(2)}) async-start(bf16[8,128,512]{2,1,0:T(8,128)(2,1)} %pad_maximum_fusion), calls=%async_computation | async-start | bytes 2097152 | tf_op jit(solution)/shard_map/all_to_all | solution.py:53
  34.8 0.6 dynamic_slice.28
  38.0 14.6 %all-to-all-done = bf16[8,128,512]{2,1,0:T(8,128)(2,1)S(1)} async-done(((bf16[8,128,512]{2,1,0:T(8,128)(2,1)}), bf16[8,128,512]{2,1,0:T(8,128)(2,1)S(1)}, u32[]{:S(2)}, u32[]{:S(2)}) %all-to-all-start) | async-done | bytes 1048608 | tf_op jit(solution)/shard_map/all_to_all | solution.py:53
  52.8 0.9 pad_maximum_fusion.1
  53.7 9.0 %all-to-all-start.1 = ((bf16[16,32,640]{2,1,0:T(8,128)(2,1)}), bf16[16,32,640]{2,1,0:T(8,128)(2,1)S(1)}, u32[]{:S(2)}, u32[]{:S(2)}) async-start(bf16[16,32,640]{2,1,0:T(8,128)(2,1)} %pad_maximum_fusion.1), calls=%async_computation.1 | async-start | bytes 1310720 | tf_op jit(solution)/shard_map/all_to_all | solution.py:37
  62.7 13.9 %all-to-all-done.1 = bf16[16,32,640]{2,1,0:T(8,128)(2,1)S(1)} async-done(((bf16[16,32,640]{2,1,0:T(8,128)(2,1)}), bf16[16,32,640]{2,1,0:T(8,128)(2,1)S(1)}, u32[]{:S(2)}, u32[]{:S(2)}) %all-to-all-start.1) | async-done | bytes 655392 | tf_op jit(solution)/shard_map/all_to_all | solution.py:37
  76.8 1.9 %collective-permute-start.2 = (bf16[640,640]{1,0:T(8,128)(2,1)S(1)}, bf16[640,640]{1,0:T(8,128)(2,1)S(1)}, u32[]{:S(2)}, u32[]{:S(2)}) collective-permute-start(bf16[640,640]{1,0:T(8,128)(2,1)S(1)} %maximum_maximum_fusion), channel_id=1, source_target_pairs={{0,16},{16,0},{32,48},{48,32},{64,80},{80,64},{96,112},{112,96},{1... | collective-permute-start | bytes 2457608 | tf_op jit(solution)/shard_map/ppermute | solution.py:27
  78.7 2.3 %collective-permute-done.2 = bf16[640,640]{1,0:T(8,128)(2,1)S(1)} collective-permute-done((bf16[640,640]{1,0:T(8,128)(2,1)S(1)}, bf16[640,640]{1,0:T(8,128)(2,1)S(1)}, u32[]{:S(2)}, u32[]{:S(2)}) %collective-permute-start.2) | collective-permute-done | bytes 819232 | tf_op jit(solution)/shard_map/ppermute | solution.py:27
  82.4 0.9 broadcast_in_dim.406
  83.3 8.3 %all-to-all-start.2 = ((bf16[8,96,512]{2,1,0:T(8,128)(2,1)}), bf16[8,96,512]{2,1,0:T(8,128)(2,1)S(1)}, u32[]{:S(2)}, u32[]{:S(2)}) async-start(bf16[8,96,512]{2,1,0:T(8,128)(2,1)} %broadcast_in_dim.406), calls=%async_computation.2 | async-start | bytes 1572864 | tf_op jit(solution)/shard_map/all_to_all | solution.py:53
  93.0 13.6 %all-to-all-done.2 = bf16[8,96,512]{2,1,0:T(8,128)(2,1)S(1)} async-done(((bf16[8,96,512]{2,1,0:T(8,128)(2,1)}), bf16[8,96,512]{2,1,0:T(8,128)(2,1)S(1)}, u32[]{:S(2)}, u32[]{:S(2)}) %all-to-all-start.2) | async-done | bytes 786464 | tf_op jit(solution)/shard_map/all_to_all | solution.py:53
  107.3 4.0 %collective-permute-start.3 = (bf16[288,512]{1,0:T(8,128)(2,1)S(1)}, bf16[288,512]{1,0:T(8,128)(2,1)S(1)}, u32[]{:S(2)}, u32[]{:S(2)}) collective-permute-start(bf16[288,512]{1,0:T(8,128)(2,1)S(1)} %pad_maximum_fusion.3), channel_id=1, source_target_pairs={{0,32},{16,17},{1,33},{17,16},{2,34},{18,19},{3,35},{19,18},{4,36}... | collective-permute-start | bytes 884744 | tf_op jit(solution)/shard_map/ppermute | solution.py:64
  111.3 5.5 %collective-permute-done.3 = bf16[288,512]{1,0:T(8,128)(2,1)S(1)} collective-permute-done((bf16[288,512]{1,0:T(8,128)(2,1)S(1)}, bf16[288,512]{1,0:T(8,128)(2,1)S(1)}, u32[]{:S(2)}, u32[]{:S(2)}) %collective-permute-start.3) | collective-permute-done | bytes 294944 | tf_op jit(solution)/shard_map/ppermute | solution.py:64
  117.5 2.1 %collective-permute-start.4 = (bf16[144,512]{1,0:T(8,128)(2,1)S(1)}, bf16[144,512]{1,0:T(8,128)(2,1)S(1)}, u32[]{:S(2)}, u32[]{:S(2)}) collective-permute-start(bf16[144,512]{1,0:T(8,128)(2,1)S(1)} %maximum_select_fusion.1), channel_id=1, source_target_pairs={{0,16},{16,0},{32,48},{48,32},{64,80},{80,64},{96,112},{112,96},{1... | collective-permute-start | bytes 442376 | tf_op jit(solution)/shard_map/ppermute | solution.py:27
  119.5 1.3 %collective-permute-done.4 = bf16[144,512]{1,0:T(8,128)(2,1)S(1)} collective-permute-done((bf16[144,512]{1,0:T(8,128)(2,1)S(1)}, bf16[144,512]{1,0:T(8,128)(2,1)S(1)}, u32[]{:S(2)}, u32[]{:S(2)}) %collective-permute-start.4) | collective-permute-done | bytes 147488 | tf_op jit(solution)/shard_map/ppermute | solution.py:27
  120.9 0.8 fusion.21
  121.7 0.6 fusion.48
  (87 shorter events, 6.4 us)
Async XLA Ops:
  2.9 11.5 %copy-start.1 = (bf16[3,4,16,512]{3,2,1,0:T(8,128)(2,1)S(1)}, bf16[3,4,16,512]{3,2,1,0:T(8,128)(2,1)}, u32[]{:S(2)}) copy-start(bf16[3,4,16,512]{3,2,1,0:T(8,128)(2,1)} %get-tuple-element.10) | copy-start | bytes 589828
  2.9 10.5 %collective-permute-start = (bf16[512,512]{1,0:T(8,128)(2,1)}, bf16[512,512]{1,0:T(8,128)(2,1)S(1)}, u32[]{:S(2)}, u32[]{:S(2)}) collective-permute-start(bf16[512,512]{1,0:T(8,128)(2,1)} %get-tuple-element.9), channel_id=1, source_target_pairs={{0,16},{16,0},{32,48},{48,32},{64,80},{80,64},{96,112},{112,96},{1... | collective-permute-start | bytes 1572872 | tf_op jit(solution)/shard_map/ppermute | solution.py:27
  13.3 1.1 copy-start
  14.6 0.7 copy-start.6
  15.5 10.4 %collective-permute-start.1 = (bf16[384,512]{1,0:T(8,128)(2,1)S(1)}, bf16[384,512]{1,0:T(8,128)(2,1)S(1)}, u32[]{:S(2)}, u32[]{:S(2)}) collective-permute-start(bf16[384,512]{1,0:T(8,128)(2,1)S(1)} %pad_maximum_fusion.2), channel_id=1, source_target_pairs={{0,32},{16,17},{1,33},{17,16},{2,34},{18,19},{3,35},{19,18},{4,36}... | collective-permute-start | bytes 1179656 | tf_op jit(solution)/shard_map/ppermute | solution.py:64
  27.7 25.0 %all-to-all-start = ((bf16[8,128,512]{2,1,0:T(8,128)(2,1)}), bf16[8,128,512]{2,1,0:T(8,128)(2,1)S(1)}, u32[]{:S(2)}, u32[]{:S(2)}) async-start(bf16[8,128,512]{2,1,0:T(8,128)(2,1)} %pad_maximum_fusion), calls=%async_computation | async-start | bytes 2097152 | tf_op jit(solution)/shard_map/all_to_all | solution.py:53
  53.7 22.9 %all-to-all-start.1 = ((bf16[16,32,640]{2,1,0:T(8,128)(2,1)}), bf16[16,32,640]{2,1,0:T(8,128)(2,1)S(1)}, u32[]{:S(2)}, u32[]{:S(2)}) async-start(bf16[16,32,640]{2,1,0:T(8,128)(2,1)} %pad_maximum_fusion.1), calls=%async_computation.1 | async-start | bytes 1310720 | tf_op jit(solution)/shard_map/all_to_all | solution.py:37
  76.8 4.2 %collective-permute-start.2 = (bf16[640,640]{1,0:T(8,128)(2,1)S(1)}, bf16[640,640]{1,0:T(8,128)(2,1)S(1)}, u32[]{:S(2)}, u32[]{:S(2)}) collective-permute-start(bf16[640,640]{1,0:T(8,128)(2,1)S(1)} %maximum_maximum_fusion), channel_id=1, source_target_pairs={{0,16},{16,0},{32,48},{48,32},{64,80},{80,64},{96,112},{112,96},{1... | collective-permute-start | bytes 2457608 | tf_op jit(solution)/shard_map/ppermute | solution.py:27
  83.3 23.3 %all-to-all-start.2 = ((bf16[8,96,512]{2,1,0:T(8,128)(2,1)}), bf16[8,96,512]{2,1,0:T(8,128)(2,1)S(1)}, u32[]{:S(2)}, u32[]{:S(2)}) async-start(bf16[8,96,512]{2,1,0:T(8,128)(2,1)} %broadcast_in_dim.406), calls=%async_computation.2 | async-start | bytes 1572864 | tf_op jit(solution)/shard_map/all_to_all | solution.py:53
  107.3 9.5 %collective-permute-start.3 = (bf16[288,512]{1,0:T(8,128)(2,1)S(1)}, bf16[288,512]{1,0:T(8,128)(2,1)S(1)}, u32[]{:S(2)}, u32[]{:S(2)}) collective-permute-start(bf16[288,512]{1,0:T(8,128)(2,1)S(1)} %pad_maximum_fusion.3), channel_id=1, source_target_pairs={{0,32},{16,17},{1,33},{17,16},{2,34},{18,19},{3,35},{19,18},{4,36}... | collective-permute-start | bytes 884744 | tf_op jit(solution)/shard_map/ppermute | solution.py:64
  117.3 3.6 %copy-start.2 = (f32[1,3,16,512]{3,2,1,0:T(8,128)S(1)}, f32[1,3,16,512]{3,2,1,0:T(8,128)}, u32[]{:S(2)}) copy-start(f32[1,3,16,512]{3,2,1,0:T(8,128)} %moment.1) | copy-start | bytes 294916
  117.3 3.6 %copy-start.3 = (f32[1,3,16,512]{3,2,1,0:T(8,128)S(1)}, f32[1,3,16,512]{3,2,1,0:T(8,128)}, u32[]{:S(2)}) copy-start(f32[1,3,16,512]{3,2,1,0:T(8,128)} %second.1) | copy-start | bytes 294916
  117.3 3.6 %copy-start.4 = (f32[1,3,16,512]{3,2,1,0:T(8,128)S(1)}, f32[1,3,16,512]{3,2,1,0:T(8,128)}, u32[]{:S(2)}) copy-start(f32[1,3,16,512]{3,2,1,0:T(8,128)} %param.12) | copy-start | bytes 294916
  117.3 3.6 %copy-start.5 = (f32[1,3,16,512]{3,2,1,0:T(8,128)S(1)}, f32[1,3,16,512]{3,2,1,0:T(8,128)}, u32[]{:S(2)}) copy-start(f32[1,3,16,512]{3,2,1,0:T(8,128)} %param.13) | copy-start | bytes 294916
  117.5 3.4 %collective-permute-start.4 = (bf16[144,512]{1,0:T(8,128)(2,1)S(1)}, bf16[144,512]{1,0:T(8,128)(2,1)S(1)}, u32[]{:S(2)}, u32[]{:S(2)}) collective-permute-start(bf16[144,512]{1,0:T(8,128)(2,1)S(1)} %maximum_select_fusion.1), channel_id=1, source_target_pairs={{0,16},{16,0},{32,48},{48,32},{64,80},{80,64},{96,112},{112,96},{1... | collective-permute-start | bytes 442376 | tf_op jit(solution)/shard_map/ppermute | solution.py:27

commit v12 on v11

--- a/solution.py
+++ b/solution.py
@@ -166,7 +166,6 @@
     payload = jnp.concatenate(
         [jnp.where(first, sent, chip_slots[:sent_num]), chip_slots[sent_num:]], 0
     )
-    payload, assign = lax.optimization_barrier((payload, assign))
     beside = swap_x(payload)
     numbers = slot_numbers(assign)
     sums = kept.astype(jnp.float32) + beside[:sent_num].reshape(kept.shape).astype(jnp.float32)

time: 123 us -> 122 us (level)
  waiting for transfers between devices: 61 us -> 59.6 us
    ppermute x3, waiting for transfers between devices: 5.26 us -> 3.59 us  [swap_cores(): lax.ppermute(value, 'dp', [(i, i ^ 1) for i in range(lax.axis_size('dp'))])]
  transfers between devices with their start and end apart: 8 -> 8, of which waited for: 8 -> 7; matrix products, arithmetic and copies ran while one was open for 2% -> 3% of each run, Pallas kernels for 0% -> 0%
where the time goes in v12:
time: 122 us
  waiting for transfers between devices  59.6 us (49%)
  starting transfers between devices  43 us (35%)
  other arithmetic  7.26 us (6%)
  local copies, waits for them, and re-layouts  4.47 us (4%)
  between operations  3.86 us (3%)
  Pallas kernels  2.21 us (2%)
  matrix products  1.44 us (1%)
    all_to_all x2, waiting for transfers between devices, exchange_lines(): lax.all_to_all(pieces, ('dp', 'owner'), 0, 0, axis_index_groups=groups)  28.2 us
    all_to_all x2, starting transfers between devices, exchange_lines(): lax.all_to_all(pieces, ('dp', 'owner'), 0, 0, axis_index_groups=groups)  15.9 us
    ppermute x2, waiting for transfers between devices, swap_x(): return lax.ppermute(value, ('dp', 'owner'), pairs)  14.3 us
    all_to_all x1, waiting for transfers between devices, exchange_dp(): return lax.all_to_all(pieces, 'dp', 0, 0, axis_index_groups=groups)  13.5 us
    ppermute x3, starting transfers between devices, swap_cores(): lax.ppermute(value, 'dp', [(i, i ^ 1) for i in range(lax.axis_size('dp'))])  12.7 us
    all_to_all x1, starting transfers between devices, exchange_dp(): return lax.all_to_all(pieces, 'dp', 0, 0, axis_index_groups=groups)  9.07 us
    ppermute x2, starting transfers between devices, swap_x(): return lax.ppermute(value, ('dp', 'owner'), pairs)  5.36 us
    ppermute x3, waiting for transfers between devices, swap_cores(): lax.ppermute(value, 'dp', [(i, i ^ 1) for i in range(lax.axis_size('dp'))])  3.59 us
  transfers between devices with their start and end apart: 8, of which 7 were waited for; matrix products, arithmetic and copies ran while one was open for 3% of the time, Pallas kernels for 0%

profile of v12, /device:TPU:1, one launch (start us, length us, event | category | flops | bytes accessed | tf_op | source)
XLA Modules:
  0.0 121.9 jit_solution(5242268078492320688)
XLA Ops:
  0.6 2.2 %first_payload.1 = (bf16[3,4,16,512]{3,2,1,0:T(8,128)(2,1)}, bf16[512,512]{1,0:T(8,128)(2,1)}) custom-call(s32[1]{0:T(128)} %bitcast.1.core, bf16[1,1,512,512]{3,2,1,0:T(8,128)(2,1)} %grads.1, bf16[1,3,16,512]{3,2,1,0:T(8,128)(2,1)} %left.1, bf16[1,3,16,512]{3,2,1,0:T(8,128)(2,1)} %right.1, f32[1,3,16,512]{3,2,1,0:T(8,128)} %moment.1, f32[1,3,16,512]{3,2,1,0:T(8,128)} %second.1), custom_call_target="tpu_custom_call" | custom-call | tf_op jit(solution)/shard_map/first_payload/pallas_call | solution.py:107
  2.9 8.7 %collective-permute-start = (bf16[512,512]{1,0:T(8,128)(2,1)}, bf16[512,512]{1,0:T(8,128)(2,1)S(1)}, u32[]{:S(2)}, u32[]{:S(2)}) collective-permute-start(bf16[512,512]{1,0:T(8,128)(2,1)} %get-tuple-element.7), channel_id=1, source_target_pairs={{0,16},{16,0},{32,48},{48,32},{64,80},{80,64},{96,112},{112,96},{1... | collective-permute-start | bytes 1572872 | tf_op jit(solution)/shard_map/ppermute | solution.py:27
  11.7 0.7 reshape.291
  12.4 0.9 convert_reduce_fusion
  13.7 1.0 fusion.10
  15.0 1.9 %collective-permute-start.1 = (bf16[384,512]{1,0:T(8,128)(2,1)S(1)}, bf16[384,512]{1,0:T(8,128)(2,1)S(1)}, u32[]{:S(2)}, u32[]{:S(2)}) collective-permute-start(bf16[384,512]{1,0:T(8,128)(2,1)S(1)} %pad_maximum_fusion.2), channel_id=1, source_target_pairs={{0,32},{16,17},{1,33},{17,16},{2,34},{18,19},{3,35},{19,18},{4,36}... | collective-permute-start | bytes 1179656 | tf_op jit(solution)/shard_map/ppermute | solution.py:64
  17.1 8.6 %collective-permute-done.1 = bf16[384,512]{1,0:T(8,128)(2,1)S(1)} collective-permute-done((bf16[384,512]{1,0:T(8,128)(2,1)S(1)}, bf16[384,512]{1,0:T(8,128)(2,1)S(1)}, u32[]{:S(2)}, u32[]{:S(2)}) %collective-permute-start.1) | collective-permute-done | bytes 393248 | tf_op jit(solution)/shard_map/ppermute | solution.py:64
  26.3 1.1 pad_maximum_fusion
  27.4 7.2 %all-to-all-start = ((bf16[8,128,512]{2,1,0:T(8,128)(2,1)}), bf16[8,128,512]{2,1,0:T(8,128)(2,1)S(1)}, u32[]{:S(2)}, u32[]{:S(2)}) async-start(bf16[8,128,512]{2,1,0:T(8,128)(2,1)} %pad_maximum_fusion), calls=%async_computation | async-start | bytes 2097152 | tf_op jit(solution)/shard_map/all_to_all | solution.py:53
  37.8 14.6 %all-to-all-done = bf16[8,128,512]{2,1,0:T(8,128)(2,1)S(1)} async-done(((bf16[8,128,512]{2,1,0:T(8,128)(2,1)}), bf16[8,128,512]{2,1,0:T(8,128)(2,1)S(1)}, u32[]{:S(2)}, u32[]{:S(2)}) %all-to-all-start) | async-done | bytes 1048608 | tf_op jit(solution)/shard_map/all_to_all | solution.py:53
  52.6 0.9 pad_maximum_fusion.1
  53.5 9.1 %all-to-all-start.1 = ((bf16[16,32,640]{2,1,0:T(8,128)(2,1)}), bf16[16,32,640]{2,1,0:T(8,128)(2,1)S(1)}, u32[]{:S(2)}, u32[]{:S(2)}) async-start(bf16[16,32,640]{2,1,0:T(8,128)(2,1)} %pad_maximum_fusion.1), calls=%async_computation.1 | async-start | bytes 1310720 | tf_op jit(solution)/shard_map/all_to_all | solution.py:37
  62.6 13.5 %all-to-all-done.1 = bf16[16,32,640]{2,1,0:T(8,128)(2,1)S(1)} async-done(((bf16[16,32,640]{2,1,0:T(8,128)(2,1)}), bf16[16,32,640]{2,1,0:T(8,128)(2,1)S(1)}, u32[]{:S(2)}, u32[]{:S(2)}) %all-to-all-start.1) | async-done | bytes 655392 | tf_op jit(solution)/shard_map/all_to_all | solution.py:37
  76.2 1.9 %collective-permute-start.2 = (bf16[640,640]{1,0:T(8,128)(2,1)S(1)}, bf16[640,640]{1,0:T(8,128)(2,1)S(1)}, u32[]{:S(2)}, u32[]{:S(2)}) collective-permute-start(bf16[640,640]{1,0:T(8,128)(2,1)S(1)} %maximum_maximum_fusion), channel_id=1, source_target_pairs={{0,16},{16,0},{32,48},{48,32},{64,80},{80,64},{96,112},{112,96},{1... | collective-permute-start | bytes 2457608 | tf_op jit(solution)/shard_map/ppermute | solution.py:27
  78.2 2.3 %collective-permute-done.2 = bf16[640,640]{1,0:T(8,128)(2,1)S(1)} collective-permute-done((bf16[640,640]{1,0:T(8,128)(2,1)S(1)}, bf16[640,640]{1,0:T(8,128)(2,1)S(1)}, u32[]{:S(2)}, u32[]{:S(2)}) %collective-permute-start.2) | collective-permute-done | bytes 819232 | tf_op jit(solution)/shard_map/ppermute | solution.py:27
  81.8 0.9 broadcast_in_dim.406
  82.8 8.7 %all-to-all-start.2 = ((bf16[8,96,512]{2,1,0:T(8,128)(2,1)}), bf16[8,96,512]{2,1,0:T(8,128)(2,1)S(1)}, u32[]{:S(2)}, u32[]{:S(2)}) async-start(bf16[8,96,512]{2,1,0:T(8,128)(2,1)} %broadcast_in_dim.406), calls=%async_computation.2 | async-start | bytes 1572864 | tf_op jit(solution)/shard_map/all_to_all | solution.py:53
  92.9 13.6 %all-to-all-done.2 = bf16[8,96,512]{2,1,0:T(8,128)(2,1)S(1)} async-done(((bf16[8,96,512]{2,1,0:T(8,128)(2,1)}), bf16[8,96,512]{2,1,0:T(8,128)(2,1)S(1)}, u32[]{:S(2)}, u32[]{:S(2)}) %all-to-all-start.2) | async-done | bytes 786464 | tf_op jit(solution)/shard_map/all_to_all | solution.py:53
  107.2 3.4 %collective-permute-start.3 = (bf16[288,512]{1,0:T(8,128)(2,1)S(1)}, bf16[288,512]{1,0:T(8,128)(2,1)S(1)}, u32[]{:S(2)}, u32[]{:S(2)}) collective-permute-start(bf16[288,512]{1,0:T(8,128)(2,1)S(1)} %pad_maximum_fusion.3), channel_id=1, source_target_pairs={{0,32},{16,17},{1,33},{17,16},{2,34},{18,19},{3,35},{19,18},{4,36}... | collective-permute-start | bytes 884744 | tf_op jit(solution)/shard_map/ppermute | solution.py:64
  110.7 5.7 %collective-permute-done.3 = bf16[288,512]{1,0:T(8,128)(2,1)S(1)} collective-permute-done((bf16[288,512]{1,0:T(8,128)(2,1)S(1)}, bf16[288,512]{1,0:T(8,128)(2,1)S(1)}, u32[]{:S(2)}, u32[]{:S(2)}) %collective-permute-start.3) | collective-permute-done | bytes 294944 | tf_op jit(solution)/shard_map/ppermute | solution.py:64
  117.0 2.1 %collective-permute-start.4 = (bf16[144,512]{1,0:T(8,128)(2,1)S(1)}, bf16[144,512]{1,0:T(8,128)(2,1)S(1)}, u32[]{:S(2)}, u32[]{:S(2)}) collective-permute-start(bf16[144,512]{1,0:T(8,128)(2,1)S(1)} %maximum_select_fusion.1), channel_id=1, source_target_pairs={{0,16},{16,0},{32,48},{48,32},{64,80},{80,64},{96,112},{112,96},{1... | collective-permute-start | bytes 442376 | tf_op jit(solution)/shard_map/ppermute | solution.py:27
  119.1 1.3 %collective-permute-done.4 = bf16[144,512]{1,0:T(8,128)(2,1)S(1)} collective-permute-done((bf16[144,512]{1,0:T(8,128)(2,1)S(1)}, bf16[144,512]{1,0:T(8,128)(2,1)S(1)}, u32[]{:S(2)}, u32[]{:S(2)}) %collective-permute-start.4) | collective-permute-done | bytes 147488 | tf_op jit(solution)/shard_map/ppermute | solution.py:27
  120.5 0.8 fusion.21
  121.3 0.6 fusion.48
  (87 shorter events, 6.2 us)
Async XLA Ops:
  2.9 11.8 %copy-start.1 = (bf16[3,4,16,512]{3,2,1,0:T(8,128)(2,1)S(1)}, bf16[3,4,16,512]{3,2,1,0:T(8,128)(2,1)}, u32[]{:S(2)}) copy-start(bf16[3,4,16,512]{3,2,1,0:T(8,128)(2,1)} %get-tuple-element.8) | copy-start | bytes 589828
  2.9 10.7 %collective-permute-start = (bf16[512,512]{1,0:T(8,128)(2,1)}, bf16[512,512]{1,0:T(8,128)(2,1)S(1)}, u32[]{:S(2)}, u32[]{:S(2)}) collective-permute-start(bf16[512,512]{1,0:T(8,128)(2,1)} %get-tuple-element.7), channel_id=1, source_target_pairs={{0,16},{16,0},{32,48},{48,32},{64,80},{80,64},{96,112},{112,96},{1... | collective-permute-start | bytes 1572872 | tf_op jit(solution)/shard_map/ppermute | solution.py:27
  13.6 1.1 copy-start
  15.0 10.6 %collective-permute-start.1 = (bf16[384,512]{1,0:T(8,128)(2,1)S(1)}, bf16[384,512]{1,0:T(8,128)(2,1)S(1)}, u32[]{:S(2)}, u32[]{:S(2)}) collective-permute-start(bf16[384,512]{1,0:T(8,128)(2,1)S(1)} %pad_maximum_fusion.2), channel_id=1, source_target_pairs={{0,32},{16,17},{1,33},{17,16},{2,34},{18,19},{3,35},{19,18},{4,36}... | collective-permute-start | bytes 1179656 | tf_op jit(solution)/shard_map/ppermute | solution.py:64
  27.4 7.2 %copy-start.6 = (s32[16]{0:T(128)S(1)}, s32[16]{0:T(128)}, u32[]{:S(2)}) copy-start(s32[16]{0:T(128)} %param.9) | copy-start | bytes 196
  27.4 25.0 %all-to-all-start = ((bf16[8,128,512]{2,1,0:T(8,128)(2,1)}), bf16[8,128,512]{2,1,0:T(8,128)(2,1)S(1)}, u32[]{:S(2)}, u32[]{:S(2)}) async-start(bf16[8,128,512]{2,1,0:T(8,128)(2,1)} %pad_maximum_fusion), calls=%async_computation | async-start | bytes 2097152 | tf_op jit(solution)/shard_map/all_to_all | solution.py:53
  53.5 22.6 %all-to-all-start.1 = ((bf16[16,32,640]{2,1,0:T(8,128)(2,1)}), bf16[16,32,640]{2,1,0:T(8,128)(2,1)S(1)}, u32[]{:S(2)}, u32[]{:S(2)}) async-start(bf16[16,32,640]{2,1,0:T(8,128)(2,1)} %pad_maximum_fusion.1), calls=%async_computation.1 | async-start | bytes 1310720 | tf_op jit(solution)/shard_map/all_to_all | solution.py:37
  76.2 4.2 %collective-permute-start.2 = (bf16[640,640]{1,0:T(8,128)(2,1)S(1)}, bf16[640,640]{1,0:T(8,128)(2,1)S(1)}, u32[]{:S(2)}, u32[]{:S(2)}) collective-permute-start(bf16[640,640]{1,0:T(8,128)(2,1)S(1)} %maximum_maximum_fusion), channel_id=1, source_target_pairs={{0,16},{16,0},{32,48},{48,32},{64,80},{80,64},{96,112},{112,96},{1... | collective-permute-start | bytes 2457608 | tf_op jit(solution)/shard_map/ppermute | solution.py:27
  82.8 23.7 %all-to-all-start.2 = ((bf16[8,96,512]{2,1,0:T(8,128)(2,1)}), bf16[8,96,512]{2,1,0:T(8,128)(2,1)S(1)}, u32[]{:S(2)}, u32[]{:S(2)}) async-start(bf16[8,96,512]{2,1,0:T(8,128)(2,1)} %broadcast_in_dim.406), calls=%async_computation.2 | async-start | bytes 1572864 | tf_op jit(solution)/shard_map/all_to_all | solution.py:53
  107.2 9.2 %collective-permute-start.3 = (bf16[288,512]{1,0:T(8,128)(2,1)S(1)}, bf16[288,512]{1,0:T(8,128)(2,1)S(1)}, u32[]{:S(2)}, u32[]{:S(2)}) collective-permute-start(bf16[288,512]{1,0:T(8,128)(2,1)S(1)} %pad_maximum_fusion.3), channel_id=1, source_target_pairs={{0,32},{16,17},{1,33},{17,16},{2,34},{18,19},{3,35},{19,18},{4,36}... | collective-permute-start | bytes 884744 | tf_op jit(solution)/shard_map/ppermute | solution.py:64
  116.9 3.6 %copy-start.2 = (f32[1,3,16,512]{3,2,1,0:T(8,128)S(1)}, f32[1,3,16,512]{3,2,1,0:T(8,128)}, u32[]{:S(2)}) copy-start(f32[1,3,16,512]{3,2,1,0:T(8,128)} %moment.1) | copy-start | bytes 294916
  116.9 3.6 %copy-start.3 = (f32[1,3,16,512]{3,2,1,0:T(8,128)S(1)}, f32[1,3,16,512]{3,2,1,0:T(8,128)}, u32[]{:S(2)}) copy-start(f32[1,3,16,512]{3,2,1,0:T(8,128)} %second.1) | copy-start | bytes 294916
  116.9 3.6 %copy-start.4 = (f32[1,3,16,512]{3,2,1,0:T(8,128)S(1)}, f32[1,3,16,512]{3,2,1,0:T(8,128)}, u32[]{:S(2)}) copy-start(f32[1,3,16,512]{3,2,1,0:T(8,128)} %param.12) | copy-start | bytes 294916
  116.9 3.6 %copy-start.5 = (f32[1,3,16,512]{3,2,1,0:T(8,128)S(1)}, f32[1,3,16,512]{3,2,1,0:T(8,128)}, u32[]{:S(2)}) copy-start(f32[1,3,16,512]{3,2,1,0:T(8,128)} %param.13) | copy-start | bytes 294916
  117.0 3.4 %collective-permute-start.4 = (bf16[144,512]{1,0:T(8,128)(2,1)S(1)}, bf16[144,512]{1,0:T(8,128)(2,1)S(1)}, u32[]{:S(2)}, u32[]{:S(2)}) collective-permute-start(bf16[144,512]{1,0:T(8,128)(2,1)S(1)} %maximum_select_fusion.1), channel_id=1, source_target_pairs={{0,16},{16,0},{32,48},{48,32},{64,80},{80,64},{96,112},{112,96},{1... | collective-permute-start | bytes 442376 | tf_op jit(solution)/shard_map/ppermute | solution.py:27
